TPU v7x, 128 devices: a whole 4x4x4 slice. The times are simulated.
128 devices in a mesh: dp: 32 (over z, x, core), mp: 4 (over y).
Axes of the slice: x: 4, y: 4, z: 4, core: 2. Of those that a mesh axis runs over, the one named last changes fastest.
Arguments:
- pixels: bfloat16 [8192, 192], P('dp'), may hold values from -6 to 6
- targets: float32 [8192, 192], P('dp', 'mp'), may hold values from -6 to 6
- valid_mask: int32 [8192, 4], P('dp'), may hold values from 0 to 1, as said below
- segments: int32 [32, 256], P('dp'), may hold values from 0 to 3, never falling along the last dimension, each value on 1 to 128 neighbouring positions
- lead_index: int32 [32, 4], P('dp'), may hold values from 0 to 27
- latitude: int32 [8192], P('dp'), may hold values from 0 to 31
- var_ids: int32 [48], replicated, may hold values from 0 to 47, each once
- running_error: float32 [48], replicated, may hold values from 0.5 to 2
- agg_weight: float32 [4, 1024, 1024], P(None, 'dp', 'mp'), as said below
- attn_weight: float32 [4, 1024, 1024], P(None, 'dp', 'mp'), as said below
- mlp_weight: float32 [2, 1024, 4096], P(None, 'dp', 'mp'), as said below
- head_weight: float32 [1024, 192], P('dp', 'mp'), may hold values from -0.1875 to 0.1875
- embed_weight: float32 [48, 5, 1024], P(None, None, ('dp', 'mp')), may hold values from -3 to 3
- vectors: float32 [17, 1024], P(None, ('dp', 'mp')), as said below
- agg_first: float32 [4, 1024, 1024], P(None, 'dp', 'mp'), as said below
- attn_first: float32 [4, 1024, 1024], P(None, 'dp', 'mp'), as said below
- mlp_first: float32 [2, 1024, 4096], P(None, 'dp', 'mp'), as said below
- head_first: float32 [1024, 192], P('dp', 'mp'), as said below
- embed_first: float32 [48, 5, 1024], P(None, None, ('dp', 'mp')), as said below
- vector_first: float32 [17, 1024], P(None, ('dp', 'mp')), as said below
- agg_second: float32 [4, 1024, 1024], P(None, 'dp', 'mp'), as said below
- attn_second: float32 [4, 1024, 1024], P(None, 'dp', 'mp'), as said below
- mlp_second: float32 [2, 1024, 4096], P(None, 'dp', 'mp'), as said below
- head_second: float32 [1024, 192], P('dp', 'mp'), as said below
- embed_second: float32 [48, 5, 1024], P(None, None, ('dp', 'mp')), as said below
- vector_second: float32 [17, 1024], P(None, ('dp', 'mp')), as said below
Outputs:
- loss_sum: float32 [], replicated
- valid_count: float32 [], replicated
- running_out: float32 [48], replicated
- trust_ratios: float32 [29], replicated
- weight_norms: float32 [29], replicated
- agg_moment: float32 [4, 1024, 1024], P(None, 'dp', 'mp')
- attn_moment: float32 [4, 1024, 1024], P(None, 'dp', 'mp')
- mlp_moment: float32 [2, 1024, 4096], P(None, 'dp', 'mp')
- head_moment: float32 [1024, 192], P('dp', 'mp')
- embed_moment: float32 [48, 5, 1024], P(None, None, ('dp', 'mp'))
- vector_moment: float32 [17, 1024], P(None, ('dp', 'mp'))
- agg_square: float32 [4, 1024, 1024], P(None, 'dp', 'mp')
- attn_square: float32 [4, 1024, 1024], P(None, 'dp', 'mp')
- mlp_square: float32 [2, 1024, 4096], P(None, 'dp', 'mp')
- head_square: float32 [1024, 192], P('dp', 'mp')
- embed_square: float32 [48, 5, 1024], P(None, None, ('dp', 'mp'))
- vector_square: float32 [17, 1024], P(None, ('dp', 'mp'))
- agg_new: float32 [4, 1024, 1024], P(None, 'dp', 'mp')
- attn_new: float32 [4, 1024, 1024], P(None, 'dp', 'mp')
- mlp_new: float32 [2, 1024, 4096], P(None, 'dp', 'mp')
- head_new: float32 [1024, 192], P('dp', 'mp')
- embed_new: float32 [48, 5, 1024], P(None, None, ('dp', 'mp'))
- vector_new: float32 [17, 1024], P(None, ('dp', 'mp'))
Inputs may be any that keep to these rules, and one draw needn't show every extreme that they name: `valid_mask`: 1 marks a valid pixel. `agg_weight`: projection weights. `attn_weight`: projection weights. `mlp_weight`: projection weights. `vectors`: gains near one, other rows of both signs. `agg_first`: first moments of both signs. `attn_first`: first moments of both signs. `mlp_first`: first moments of both signs. `head_first`: first moments of both signs. `embed_first`: first moments of both signs. `vector_first`: first moments of both signs. `agg_second`: positive second moments. `attn_second`: positive second moments. `mlp_second`: positive second moments. `head_second`: positive second moments. `embed_second`: positive second moments. `vector_second`: positive second moments.
All inputs are finite; a program needn't handle non-finite values.
Results may differ from a plain program's by a relative error of at most 0.019.
Values may be sent and summed in bfloat16 or wider, within the bound.
A program may use at most 192 MiB of HBM per device.

v0:
```python
import math

import jax
import jax.numpy as jnp
from jax import lax
from jax.sharding import PartitionSpec as P

D = 1024
HEAD_DIM = 64
FF = 4096
NVAR = 48
P_SIZE = 4
SEGS = 4
LEADS = 28
LATS = 32
STEP = 10


HIGH = lax.Precision.HIGHEST
NORM_EPS = 1e-06
BETA_ONE = 0.9
BETA_TWO = 0.999
LEARN_RATE = 0.3
WEIGHT_DECAY = 0.01
ADAM_EPS = 1e-08
STATS_DECAY = 0.9
CONTRACT_ROWS = (((0,), (0,)), ((), ()))
CONTRACT_COLS = (((1,), (1,)), ((), ()))


def layer_norm(values, gain_row, bias_row):
    centre = jnp.mean(values, -1, keepdims=True)
    shifted = values - centre
    spread = jnp.mean(shifted * shifted, -1, keepdims=True)
    return shifted * lax.rsqrt(spread + NORM_EPS) * gain_row + bias_row


def norm_back(values, gain_row, bias_row, incoming):
    unused, pullback = jax.vjp(layer_norm, values, gain_row, bias_row)
    return pullback(incoming)


def exact_gelu(values):
    return jax.nn.gelu(values, approximate=False)


def latitude_weights():
    centres = (jnp.arange(LATS, dtype=jnp.float32) + 0.5) * (180.0 / LATS) - 90.0
    cosines = jnp.cos(centres * (math.pi / 180.0))
    return cosines / jnp.mean(cosines)


def adam_direction(weight, gradient, first, second):
    first_new = BETA_ONE * first + (1.0 - BETA_ONE) * gradient
    second_new = BETA_TWO * second + (1.0 - BETA_TWO) * gradient * gradient
    first_hat = first_new / (1.0 - BETA_ONE**STEP)
    second_hat = second_new / (1.0 - BETA_TWO**STEP)
    direction = first_hat / (jnp.sqrt(second_hat) + ADAM_EPS) + WEIGHT_DECAY * weight
    return (first_new, second_new, direction)


def tensor_squares(values, axes_set):
    if axes_set is None:
        return jnp.sum(values * values)[None]
    return jnp.sum(values * values, axis=axes_set)


def apply_trust(weights, stepped, trust_ratios, axes_list):
    results = []
    offset = 0
    for weight, stepped_item, axes_set in zip(weights, stepped, axes_list):
        if axes_set is None:
            part_trust = trust_ratios[offset]
            offset += 1
        else:
            number = weight.shape[0]
            part_trust = trust_ratios[offset : offset + number].reshape(
                (number,) + (1,) * len(axes_set)
            )
            offset += number
        results.append(weight - LEARN_RATE * part_trust * stepped_item[2])
    return results


def placed(values, total, offset):
    return lax.dynamic_update_slice_in_dim(jnp.zeros((total,), jnp.float32), values, offset, 0)


def contract_rows(pairs):
    result = None
    for left, weight in pairs:
        term = lax.dot_general(left, weight, CONTRACT_COLS, preferred_element_type=jnp.float32)
        result = term if result is None else result + term
    return result


def reduce_rows(pairs, share):

    def term_fn(start, number):
        return contract_rows(pairs)

    return lax.psum_scatter(
        term_fn(jnp.int32(0), share * lax.axis_size("mp")), "mp", scatter_dimension=0, tiled=True
    )


def reduce_grads(pairs, share):

    def term_fn(start, number):
        return contract_rows(pairs)

    return lax.psum_scatter(
        term_fn(jnp.int32(0), share * lax.axis_size("mp")).astype(jnp.bfloat16),
        "mp",
        scatter_dimension=0,
        tiled=True,
    ).astype(jnp.float32)


def gather_rows(values):
    return lax.all_gather(values, "mp", axis=0, tiled=True)


def gather_grads(values):
    return lax.all_gather(values, "mp", axis=0, tiled=True)


def on_device(
    pixels,
    targets,
    valid_mask,
    segments,
    lead_index,
    latitude,
    var_ids,
    running_error,
    agg_weight,
    attn_weight,
    mlp_weight,
    head_weight,
    embed_weight,
    vectors,
    agg_first,
    attn_first,
    mlp_first,
    head_first,
    embed_first,
    vector_first,
    agg_second,
    attn_second,
    mlp_second,
    head_second,
    embed_second,
    vector_second,
):
    low_type = jnp.bfloat16
    wide_type = jnp.float32
    groups_mp = lax.axis_size("mp")
    place = lax.axis_index("mp")
    length = pixels.shape[0]
    share = length // groups_mp
    scale = 1.0 / math.sqrt(HEAD_DIM)
    ratio = FF // D
    keep = valid_mask.astype(wide_type)
    head_cols = head_weight.shape[1]
    mine_vars = head_cols // P_SIZE
    total_count = None
    agg_w, attn_w, mlp_w, head_w = (
        lax.all_gather(agg_weight.astype(low_type), "dp", axis=1, tiled=True),
        lax.all_gather(attn_weight.astype(low_type), "dp", axis=1, tiled=True),
        lax.all_gather(mlp_weight.astype(low_type), "dp", axis=1, tiled=True),
        lax.all_gather(head_weight.astype(low_type), "dp", axis=0, tiled=True),
    )
    embed_all, vector_all = (
        lax.all_gather(embed_weight, ("dp", "mp"), axis=2, tiled=True),
        lax.all_gather(vectors, ("dp", "mp"), axis=1, tiled=True),
    )
    cols = attn_w.shape[2]
    local_heads = cols // HEAD_DIM
    ff_cols = mlp_w.shape[2]
    mine_start = place * share
    segment_row = segments[0]
    same_crop = segment_row[:, None] == segment_row[None, :]
    crop_hot = (segment_row[:, None] == jnp.arange(SEGS, dtype=jnp.int32)[None, :]).astype(
        wide_type
    )
    lead_values = (lead_index[0] + 1).astype(wide_type) / LEADS
    lead_all = jnp.dot(crop_hot, lead_values, precision=HIGH)
    lead_mine = lax.dynamic_slice_in_dim(lead_all, mine_start, share, 0)
    lat_hot = (latitude[:, None] == jnp.arange(LATS, dtype=jnp.int32)[None, :]).astype(wide_type)
    lat_w = jnp.dot(lat_hot, latitude_weights(), precision=HIGH)
    var_hot = (var_ids[:, None] == jnp.arange(NVAR, dtype=jnp.int32)[None, :]).astype(wide_type)
    chosen = jnp.einsum("cv,vpd->cpd", var_hot, embed_all, precision=HIGH)
    pixel_cube = pixels.reshape(length, NVAR, P_SIZE)
    tokens_v = (
        jnp.einsum("tcp,cpd->tcd", pixel_cube.astype(wide_type), chosen[:, :P_SIZE], precision=HIGH)
        + chosen[:, P_SIZE][None]
    ).astype(low_type)
    flat_v = tokens_v.reshape(length * NVAR, D)
    kv_weight = jnp.concatenate([agg_w[1], agg_w[2]], 1)
    query_a = (
        jnp.dot(vector_all[0], agg_w[0].astype(wide_type), precision=HIGH)
        .astype(low_type)
        .reshape(local_heads, HEAD_DIM)
    )
    kv_a = (
        jnp.dot(flat_v, kv_weight, preferred_element_type=wide_type)
        .astype(low_type)
        .reshape(length, NVAR, 2, local_heads, HEAD_DIM)
    )
    keys_a = kv_a[:, :, 0]
    vals_a = kv_a[:, :, 1]
    scores_a = jnp.einsum("tchd,hd->thc", keys_a, query_a, preferred_element_type=wide_type) * scale
    probs_a = jax.nn.softmax(scores_a, -1)
    weights_a = probs_a.astype(low_type)
    mixed_a = (
        jnp.einsum("thc,tchd->thd", weights_a, vals_a, preferred_element_type=wide_type)
        .astype(low_type)
        .reshape(length, cols)
    )
    stream0 = (
        reduce_rows(((mixed_a, agg_w[3]),), share)
        + vector_all[1]
        + lead_mine[:, None] * vector_all[2]
    )
    normed1 = layer_norm(stream0, vector_all[3], vector_all[4]).astype(low_type)
    whole1 = gather_rows(normed1)
    projected = jnp.einsum("td,kde->kte", whole1, attn_w[:3], preferred_element_type=wide_type)
    q_bias = lax.dynamic_slice_in_dim(vector_all[5], place * cols, cols, 0)
    v_bias = lax.dynamic_slice_in_dim(vector_all[6], place * cols, cols, 0)
    queries = (projected[0] + q_bias).astype(low_type).reshape(length, local_heads, HEAD_DIM)
    key_rows = projected[1].astype(low_type).reshape(length, local_heads, HEAD_DIM)
    value_rows = (projected[2] + v_bias).astype(low_type).reshape(length, local_heads, HEAD_DIM)

    def block_scores():
        raw_scores = (
            jnp.einsum("thd,uhd->htu", queries, key_rows, preferred_element_type=wide_type) * scale
        )
        return jnp.where(same_crop[None], raw_scores, -1e30)

    scores_b = block_scores()
    log_total = jax.nn.logsumexp(scores_b, -1, keepdims=True)
    weights_b = jnp.exp(scores_b - log_total).astype(low_type)
    mixture = (
        jnp.einsum("htu,uhd->thd", weights_b, value_rows, preferred_element_type=wide_type)
        .astype(low_type)
        .reshape(length, cols)
    )
    stream1 = stream0 + reduce_rows(((mixture, attn_w[3]),), share) + vector_all[7]
    normed2 = layer_norm(stream1, vector_all[8], vector_all[9]).astype(low_type)
    whole2 = gather_rows(normed2)
    ff_bias = lax.dynamic_slice_in_dim(
        vector_all[10 : 10 + ratio].reshape(FF), place * ff_cols, ff_cols, 0
    )
    inner = jnp.dot(whole2, mlp_w[0], preferred_element_type=wide_type) + ff_bias
    hidden = exact_gelu(inner).astype(low_type)
    stream2 = stream1 + reduce_rows(((hidden, mlp_w[1]),), share) + vector_all[10 + ratio]
    normed3 = layer_norm(stream2, vector_all[11 + ratio], vector_all[12 + ratio]).astype(low_type)
    whole3 = gather_rows(normed3)
    predicted = jnp.dot(whole3, head_w, preferred_element_type=wide_type)
    misfit = predicted - targets
    loss_weight = jnp.broadcast_to(
        lat_w[:, None, None] * keep[:, None, :], (length, mine_vars, P_SIZE)
    ).reshape(length, head_cols)
    error_local = jnp.sum(
        (loss_weight * misfit * misfit).reshape(length, mine_vars, P_SIZE), (0, 2)
    )
    error_vec = placed(error_local, NVAR, place * mine_vars)
    error_all, total_count = lax.psum((error_vec, jnp.sum(keep) * mine_vars), ("dp", "mp"))
    dpredict = (2.0 * loss_weight * misfit / total_count).astype(low_type)
    grad_head = lax.dot_general(whole3, dpredict, CONTRACT_ROWS, preferred_element_type=wide_type)
    dnormed3 = reduce_grads(((dpredict, head_w),), share)
    dstream2, dgain3, dbias3 = norm_back(
        stream2, vector_all[11 + ratio], vector_all[12 + ratio], dnormed3
    )
    dbranch2 = gather_grads(dstream2.astype(low_type))
    grad_second = lax.dot_general(dbranch2, hidden, CONTRACT_ROWS, preferred_element_type=wide_type)
    dhidden = jnp.dot(dbranch2, mlp_w[1], preferred_element_type=wide_type)
    unused, gelu_pull = jax.vjp(exact_gelu, inner)
    dinner = gelu_pull(dhidden)[0].astype(low_type)
    grad_first = lax.dot_general(whole2, dinner, CONTRACT_ROWS, preferred_element_type=wide_type)
    grad_mlp = jnp.stack([grad_first, grad_second])
    head_part = None
    mlp_part = None
    dnormed2 = reduce_grads(((dinner, mlp_w[0]),), share)
    dlocal2, dgain2, dbias2 = norm_back(stream1, vector_all[8], vector_all[9], dnormed2)
    dstream1 = dstream2 + dlocal2
    dbranch1 = gather_grads(dstream1.astype(low_type))
    grad_out_b = lax.dot_general(dbranch1, mixture, CONTRACT_ROWS, preferred_element_type=wide_type)
    dmixture = (
        jnp.dot(dbranch1, attn_w[3], preferred_element_type=wide_type)
        .astype(low_type)
        .reshape(length, local_heads, HEAD_DIM)
    )
    probs_b = jnp.exp(block_scores() - log_total)
    weights_b = probs_b.astype(low_type)
    dvalues = jnp.einsum(
        "htu,thd->uhd", weights_b, dmixture, preferred_element_type=wide_type
    ).astype(low_type)
    dprob_b = jnp.einsum("thd,uhd->htu", dmixture, value_rows, preferred_element_type=wide_type)
    dscore_b = (probs_b * (dprob_b - jnp.sum(probs_b * dprob_b, -1, keepdims=True))).astype(
        low_type
    )
    dqueries = (
        jnp.einsum("htu,uhd->thd", dscore_b, key_rows, preferred_element_type=wide_type) * scale
    ).astype(low_type)
    dkeys = (
        jnp.einsum("htu,thd->uhd", dscore_b, queries, preferred_element_type=wide_type) * scale
    ).astype(low_type)
    dqkv = jnp.stack(
        [dqueries.reshape(length, cols), dkeys.reshape(length, cols), dvalues.reshape(length, cols)]
    )
    grad_qkv = jnp.einsum("td,kte->kde", whole1, dqkv, preferred_element_type=wide_type)
    grad_attn = jnp.concatenate([grad_qkv, grad_out_b[None]], 0)
    dq_bias = jnp.sum(dqkv[0].astype(wide_type), 0)
    dv_bias = jnp.sum(dqkv[2].astype(wide_type), 0)
    dnormed1 = reduce_grads(
        ((dqkv[0], attn_w[0]), (dqkv[1], attn_w[1]), (dqkv[2], attn_w[2])), share
    )
    dlocal1, dgain1, dbias1 = norm_back(stream0, vector_all[3], vector_all[4], dnormed1)
    dstream0 = dstream1 + dlocal1
    dbranch0 = gather_grads(dstream0.astype(low_type))
    grad_out_a = lax.dot_general(dbranch0, mixed_a, CONTRACT_ROWS, preferred_element_type=wide_type)
    dmixed_a = (
        jnp.dot(dbranch0, agg_w[3], preferred_element_type=wide_type)
        .astype(low_type)
        .reshape(length, local_heads, HEAD_DIM)
    )
    dvals_a = jnp.einsum(
        "thc,thd->tchd", weights_a, dmixed_a, preferred_element_type=wide_type
    ).astype(low_type)
    dprob_a = jnp.einsum("thd,tchd->thc", dmixed_a, vals_a, preferred_element_type=wide_type)
    dscore_a = (probs_a * (dprob_a - jnp.sum(probs_a * dprob_a, -1, keepdims=True))).astype(
        low_type
    )
    dkeys_a = (
        jnp.einsum("thc,hd->tchd", dscore_a, query_a, preferred_element_type=wide_type) * scale
    ).astype(low_type)
    dquery_a = (
        jnp.einsum("thc,tchd->hd", dscore_a, keys_a, preferred_element_type=wide_type) * scale
    ).reshape(cols)
    dkv_a = jnp.stack([dkeys_a, dvals_a], 2).reshape(length * NVAR, 2 * cols)
    grad_kv = lax.dot_general(flat_v, dkv_a, CONTRACT_ROWS, preferred_element_type=wide_type)
    grad_query_w = vector_all[0][:, None] * dquery_a[None, :]
    grad_agg = jnp.stack([grad_query_w, grad_kv[:, :cols], grad_kv[:, cols:], grad_out_a])
    dquery_base = jnp.dot(agg_w[0].astype(wide_type), dquery_a, precision=HIGH)
    pixel_ext = jnp.concatenate([pixel_cube, jnp.ones((length, NVAR, 1), low_type)], 2)
    paired = jnp.einsum(
        "tcp,tce->cpe",
        pixel_ext,
        dkv_a.reshape(length, NVAR, 2 * cols),
        preferred_element_type=wide_type,
    )
    dchosen = jnp.einsum("cpe,de->cpd", paired, kv_weight.astype(wide_type), precision=HIGH)
    grad_embed = jnp.einsum("cv,cpd->vpd", var_hot, dchosen, precision=HIGH)
    head_rows = jnp.stack(
        [
            dquery_base,
            jnp.sum(dstream0, 0),
            jnp.sum(lead_mine[:, None] * dstream0, 0),
            dgain1,
            dbias1,
            placed(dq_bias, D, place * cols),
            placed(dv_bias, D, place * cols),
            jnp.sum(dstream1, 0),
            dgain2,
            dbias2,
        ]
    )
    ff_rows = placed(jnp.sum(dinner.astype(wide_type), 0), FF, place * ff_cols).reshape(ratio, D)
    tail_rows = jnp.stack([jnp.sum(dstream2, 0), dgain3, dbias3])
    grad_vec = jnp.concatenate([head_rows, ff_rows, tail_rows], 0)
    agg_part, attn_part, mlp_part, head_part = (
        lax.psum_scatter(
            grad_agg.astype(jnp.bfloat16), "dp", scatter_dimension=1, tiled=True
        ).astype(jnp.float32),
        lax.psum_scatter(
            grad_attn.astype(jnp.bfloat16), "dp", scatter_dimension=1, tiled=True
        ).astype(jnp.float32),
        lax.psum_scatter(
            grad_mlp.astype(jnp.bfloat16), "dp", scatter_dimension=1, tiled=True
        ).astype(jnp.float32),
        lax.psum_scatter(
            grad_head.astype(jnp.bfloat16), "dp", scatter_dimension=0, tiled=True
        ).astype(jnp.float32),
    )
    embed_part, vector_part = (
        lax.psum_scatter(grad_embed, ("dp", "mp"), scatter_dimension=2, tiled=True),
        lax.psum_scatter(grad_vec, ("dp", "mp"), scatter_dimension=1, tiled=True),
    )
    params = (agg_weight, attn_weight, mlp_weight, head_weight, embed_weight, vectors)
    grads = (agg_part, attn_part, mlp_part, head_part, embed_part, vector_part)
    firsts = (agg_first, attn_first, mlp_first, head_first, embed_first, vector_first)
    seconds = (agg_second, attn_second, mlp_second, head_second, embed_second, vector_second)
    axes_list = ((1, 2), (1, 2), (1, 2), None, None, (1,))
    stepped = [adam_direction(w, g, m, s) for w, g, m, s in zip(params, grads, firsts, seconds)]
    weight_sq = jnp.concatenate([tensor_squares(w, a) for w, a in zip(params, axes_list)])
    update_sq = jnp.concatenate([tensor_squares(item[2], a) for item, a in zip(stepped, axes_list)])
    weight_sq, update_sq = lax.psum((weight_sq, update_sq), ("dp", "mp"))
    weight_norms = jnp.sqrt(weight_sq)
    trust_ratios = weight_norms / jnp.sqrt(update_sq)
    news = apply_trust(params, stepped, trust_ratios, axes_list)
    loss_sum = jnp.sum(error_all)
    running_out = STATS_DECAY * running_error + (1.0 - STATS_DECAY) * error_all * (
        NVAR / total_count
    )
    return (
        loss_sum,
        total_count,
        running_out,
        trust_ratios,
        weight_norms,
        stepped[0][0],
        stepped[1][0],
        stepped[2][0],
        stepped[3][0],
        stepped[4][0],
        stepped[5][0],
        stepped[0][1],
        stepped[1][1],
        stepped[2][1],
        stepped[3][1],
        stepped[4][1],
        stepped[5][1],
        news[0],
        news[1],
        news[2],
        news[3],
        news[4],
        news[5],
    )


def solution(mesh):
    in_specs = (
        P("dp", None),
        P("dp", "mp"),
        P("dp", None),
        P("dp", None),
        P("dp", None),
        P("dp"),
        P(),
        P(),
        P(None, "dp", "mp"),
        P(None, "dp", "mp"),
        P(None, "dp", "mp"),
        P("dp", "mp"),
        P(None, None, ("dp", "mp")),
        P(None, ("dp", "mp")),
        P(None, "dp", "mp"),
        P(None, "dp", "mp"),
        P(None, "dp", "mp"),
        P("dp", "mp"),
        P(None, None, ("dp", "mp")),
        P(None, ("dp", "mp")),
        P(None, "dp", "mp"),
        P(None, "dp", "mp"),
        P(None, "dp", "mp"),
        P("dp", "mp"),
        P(None, None, ("dp", "mp")),
        P(None, ("dp", "mp")),
    )
    out_specs = (
        P(),
        P(),
        P(),
        P(),
        P(),
        P(None, "dp", "mp"),
        P(None, "dp", "mp"),
        P(None, "dp", "mp"),
        P("dp", "mp"),
        P(None, None, ("dp", "mp")),
        P(None, ("dp", "mp")),
        P(None, "dp", "mp"),
        P(None, "dp", "mp"),
        P(None, "dp", "mp"),
        P("dp", "mp"),
        P(None, None, ("dp", "mp")),
        P(None, ("dp", "mp")),
        P(None, "dp", "mp"),
        P(None, "dp", "mp"),
        P(None, "dp", "mp"),
        P("dp", "mp"),
        P(None, None, ("dp", "mp")),
        P(None, ("dp", "mp")),
    )
    return jax.shard_map(
        on_device, mesh=mesh, in_specs=in_specs, out_specs=out_specs, check_vma=False
    )
```

profile of v0, /device:TPU:1, one launch (start us, length us, event | category | flops | bytes accessed | tf_op | source)
XLA Modules:
  0.0 1870.1 jit_solution(13510770947402169847)
XLA Ops:
  10.6 68.3 %all_gather.38 = f32[48,5,1024]{0,2,1:T(8,128)S(1)} all-gather(f32[48,5,8]{0,2,1:T(8,128)} %param.38), channel_id=1, replica_groups=mesh['dp'=32,'mp'=4] {'dp','mp'}, dimensions={2}, use_global_device_ids=true | all-gather | bytes 990720 | tf_op jit(solution)/shard_map/all_gather | solution.py:175
  78.9 2.4 fusion.80
  81.4 21.9 %fusion = bf16[256,48,1024]{2,0,1:T(8,128)(2,1)S(1)} fusion(f32[48,1024]{1,0:T(8,128)S(1)} %slice_bitcast_fusion.23, bf16[256,48,4]{0,2,1:T(4,128)(2,1)S(1)} %reshape.352, f32[48,4,1024]{2,0,1:T(8,128)S(1)} %slice.174), kind=kOutput, calls=%fused_computation.1 | convolution fusion | flops 629145600 | bytes 26247168 | tf_op jit(solution)/shard_map/tcp,cpd->tcd/dot_general | solution.py:196
  103.3 42.9 %copy.137 = bf16[256,48,1024]{2,1,0:T(8,128)(2,1)} copy(bf16[256,48,1024]{2,0,1:T(8,128)(2,1)S(1)} %fusion) | data formatting | bytes 50331648 | tf_op jit(solution)/shard_map/convert_element_type | solution.py:198
  146.2 51.3 %all_gather.36 = f32[17,1024]{0,1:T(8,128)S(1)} all-gather(f32[17,8]{0,1:T(8,128)S(1)} %copy-done.65), channel_id=1, replica_groups=mesh['dp'=32,'mp'=4] {'dp','mp'}, dimensions={1}, use_global_device_ids=true | all-gather | bytes 70176 | tf_op jit(solution)/shard_map/all_gather | solution.py:176
  197.6 4.4 slice_reduce_fusion.1
  203.2 24.9 %convolution_convert_fusion = bf16[12288,512]{1,0:T(8,128)(2,1)} fusion(bf16[12288,1024]{1,0:T(8,128)(2,1)} %bitcast.231, bf16[1024,256]{1,0:T(8,128)(2,1)S(1)} %get-tuple-element.188, bf16[1024,256]{1,0:T(8,128)(2,1)S(1)} %get-tuple-element.187), kind=kOutput, calls=%fused_computation.4 | convolution fusion | flops 12893290496 | bytes 38797312 | tf_op jit(solution)/shard_map/dot_general | solution.py:207
  228.1 38.2 %reshape.354 = bf16[256,48,2,4,64]{4,3,2,1,0:T(4,128)(2,1)} reshape(bf16[12288,512]{1,0:T(8,128)(2,1)} %convolution_convert_fusion) | data formatting | bytes 25165824 | tf_op jit(solution)/shard_map/reshape | solution.py:209
  266.4 11.5 slice_bitcast_fusion
  277.9 19.4 %copy.157 = bf16[256,48,4,64]{0,3,1,2:T(8,128)(2,1)} copy(bf16[256,48,4,64]{3,2,1,0:T(4,128)(2,1)} %slice_bitcast_fusion) | data formatting | bytes 12582912 | tf_op jit(solution)/shard_map/squeeze | solution.py:211
  297.6 3.7 fusion.134
  302.5 4.9 copy.187
  307.5 25.4 %multiply_reduce_fusion.1 = bf16[256,4,64]{2,1,0:T(4,128)(2,1)S(1)} fusion(f32[256,4,48]{1,2,0:T(8,128)} %copy.187, bf16[256,48,2,4,64]{4,3,2,1,0:T(4,128)(2,1)} %reshape.354), kind=kLoop, calls=%fused_computation.3 | loop fusion | flops 9371648 | bytes 6619136
  336.3 9.0 fusion.130
  345.3 8.4 reduce-scatter.13.cloned.1.call-done
  357.2 11.2 all_gather.39
  372.8 23.7 %reduce-scatter.15.cloned.1.call-done = f32[64,1024]{1,0:T(8,128)} async-done(((f32[256,1024]{1,0:T(8,128)}), f32[64,1024]{1,0:T(8,128)}) %reduce-scatter.15.cloned.1.call-update) | async-done | bytes 262160 | tf_op jit(solution)/shard_map/reduce_scatter | solution.py:102
  398.1 11.3 all_gather.41
  409.4 38.4 %all-gather.8.cloned.1.call-done = bf16[2,1024,1024]{2,1,0:T(8,128)(2,1)} async-done(((bf16[2,32,1024]{2,1,0:T(8,128)(2,1)}), bf16[2,1024,1024]{2,1,0:T(8,128)(2,1)}) %all-gather.8.cloned.1.call-update) | async-done | bytes 4194320 | tf_op jit(solution)/shard_map/all_gather | solution.py:171
  447.8 5.9 multiply_convert_fusion.4
  459.3 64.8 %psum.29 = f32[]{:T(128)} all-reduce(f32[]{:T(128)S(6)} %mul.693), channel_id=1, replica_groups=mesh['dp'=32,'mp'=4] {'dp','mp'}, use_global_device_ids=true, to_apply=%region_19.20 | all-reduce | flops 1 | bytes 8 | tf_op jit(solution)/shard_map/psum | solution.py:269
  524.1 25.0 %all_gather.44 = bf16[1024,48]{1,0:T(8,128)(2,1)S(1)} all-gather(bf16[32,48]{1,0:T(8,128)(2,1)S(1)} %convert_element_type.204), channel_id=1, replica_groups=mesh['dp'=32,'mp'=4] {'dp'}, dimensions={0}, use_global_device_ids=true | all-gather | bytes 101376 | tf_op jit(solution)/shard_map/all_gather | solution.py:172
  550.6 10.3 all_gather.43
  564.5 19.4 %reduce-scatter.19.cloned.1.call-done = bf16[64,1024]{1,0:T(8,128)(2,1)} async-done(((bf16[256,1024]{1,0:T(8,128)(2,1)}), bf16[64,1024]{1,0:T(8,128)(2,1)}) %reduce-scatter.19.cloned.1.call-update) | async-done | bytes 131088 | tf_op jit(solution)/shard_map/reduce_scatter | solution.py:112
  587.3 11.2 all_gather.45
  599.3 3.8 convert_reduce_fusion
  605.5 23.0 %reduce-scatter.21.cloned.1.call-done = bf16[64,1024]{1,0:T(8,128)(2,1)} async-done(((bf16[256,1024]{1,0:T(8,128)(2,1)}), bf16[64,1024]{1,0:T(8,128)(2,1)}) %reduce-scatter.21.cloned.1.call-update) | async-done | bytes 131088 | tf_op jit(solution)/shard_map/reduce_scatter | solution.py:112
  633.5 11.1 all_gather.46
  652.7 21.2 %reduce-scatter.23.cloned.1.call-done = bf16[64,1024]{1,0:T(8,128)(2,1)} async-done(((bf16[256,1024]{1,0:T(8,128)(2,1)}), bf16[64,1024]{1,0:T(8,128)(2,1)}) %reduce-scatter.23.cloned.1.call-update) | async-done | bytes 131088 | tf_op jit(solution)/shard_map/reduce_scatter | solution.py:112
  677.4 11.5 all_gather.47
  690.5 18.4 multiply_reduce_fusion
  708.9 5.3 copy.175
  714.3 4.5 fusion.59
  718.9 2.5 fusion.2
  721.4 4.6 fusion.1
  726.1 4.8 pad_maximum_fusion
  731.0 4.6 fusion.61
  739.4 2.4 fusion.22
  742.1 3.8 fusion.78
  748.7 38.6 %copy.149 = bf16[256,48,2,4,64]{4,3,2,1,0:T(4,128)(2,1)} copy(bf16[256,48,2,4,64]{0,4,3,2,1:T(8,128)(2,1)} %copy-done) | data formatting | bytes 25165824 | tf_op jit(solution)/shard_map/stack | solution.py:342
  787.3 39.0 %reshape.360 = bf16[12288,512]{1,0:T(8,128)(2,1)} reshape(bf16[256,48,2,4,64]{4,3,2,1,0:T(4,128)(2,1)} %copy.149) | data formatting | bytes 25165824 | tf_op jit(solution)/shard_map/reshape | solution.py:342
  826.9 20.0 %convolution_convert_fusion.2 = bf16[1024,512]{1,0:T(8,128)(2,1)S(1)} fusion(bf16[12288,1024]{1,0:T(8,128)(2,1)} %bitcast.232, bf16[12288,512]{1,0:T(8,128)(2,1)} %reshape.360), kind=kOutput, calls=%fused_computation.27 | convolution fusion | flops 12885426176 | bytes 38797312 | tf_op jit(solution)/shard_map/dot_general | solution.py:343
  856.6 43.6 %all-reduce.5.cloned.1.call-done = f32[17,1024]{1,0:T(8,128)} async-done(((f32[17,1024]{1,0:T(8,128)}), f32[17,1024]{1,0:T(8,128)}) %all-reduce.5.cloned.1.call-update) | async-done | bytes 69648
  901.2 633.1 %reduce-scatter.33.cloned.1.call-done = f32[48,5,8]{0,2,1:T(8,128)} async-done(((f32[48,5,1024]{0,2,1:T(8,128)}), f32[48,5,8]{0,2,1:T(8,128)}) %reduce-scatter.33.cloned.1.call-update) | async-done | bytes 7696 | tf_op jit(solution)/shard_map/reduce_scatter | solution.py:388
  1535.7 82.4 %reduce-scatter.27.cloned.1.call-done = bf16[4,32,256]{2,1,0:T(8,128)(2,1)} async-done(((bf16[4,1024,256]{2,1,0:T(8,128)(2,1)}), bf16[4,32,256]{2,1,0:T(8,128)(2,1)}) %reduce-scatter.27.cloned.1.call-update) | async-done | bytes 65552 | tf_op jit(solution)/shard_map/reduce_scatter | solution.py:377
  1619.1 81.0 %reduce-scatter.25.cloned.1.call-done = bf16[4,32,256]{2,1,0:T(8,128)(2,1)} async-done(((bf16[4,1024,256]{2,1,0:T(8,128)(2,1)}), bf16[4,32,256]{2,1,0:T(8,128)(2,1)}) %reduce-scatter.25.cloned.1.call-update) | async-done | bytes 65552 | tf_op jit(solution)/shard_map/reduce_scatter | solution.py:374
  1701.2 84.2 %reduce-scatter.29.cloned.1.call-done = bf16[2,32,1024]{2,1,0:T(8,128)(2,1)} async-done(((bf16[2,1024,1024]{2,1,0:T(8,128)(2,1)}), bf16[2,32,1024]{2,1,0:T(8,128)(2,1)}) %reduce-scatter.29.cloned.1.call-update) | async-done | bytes 131088 | tf_op jit(solution)/shard_map/reduce_scatter | solution.py:380
  1789.4 65.9 %all-reduce.2 = (f32[48]{0:T(128)S(1)}, f32[29]{0:T(128)S(1)}, f32[29]{0:T(128)S(1)}) all-reduce(f32[48]{0:T(128)S(1)} %dynamic_update_slice.14, f32[29]{0:T(128)S(1)} %concatenate.20, f32[29]{0:T(128)S(1)} %concatenate.24), channel_id=1, replica_groups=mesh['dp'=32,'mp'=4] {'dp','mp'}, use_global_device_ids=true, to_apply=%region_16.17 | all-reduce | flops 106 | bytes 848 | tf_op jit(solution)/shard_map/psum | solution.py:269
  (402 shorter events, 83.8 us)
Async XLA Ops:
  7.2 194.8 %all-gather.4.cloned.1.call-start = ((), (), s32[]{:S(2)}) async-start(), calls=%async_computation.11 | async-start | bytes 2162688 | tf_op jit(solution)/shard_map/all_gather | solution.py:169
  8.8 72.6 %copy-start.58 = (bf16[256,192]{0,1:T(8,128)(2,1)S(1)}, bf16[256,192]{0,1:T(8,128)(2,1)}, u32[]{:S(2)}) copy-start(bf16[256,192]{0,1:T(8,128)(2,1)} %param.26) | copy-start | bytes 294916
  8.8 327.5 %all-gather.6.cloned.1.call-start = ((), (), s32[]{:S(2)}) async-start(), calls=%async_computation.13 | async-start | bytes 2162688 | tf_op jit(solution)/shard_map/all_gather | solution.py:170
  10.5 343.2 %reduce-scatter.13.cloned.1.call-start = ((), (), s32[]{:S(2)}) async-start(), calls=%async_computation.12 | async-start | bytes 1310720 | tf_op jit(solution)/shard_map/reduce_scatter | solution.py:102
  201.9 95.3 %copy-start.63 = (f32[1024]{0:T(1024)}, f32[1024]{0:T(1024)S(1)}, u32[]{:S(2)}) copy-start(f32[1024]{0:T(1024)S(1)} %get-tuple-element.125) | copy-start | bytes 12292
  334.5 62.1 %reduce-scatter.15.cloned.1.call-start = ((), (), s32[]{:S(2)}) async-start(), calls=%async_computation.14 | async-start | bytes 1310720 | tf_op jit(solution)/shard_map/reduce_scatter | solution.py:102
  336.2 60.4 %copy-start.67 = (f32[64]{0:T(128)}, f32[64]{0:T(128)S(1)}, u32[]{:S(2)}) copy-start(f32[64]{0:T(128)S(1)} %dynamic_slice.12) | copy-start | bytes 772
  371.6 76.2 %all-gather.8.cloned.1.call-start = ((), (), s32[]{:S(2)}) async-start(), calls=%async_computation.15 | async-start | bytes 4325376 | tf_op jit(solution)/shard_map/all_gather | solution.py:171
  372.4 176.8 %reduce-scatter.17.cloned.1.call-start = ((), (), s32[]{:S(2)}) async-start(), calls=%async_computation.16 | async-start | bytes 1310720 | tf_op jit(solution)/shard_map/reduce_scatter | solution.py:102
  397.7 56.1 %copy-start.86 = (f32[64]{0:T(128)}, f32[64]{0:T(128)S(1)}, u32[]{:S(2)}) copy-start(f32[64]{0:T(128)S(1)} %broadcast_multiply_fusion.2) | copy-start | bytes 772
  397.9 55.9 %copy-start.104 = (f32[64]{0:T(128)}, f32[64]{0:T(128)S(1)}, u32[]{:S(2)}) copy-start(f32[64]{0:T(128)S(1)} %multiply_reduce_fusion.7) | copy-start | bytes 772
  398.0 55.8 %copy-start.91 = (f32[64]{0:T(128)}, f32[64]{0:T(128)S(1)}, u32[]{:S(2)}) copy-start(f32[64]{0:T(128)S(1)} %fusion.99) | copy-start | bytes 772
  453.8 70.2 %copy-start.52 = (f32[32,48]{1,0:T(8,128)S(1)}, f32[32,48]{1,0:T(8,128)}, u32[]{:S(2)}) copy-start(f32[32,48]{1,0:T(8,128)} %param.37) | copy-start | bytes 18436
  454.6 94.5 %copy-start.75 = (f32[1024]{0:T(1024)S(1)}, f32[1024]{0:T(1024)}, u32[]{:S(2)}) copy-start(f32[1024]{0:T(1024)} %get-tuple-element.117) | copy-start | bytes 12292
  454.6 95.9 %copy-start.74 = (f32[1024]{0:T(1024)S(1)}, f32[1024]{0:T(1024)}, u32[]{:S(2)}) copy-start(f32[1024]{0:T(1024)} %get-tuple-element.116) | copy-start | bytes 12292
  456.4 127.5 %reduce-scatter.19.cloned.1.call-start = ((), (), s32[]{:S(2)}) async-start(), calls=%async_computation.17 | async-start | bytes 655360 | tf_op jit(solution)/shard_map/reduce_scatter | solution.py:112
  564.4 64.1 %reduce-scatter.21.cloned.1.call-start = ((), (), s32[]{:S(2)}) async-start(), calls=%async_computation.18 | async-start | bytes 655360 | tf_op jit(solution)/shard_map/reduce_scatter | solution.py:112
  605.5 68.4 %reduce-scatter.23.cloned.1.call-start = ((), (), s32[]{:S(2)}) async-start(), calls=%async_computation.19 | async-start | bytes 655360 | tf_op jit(solution)/shard_map/reduce_scatter | solution.py:112
  650.9 204.4 %reduce-scatter.31.cloned.1.call-start = ((), (), s32[]{:S(2)}) async-start(), calls=%async_computation.23 | async-start | bytes 270336 | tf_op jit(solution)/shard_map/reduce_scatter | solution.py:383
  652.1 248.1 %all-reduce.5.cloned.1.call-start = ((), (), s32[]{:S(2)}) async-start(), calls=%async_computation.25 | async-start | bytes 196608
  741.9 792.4 %reduce-scatter.33.cloned.1.call-start = ((), (), s32[]{:S(2)}) async-start(), calls=%async_computation.24 | async-start | bytes 2641920 | tf_op jit(solution)/shard_map/reduce_scatter | solution.py:388
  745.9 872.2 %reduce-scatter.27.cloned.1.call-start = ((), (), s32[]{:S(2)}) async-start(), calls=%async_computation.21 | async-start | bytes 2162688 | tf_op jit(solution)/shard_map/reduce_scatter | solution.py:377
  748.5 951.6 %reduce-scatter.25.cloned.1.call-start = ((), (), s32[]{:S(2)}) async-start(), calls=%async_computation.20 | async-start | bytes 2162688 | tf_op jit(solution)/shard_map/reduce_scatter | solution.py:374
  848.6 936.9 %reduce-scatter.29.cloned.1.call-start = ((), (), s32[]{:S(2)}) async-start(), calls=%async_computation.22 | async-start | bytes 4325376 | tf_op jit(solution)/shard_map/reduce_scatter | solution.py:380
  853.7 680.5 %copy-start.51 = (f32[48,5,8]{0,2,1:T(8,128)S(1)}, f32[48,5,8]{0,2,1:T(8,128)}, u32[]{:S(2)}) copy-start(f32[48,5,8]{0,2,1:T(8,128)} %param.38) | copy-start | bytes 23044
  853.8 680.5 %copy-start.69 = (f32[48,5,8]{0,2,1:T(8,128)S(1)}, f32[48,5,8]{0,2,1:T(8,128)}, u32[]{:S(2)}) copy-start(f32[48,5,8]{0,2,1:T(8,128)} %param.44) | copy-start | bytes 23044
  853.8 680.5 %copy-start.70 = (f32[48,5,8]{0,2,1:T(8,128)S(1)}, f32[48,5,8]{0,2,1:T(8,128)}, u32[]{:S(2)}) copy-start(f32[48,5,8]{0,2,1:T(8,128)} %param.50) | copy-start | bytes 23044
  853.8 764.3 %copy-start.24 = (f32[4,32,256]{2,1,0:T(8,128)S(1)}, f32[4,32,256]{2,1,0:T(8,128)}, u32[]{:S(2)}) copy-start(f32[4,32,256]{2,1,0:T(8,128)} %param.35) | copy-start | bytes 393220
  853.8 764.3 %copy-start.54 = (f32[4,32,256]{2,1,0:T(8,128)S(1)}, f32[4,32,256]{2,1,0:T(8,128)}, u32[]{:S(2)}) copy-start(f32[4,32,256]{2,1,0:T(8,128)} %param.41) | copy-start | bytes 393220
  853.8 764.3 %copy-start.55 = (f32[4,32,256]{2,1,0:T(8,128)S(1)}, f32[4,32,256]{2,1,0:T(8,128)}, u32[]{:S(2)}) copy-start(f32[4,32,256]{2,1,0:T(8,128)} %param.47) | copy-start | bytes 393220
  853.8 846.4 %copy-start.25 = (f32[4,32,256]{2,1,0:T(8,128)S(1)}, f32[4,32,256]{2,1,0:T(8,128)}, u32[]{:S(2)}) copy-start(f32[4,32,256]{2,1,0:T(8,128)} %param.34) | copy-start | bytes 393220
  853.8 846.4 %copy-start.56 = (f32[4,32,256]{2,1,0:T(8,128)S(1)}, f32[4,32,256]{2,1,0:T(8,128)}, u32[]{:S(2)}) copy-start(f32[4,32,256]{2,1,0:T(8,128)} %param.40) | copy-start | bytes 393220
  853.8 846.3 %copy-start.57 = (f32[4,32,256]{2,1,0:T(8,128)S(1)}, f32[4,32,256]{2,1,0:T(8,128)}, u32[]{:S(2)}) copy-start(f32[4,32,256]{2,1,0:T(8,128)} %param.46) | copy-start | bytes 393220
  853.9 931.6 %copy-start.47 = (f32[2,32,1024]{2,1,0:T(8,128)S(1)}, f32[2,32,1024]{2,1,0:T(8,128)}, u32[]{:S(2)}) copy-start(f32[2,32,1024]{2,1,0:T(8,128)} %param.42) | copy-start | bytes 786436
  853.9 931.6 %copy-start.48 = (f32[2,32,1024]{2,1,0:T(8,128)S(1)}, f32[2,32,1024]{2,1,0:T(8,128)}, u32[]{:S(2)}) copy-start(f32[2,32,1024]{2,1,0:T(8,128)} %param.48) | copy-start | bytes 786436
  853.9 1008.2 %copy-start.106 = (f32[48]{0:T(128)S(1)}, f32[48]{0:T(128)}, u32[]{:S(2)}) copy-start(f32[48]{0:T(128)} %param.33) | copy-start | bytes 580
  856.6 1006.6 %copy-start.61 = (f32[32,48]{1,0:T(8,128)}, f32[32,48]{1,0:T(8,128)S(1)}, u32[]{:S(2)}) copy-start(f32[32,48]{1,0:T(8,128)S(1)} %get-tuple-element.163) | copy-start | bytes 18436
  856.6 1006.6 %copy-start.62 = (f32[32,48]{1,0:T(8,128)}, f32[32,48]{1,0:T(8,128)S(1)}, u32[]{:S(2)}) copy-start(f32[32,48]{1,0:T(8,128)S(1)} %get-tuple-element.164) | copy-start | bytes 18436
  901.2 962.1 %copy-start.82 = (f32[17,8]{0,1:T(8,128)}, f32[17,8]{0,1:T(8,128)S(1)}, u32[]{:S(2)}) copy-start(f32[17,8]{0,1:T(8,128)S(1)} %get-tuple-element.156) | copy-start | bytes 1636
  901.2 962.1 %copy-start.83 = (f32[17,8]{0,1:T(8,128)}, f32[17,8]{0,1:T(8,128)S(1)}, u32[]{:S(2)}) copy-start(f32[17,8]{0,1:T(8,128)S(1)} %get-tuple-element.157) | copy-start | bytes 1636
  1535.7 327.6 %copy-start.59 = (f32[48,5,8]{0,2,1:T(8,128)}, f32[48,5,8]{0,2,1:T(8,128)S(1)}, u32[]{:S(2)}) copy-start(f32[48,5,8]{0,2,1:T(8,128)S(1)} %get-tuple-element.161) | copy-start | bytes 23044
  1535.7 327.6 %copy-start.60 = (f32[48,5,8]{0,2,1:T(8,128)}, f32[48,5,8]{0,2,1:T(8,128)S(1)}, u32[]{:S(2)}) copy-start(f32[48,5,8]{0,2,1:T(8,128)S(1)} %get-tuple-element.162) | copy-start | bytes 23044
  1619.1 244.1 %copy-start.40 = (f32[4,32,256]{2,1,0:T(8,128)}, f32[4,32,256]{2,1,0:T(8,128)S(1)}, u32[]{:S(2)}) copy-start(f32[4,32,256]{2,1,0:T(8,128)S(1)} %get-tuple-element.167) | copy-start | bytes 393220
  1619.1 244.1 %copy-start.41 = (f32[4,32,256]{2,1,0:T(8,128)}, f32[4,32,256]{2,1,0:T(8,128)S(1)}, u32[]{:S(2)}) copy-start(f32[4,32,256]{2,1,0:T(8,128)S(1)} %get-tuple-element.168) | copy-start | bytes 393220
  1701.2 162.1 %copy-start.42 = (f32[4,32,256]{2,1,0:T(8,128)}, f32[4,32,256]{2,1,0:T(8,128)S(1)}, u32[]{:S(2)}) copy-start(f32[4,32,256]{2,1,0:T(8,128)S(1)} %get-tuple-element.169) | copy-start | bytes 393220
  1701.2 162.1 %copy-start.43 = (f32[4,32,256]{2,1,0:T(8,128)}, f32[4,32,256]{2,1,0:T(8,128)S(1)}, u32[]{:S(2)}) copy-start(f32[4,32,256]{2,1,0:T(8,128)S(1)} %get-tuple-element.170) | copy-start | bytes 393220
  1786.7 76.6 %copy-start.36 = (f32[2,32,1024]{2,1,0:T(8,128)}, f32[2,32,1024]{2,1,0:T(8,128)S(1)}, u32[]{:S(2)}) copy-start(f32[2,32,1024]{2,1,0:T(8,128)S(1)} %get-tuple-element.165) | copy-start | bytes 786436
  1786.7 76.6 %copy-start.37 = (f32[2,32,1024]{2,1,0:T(8,128)}, f32[2,32,1024]{2,1,0:T(8,128)S(1)}, u32[]{:S(2)}) copy-start(f32[2,32,1024]{2,1,0:T(8,128)S(1)} %get-tuple-element.166) | copy-start | bytes 786436
  (80 other events, 1123.2 us)
Sparse Core Ops, SparseCore 0:
  10.9 47.6 all-gather.3
  61.5 44.2 all-gather.5
  334.6 19.0 reduce-scatter.12
  371.7 24.7 reduce-scatter.14
  399.3 48.5 all-gather.7
  456.5 21.3 reduce-scatter.16
  564.5 19.2 reduce-scatter.18
  605.6 22.8 reduce-scatter.20
  651.0 22.8 reduce-scatter.22
  678.2 76.4 reduce-scatter.30
  760.7 139.5 all-reduce.4
  902.5 631.7 reduce-scatter.32
  1538.2 79.7 reduce-scatter.26
  1621.9 78.2 reduce-scatter.24
  1704.1 81.2 reduce-scatter.28
where the time goes:
time: 1880 us; the launch traced here: 1870 us
  waiting for transfers between devices  1060 us (56%)
  blocking collectives  342 us (18%)
  local copies, waits for them, and re-layouts  229 us (12%)
  matrix products  123 us (7%)
  other arithmetic  97.3 us (5%)
  between operations  19.2 us (1%)
    reduce_scatter x1, waiting for transfers between devices, on_device(): lax.psum_scatter(grad_embed, ('dp', 'mp'), scatter_dimension=2, tiled=True)  633 us
    psum x2, blocking collectives, on_device(): lax.psum((error_vec, jnp.sum(keep) * mine_vars), ('dp', 'mp'))  131 us
    reduce_scatter x1, waiting for transfers between devices, on_device(): lax.psum_scatter(grad_mlp.astype(jnp.bfloat16), 'dp', scatter_dimension=1...  84.2 us
    reduce_scatter x1, waiting for transfers between devices, on_device(): lax.psum_scatter(grad_attn.astype(jnp.bfloat16), 'dp', scatter_dimension=...  82.4 us
    reduce_scatter x1, waiting for transfers between devices, on_device(): lax.psum_scatter(grad_agg.astype(jnp.bfloat16), 'dp', scatter_dimension=1...  81 us
    all_gather x1, blocking collectives, on_device(): lax.all_gather(embed_weight, ('dp', 'mp'), axis=2, tiled=True)  68.3 us
    reduce_scatter x3, waiting for transfers between devices, reduce_grads(): lax.psum_scatter(term_fn(jnp.int32(0), share * lax.axis_size('mp')).astyp...  63.6 us
    all_gather x1, blocking collectives, on_device(): lax.all_gather(vectors, ('dp', 'mp'), axis=1, tiled=True)  51.3 us
  transfers between devices with their start and end apart: 15, of which 11 were waited for; matrix products, arithmetic and copies ran while one was open for 21% of the time, Pallas kernels for 0%

commit v1 on v0

v1 whole, which is shorter than its diff:
```python
import math

import jax
import jax.numpy as jnp
from jax import lax
from jax.experimental import pallas as pl
from jax.experimental.pallas import tpu as pltpu
from jax.sharding import PartitionSpec as P

D = 1024
HEAD_DIM = 64
FF = 4096
NVAR = 48
P_SIZE = 4
SEGS = 4
LEADS = 28
LATS = 32
STEP = 10
NVEC = 17
EROWS = NVAR * (P_SIZE + 1)

HIGH = lax.Precision.HIGHEST
NORM_EPS = 1e-06
BETA_ONE = 0.9
BETA_TWO = 0.999
LEARN_RATE = 0.3
WEIGHT_DECAY = 0.01
ADAM_EPS = 1e-08
STATS_DECAY = 0.9
MESH = pl.DeviceIdType.MESH
BF = jnp.bfloat16
F32 = jnp.float32

DPN, MPN, CHIPS, SH, TOK, COLS = 32, 4, 16, 64, 256, 256
SCALE = 1.0 / math.sqrt(HEAD_DIM)


def nn(a, b, precision=None):
    return lax.dot_general(
        a, b, (((1,), (0,)), ((), ())), preferred_element_type=F32, precision=precision
    )


def nt(a, b, precision=None):
    return lax.dot_general(
        a, b, (((1,), (1,)), ((), ())), preferred_element_type=F32, precision=precision
    )


def tn(a, b, precision=None):
    return lax.dot_general(
        a, b, (((0,), (0,)), ((), ())), preferred_element_type=F32, precision=precision
    )


def latitude_weights():
    centres = (jnp.arange(LATS, dtype=F32) + 0.5) * (180.0 / LATS) - 90.0
    cosines = jnp.cos(centres * (math.pi / 180.0))
    return cosines / jnp.mean(cosines)


def moments_new(gradient, first, second):
    first_new = BETA_ONE * first + (1.0 - BETA_ONE) * gradient
    second_new = BETA_TWO * second + (1.0 - BETA_TWO) * gradient * gradient
    return first_new, second_new


def adam_direction(weight, gradient, first, second):
    first_new, second_new = moments_new(gradient, first, second)
    first_hat = first_new * (1.0 / (1.0 - BETA_ONE**STEP))
    second_hat = second_new * (1.0 / (1.0 - BETA_TWO**STEP))
    direction = first_hat / (jnp.sqrt(second_hat) + ADAM_EPS) + WEIGHT_DECAY * weight
    return (first_new, second_new, direction)


def iota(shape, dim):
    return lax.broadcasted_iota(jnp.int32, shape, dim)


def ln_parts(x):
    centre = jnp.mean(x, -1, keepdims=True)
    shifted = x - centre
    r = lax.rsqrt(jnp.mean(shifted * shifted, -1, keepdims=True) + NORM_EPS)
    return shifted * r, r


def ln_back(n, r, gain, dh):
    e = dh * gain
    dx = r * (e - jnp.mean(e, -1, keepdims=True) - n * jnp.mean(e * n, -1, keepdims=True))
    dgain = jnp.sum(dh * n, 0, keepdims=True)
    dbias = jnp.sum(dh, 0, keepdims=True)
    return dx, dgain, dbias


def mega(
    tm,
    aggw,
    attnw,
    mlpw,
    headw,
    tfirst,
    tsecond,
    aggf,
    aggs,
    attnf,
    attns,
    mlpf,
    mlps,
    headf,
    heads,
    targ,
    lossw,
    cnt,
    lead,
    segc,
    segr,
    vidx,
    pix,
    o_t,
    o_agg,
    o_attn,
    o_mlp,
    o_head,
    o_stats,
    WA3,
    WB,
    W1,
    W2,
    HW,
    VEC,
    VR,
    VRN,
    TMPV,
    TA,
    TGT,
    PIXT,
    EWP,
    EWH,
    EWC,
    EWR,
    PRP,
    PRH,
    PRC,
    PRR,
    MT,
    PT,
    OAT,
    OA,
    RSS,
    RSR,
    AG,
    QKV,
    PB,
    OB,
    DOB,
    GEL,
    GELP,
    DU,
    LN,
    XS,
    RR,
    GA3,
    GB,
    G1,
    G2,
    GH,
    GVT,
    GVP,
    GVN,
    SA3,
    SB,
    S1,
    S2,
    SHH,
    SV,
    BA3,
    BB,
    B1,
    B2,
    BH,
    BV,
    TG,
    TGR,
    HG,
    HGR,
    NX,
    NXR,
    NY,
    NYR,
    ysend,
    yrecv,
    dsend,
    drecv,
    ssend,
    srecv,
):
    d = lax.axis_index("dp")
    m = lax.axis_index("mp")
    c = lax.rem(d, 2)
    k = d // 2
    sib = d + 1 - 2 * c
    rb = pl.multiple_of(c * 512 + k * 32, 32)
    half = pl.multiple_of(c * 512, 512)
    other = pl.multiple_of(512 - c * 512, 512)
    mine = pl.multiple_of(m * SH, SH)

    def rcopy(src, dst, ss, rs, dp, mp):
        return pltpu.make_async_remote_copy(
            src_ref=src,
            dst_ref=dst,
            send_sem=ss,
            recv_sem=rs,
            device_id={"dp": dp, "mp": mp},
            device_id_type=MESH,
        )

    def drain(ref, sem):
        pltpu.make_async_copy(ref, ref, sem).wait()

    def to_peers(fn):
        for i in (2, 1, 3):
            fn(i, lax.rem(m + i, MPN))

    def to_chips(fn):
        def step(i, carry):
            kk = lax.rem(k + i, CHIPS)
            fn(kk, kk * 2 + c)
            return carry

        lax.fori_loop(1, CHIPS, step, 0)

    def gather_start(buf, g):
        block = buf.at[pl.ds(rb, 32)]
        to_chips(lambda kk, t: rcopy(block, block, dsend.at[g], drecv.at[g], t, m).start())

    def gather_cross(buf, g):
        drain(buf.at[pl.ds(0, 480)], drecv.at[g])
        part = buf.at[pl.ds(half, 512)]
        rcopy(part, part, ssend.at[g], srecv.at[g], sib, m).start()

    def gather_wait(buf, g):
        drain(buf.at[pl.ds(0, 512)], srecv.at[g])

    def gather_end(buf, g):
        drain(buf.at[pl.ds(0, 480)], dsend.at[g])
        drain(buf.at[pl.ds(0, 512)], ssend.at[g])

    def reduce_cross(buf, sbuf, g):
        rcopy(buf.at[pl.ds(other, 512)], sbuf, ssend.at[g], srecv.at[g], sib, m).start()

    def reduce_spread(buf, sbuf, bbuf, g):
        drain(sbuf, srecv.at[g])

        def add(i, carry):
            at = pl.multiple_of(i * 128, 128)
            sbuf[pl.ds(at, 128), :] = (
                sbuf[pl.ds(at, 128), :].astype(F32)
                + buf[pl.ds(pl.multiple_of(half + at, 128), 128), :].astype(F32)
            ).astype(sbuf.dtype)
            return carry

        lax.fori_loop(0, 4, add, 0)
        land = bbuf.at[pl.ds(pl.multiple_of(k * 32, 32), 32)]

        def send(kk, t):
            src = sbuf.at[pl.ds(pl.multiple_of(kk * 32, 32), 32)]
            rcopy(src, land, dsend.at[g], drecv.at[g], t, m).start()

        to_chips(send)

    def reduce_end(buf, sbuf, bbuf, g):
        drain(bbuf.at[pl.ds(0, 480)], drecv.at[g])

        def add(i, acc):
            at = pl.multiple_of(lax.rem(k + i, CHIPS) * 32, 32)
            return acc + bbuf[pl.ds(at, 32), :].astype(F32)

        total = lax.fori_loop(
            1, CHIPS, add, sbuf[pl.ds(pl.multiple_of(k * 32, 32), 32), :].astype(F32)
        )
        drain(bbuf.at[pl.ds(0, 480)], dsend.at[g])
        drain(sbuf, ssend.at[g])
        return total

    def all_sum(src, hbuf, cbuf, res, g, between):
        mine_half = pl.multiple_of(c * 128, 128)
        rcopy(
            src.at[pl.ds(pl.multiple_of(128 - c * 128, 128), 128)],
            hbuf,
            ssend.at[g],
            srecv.at[g],
            sib,
            m,
        ).start()
        drain(hbuf, srecv.at[g])
        hbuf[...] = hbuf[...] + src[pl.ds(mine_half, 128), :]
        at_k = pl.multiple_of(k * 8, 8)

        def send(kk, t):
            rcopy(
                hbuf.at[pl.ds(pl.multiple_of(kk * 8, 8), 8)],
                cbuf.at[pl.ds(at_k, 8)],
                dsend.at[g],
                drecv.at[g],
                t,
                m,
            ).start()

        to_chips(send)
        drain(cbuf.at[pl.ds(0, 120)], drecv.at[g])

        def add(i, acc):
            at = pl.multiple_of(lax.rem(k + i, CHIPS) * 8, 8)
            return acc + cbuf[pl.ds(at, 8), :]

        total = lax.fori_loop(1, CHIPS, add, hbuf[pl.ds(at_k, 8), :])
        block = pl.ds(pl.multiple_of(mine_half + at_k, 8), 8)
        res[block, :] = total
        part = res.at[block]
        to_chips(lambda kk, t: rcopy(part, part, dsend.at[g + 1], drecv.at[g + 1], t, m).start())
        between()
        drain(res.at[pl.ds(0, 120)], drecv.at[g + 1])
        part2 = res.at[pl.ds(mine_half, 128)]
        rcopy(part2, part2, ssend.at[g + 1], srecv.at[g + 1], sib, m).start()
        drain(res.at[pl.ds(0, 128)], srecv.at[g + 1])
        drain(hbuf, ssend.at[g])
        drain(res.at[pl.ds(0, 128)], ssend.at[g + 1])
        drain(cbuf.at[pl.ds(0, 120)], dsend.at[g])
        drain(res.at[pl.ds(0, 120)], dsend.at[g + 1])

    def branch_start(ix, tile_fn):
        def step(n, carry):
            RSS[ix, n] = tile_fn(pl.multiple_of(n * 256, 256)).astype(BF)

            def send(i, t):
                rcopy(
                    RSS.at[ix, n, pl.ds(pl.multiple_of(t * SH, SH), SH)],
                    RSR.at[ix, i - 1, n],
                    ysend.at[3 + ix],
                    yrecv.at[3 + ix],
                    d,
                    t,
                ).start()

            to_peers(send)
            return carry

        lax.fori_loop(0, 4, step, 0)

    def branch_sum(ix):
        drain(RSR.at[ix], yrecv.at[3 + ix])
        parts = []
        for n in range(4):
            acc = RSS[ix, n, pl.ds(mine, SH), :].astype(F32)
            for i in range(3):
                acc = acc + RSR[ix, i, n].astype(F32)
            parts.append(acc)
        return jnp.concatenate(parts, 1)

    def share_start(ix, values):
        AG[ix, pl.ds(mine, SH), :] = values
        block = AG.at[ix, pl.ds(mine, SH)]
        to_peers(
            lambda i, t: rcopy(block, block, ysend.at[8 + ix], yrecv.at[8 + ix], d, t).start()
        )

    def share_wait(ix):
        drain(AG.at[ix, pl.ds(0, 192)], yrecv.at[8 + ix])

    aw = [aggw[j].astype(BF) for j in range(3)]
    WA3[pl.ds(rb, 32), :] = aggw[3].astype(BF)
    for j in range(4):
        WB[pl.ds(rb, 32), j * 256 : (j + 1) * 256] = attnw[j].astype(BF)
    W1[pl.ds(rb, 32), :] = mlpw[0].astype(BF)
    W2[pl.ds(rb, 32), :] = mlpw[1].astype(BF)
    my_slot = pl.ds(pl.multiple_of(m * 128, 128), 128)
    HW[pl.ds(rb, 32), my_slot] = headw[...].astype(BF)
    vhot = (iota((256, 256), 0) == vidx[...]).astype(F32)
    my_eight = pl.ds(pl.multiple_of(m * 8, 8), 8)
    TA[my_eight, 0:256] = nn(tm[:, 0:256], vhot, HIGH)
    TA[my_eight, 256:384] = tm[:, 256:384]
    TGT[m] = targ[pl.ds(mine, SH), :]
    GVP[...] = jnp.zeros_like(GVP)
    GVN[...] = jnp.zeros_like(GVN)

    bar = pltpu.get_barrier_semaphore()

    def greet(i, carry):
        pl.semaphore_signal(
            bar, inc=1, device_id={"dp": lax.rem(d + i, DPN), "mp": m}, device_id_type=MESH
        )
        return carry

    lax.fori_loop(1, DPN, greet, 0)
    for i in range(1, MPN):
        pl.semaphore_signal(
            bar, inc=1, device_id={"dp": d, "mp": lax.rem(m + i, MPN)}, device_id_type=MESH
        )
    pl.semaphore_wait(bar, DPN + MPN - 2)

    def first_sends(i, t):
        part = TA.at[my_eight]
        rcopy(part, part, ysend.at[0], yrecv.at[0], d, t).start()
        slot = HW.at[pl.ds(rb, 32), my_slot]
        rcopy(slot, slot, ysend.at[1], yrecv.at[1], d, t).start()
        rcopy(
            targ.at[pl.ds(pl.multiple_of(t * SH, SH), SH)],
            TGT.at[m],
            ysend.at[2],
            yrecv.at[2],
            d,
            t,
        ).start()

    to_peers(first_sends)
    gather_start(WA3, 0)

    rows = iota((256, 192), 0)
    cols = iota((256, 192), 1)
    pick = (rows < 192) & ((lax.rem(rows, NVAR) * P_SIZE + rows // NVAR) == cols)
    pixt = nt(pick.astype(BF), pix[...])
    row_at = iota((256, TOK), 0)
    PIXT[...] = jnp.where(row_at < 192, pixt, jnp.where(row_at < EROWS, 1.0, 0.0))

    drain(TA.at[pl.ds(0, 24)], yrecv.at[0])
    drain(HW.at[pl.ds(0, 32), pl.ds(0, 384)], yrecv.at[1])
    VEC[pl.ds(rb, 32), :] = TA[:, 256:384]
    emb = TA[:, 0:256]
    EWP[:, 0:256] = tn(emb, aw[1].astype(F32), HIGH)
    EWP[:, 256:512] = tn(emb, aw[2].astype(F32), HIGH)
    EWP[240:241, 0:256] = jnp.sum(TA[:, 256:257] * aw[0].astype(F32), 0, keepdims=True)
    EWP[241:242, 0:128] = cnt[...]

    def bulk():
        gather_start(VEC, 2)
        gather_start(WB, 1)
        gather_start(W1, 3)
        gather_start(W2, 4)
        gather_start(HW, 5)

    all_sum(EWP, EWH, EWC, EWR, 6, bulk)

    head_of = (iota((256, 128), 0) // HEAD_DIM == iota((256, 128), 1)).astype(F32)
    qa = EWR[240:241, 0:256].astype(BF).astype(F32)
    total_count = EWR[241:242, 0:1]
    qe = nn(EWR[:, 0:256] * (qa * SCALE), head_of, HIGH)
    ewv = EWR[:, 256:512].astype(BF)
    for h in range(4):
        scores = PIXT[0:48, :] * qe[0:48, h : h + 1]
        for p in range(1, 5):
            at = slice(p * 48, (p + 1) * 48)
            scores = scores + PIXT[at, :] * qe[at, h : h + 1]
        e = jnp.exp(scores - jnp.max(scores, 0, keepdims=True))
        probs = e / jnp.sum(e, 0, keepdims=True)
        PT[h] = probs
        probs = probs.astype(BF).astype(F32)
        for p in range(5):
            at = slice(p * 48, (p + 1) * 48)
            MT[h, at, :] = (probs * PIXT[at, :]).astype(BF)
        MT[h, 240:256, :] = jnp.zeros((16, TOK), BF)
        OAT[h * 64 : (h + 1) * 64, :] = tn(ewv[:, h * 64 : (h + 1) * 64], MT[h])
    OA[...] = OAT[...].T.astype(BF)

    gather_cross(WA3, 0)
    gather_wait(WA3, 0)
    branch_start(0, lambda at: nt(OA[...], WA3[pl.ds(at, 256), :]))
    gather_cross(VEC, 2)
    gather_wait(VEC, 2)
    VR[...] = VEC[...].T

    def natural(i, carry):
        at = pl.multiple_of(lax.rem(i, 2) * 512 + (i // 2) * 32, 32)
        TMPV[pl.ds(pl.multiple_of(i * 32, 32), 32), :] = VEC[pl.ds(at, 32), :]
        return carry

    lax.fori_loop(0, DPN, natural, 0)
    VRN[...] = TMPV[...].T

    def vrow(i):
        return VR[i : i + 1, :]

    leads = lead[...]
    x0 = branch_sum(0) + vrow(1) + leads * vrow(2)
    n1, r1 = ln_parts(x0)
    LN[0] = n1
    RR[0] = jnp.broadcast_to(r1, (SH, 128))
    XS[...] = x0
    share_start(0, (n1 * vrow(3) + vrow(4)).astype(BF))
    gather_cross(WB, 1)
    gather_wait(WB, 1)
    share_wait(0)

    my_cols = pl.ds(pl.multiple_of(m * COLS, COLS), COLS)
    h1 = AG[0]
    QKV[0] = (nn(h1, WB[:, 0:256]) + VRN[5:6, my_cols]).astype(BF)
    QKV[1] = nn(h1, WB[:, 256:512]).astype(BF)
    QKV[2] = (nn(h1, WB[:, 512:768]) + VRN[6:7, my_cols]).astype(BF)
    same = segc[...] == segr[...]
    for h in range(4):
        at = slice(h * 64, (h + 1) * 64)
        scores = nt(QKV[0, :, at], QKV[1, :, at]) * SCALE
        scores = jnp.where(same, scores, -1e30)
        e = jnp.exp(scores - jnp.max(scores, 1, keepdims=True))
        probs = e / jnp.sum(e, 1, keepdims=True)
        PB[h] = probs
        OB[:, at] = nn(probs.astype(BF), QKV[2, :, at]).astype(BF)
    branch_start(1, lambda at: nt(OB[...], WB[pl.ds(at, 256), 768:1024]))
    gather_cross(W1, 3)
    x1 = XS[...] + branch_sum(1) + vrow(7)
    n2, r2 = ln_parts(x1)
    LN[1] = n2
    RR[1] = jnp.broadcast_to(r2, (SH, 128))
    XS[...] = x1
    share_start(1, (n2 * vrow(8) + vrow(9)).astype(BF))
    gather_wait(W1, 3)
    share_wait(1)

    def inner(n, carry):
        at = pl.ds(pl.multiple_of(n * 256, 256), 256)
        u = nn(AG[1], W1[:, at]) + VRN[pl.ds(10 + m, 1), at]
        phi = 0.5 * (1.0 + lax.erf(u * (1.0 / math.sqrt(2.0))))
        GEL[:, at] = (u * phi).astype(BF)
        GELP[:, at] = phi + u * jnp.exp(-0.5 * u * u) * (1.0 / math.sqrt(2.0 * math.pi))
        return carry

    lax.fori_loop(0, 4, inner, 0)
    gather_cross(W2, 4)
    gather_wait(W2, 4)
    branch_start(2, lambda at: nt(GEL[...], W2[pl.ds(at, 256), :]))
    gather_cross(HW, 5)
    gather_wait(HW, 5)
    x2 = XS[...] + branch_sum(2) + vrow(14)
    n3, r3 = ln_parts(x2)
    h3 = (n3 * vrow(15) + vrow(16)).astype(BF)

    drain(TGT.at[pl.ds(0, 3)], yrecv.at[2])
    pred = nn(h3, HW[...])
    weight = lossw[...]
    dpreds = []
    NX[...] = jnp.zeros_like(NX)
    for j in range(4):
        misfit = pred[:, j * 128 : (j + 1) * 128] - TGT[j]
        weighted = weight * misfit
        NX[4 + j : 5 + j, :] = jnp.sum(weighted * misfit, 0, keepdims=True)
        dpreds.append((2.0 * weighted / total_count).astype(BF))
    dpred = jnp.concatenate(dpreds, 1)
    dh3 = nt(dpred, HW[...])
    dx2, dgain, dbias = ln_back(n3, r3, vrow(15), dh3)
    share_start(2, dx2.astype(BF))
    GVP[14:15, :] = jnp.sum(dx2, 0, keepdims=True)
    GVP[15:16, :] = dgain
    GVP[16:17, :] = dbias
    GH[...] = tn(h3, dpred).astype(BF)
    XS[...] = dx2
    reduce_cross(GH, SHH, 14)
    share_wait(2)

    def back_inner(n, carry):
        at = pl.ds(pl.multiple_of(n * 256, 256), 256)
        du = (nn(AG[2], W2[:, at]) * GELP[:, at]).astype(BF)
        DU[:, at] = du
        GVN[pl.ds(10 + m, 1), at] = jnp.sum(du.astype(F32), 0, keepdims=True)
        return carry

    lax.fori_loop(0, 4, back_inner, 0)
    branch_start(3, lambda at: nt(DU[...], W1[pl.ds(at, 256), :]))

    def weight_grad(dst, left_fn, right):
        def step(n, carry):
            at = pl.multiple_of(n * 256, 256)
            dst[pl.ds(at, 256), :] = tn(left_fn(pl.ds(at, 256)), right[...]).astype(BF)
            return carry

        lax.fori_loop(0, 4, step, 0)

    weight_grad(G2, lambda at: AG[2, :, at], GEL)
    reduce_cross(G2, S2, 13)
    reduce_spread(GH, SHH, BH, 14)
    dx1, dgain, dbias = ln_back(LN[1], RR[1, :, 0:1], vrow(8), branch_sum(3))
    dx1 = dx1 + XS[...]
    share_start(3, dx1.astype(BF))
    GVP[7:8, :] = jnp.sum(dx1, 0, keepdims=True)
    GVP[8:9, :] = dgain
    GVP[9:10, :] = dbias
    XS[...] = dx1
    reduce_spread(G2, S2, B2, 13)
    weight_grad(G1, lambda at: AG[1, :, at], DU)
    reduce_cross(G1, S1, 12)
    share_wait(3)

    DOB[...] = nn(AG[3], WB[:, 768:1024]).astype(BF)
    for h in range(4):
        at = slice(h * 64, (h + 1) * 64)
        probs = PB[h]
        dout = DOB[:, at]
        dv = tn(probs.astype(BF), dout).astype(BF)
        dprob = nt(dout, QKV[2, :, at])
        ds = (probs * (dprob - jnp.sum(probs * dprob, 1, keepdims=True))).astype(BF)
        dq = (nn(ds, QKV[1, :, at]) * SCALE).astype(BF)
        dk = (tn(ds, QKV[0, :, at]) * SCALE).astype(BF)
        DU[:, h * 64 : (h + 1) * 64] = dq
        DU[:, 256 + h * 64 : 256 + (h + 1) * 64] = dk
        DU[:, 512 + h * 64 : 512 + (h + 1) * 64] = dv
    branch_start(4, lambda at: nt(DU[:, 0:768], WB[pl.ds(at, 256), 0:768]))
    GVN[5:6, my_cols] = jnp.sum(DU[:, 0:256].astype(F32), 0, keepdims=True)
    GVN[6:7, my_cols] = jnp.sum(DU[:, 512:768].astype(F32), 0, keepdims=True)
    reduce_spread(G1, S1, B1, 12)

    def attn_grad(n, carry):
        at = pl.ds(pl.multiple_of(n * 256, 256), 256)
        GB[at, 0:768] = tn(AG[0, :, at], DU[:, 0:768]).astype(BF)
        GB[at, 768:1024] = tn(AG[3, :, at], OB[...]).astype(BF)
        return carry

    lax.fori_loop(0, 4, attn_grad, 0)
    reduce_cross(GB, SB, 11)
    dx0, dgain, dbias = ln_back(LN[0], RR[0, :, 0:1], vrow(3), branch_sum(4))
    dx0 = dx0 + XS[...]
    share_start(4, dx0.astype(BF))
    GVP[1:2, :] = jnp.sum(dx0, 0, keepdims=True)
    GVP[2:3, :] = jnp.sum(leads * dx0, 0, keepdims=True)
    GVP[3:4, :] = dgain
    GVP[4:5, :] = dbias
    TMPV[...] = GVN[...].T
    GVT[...] = GVP[...].T

    def permuted(i, carry):
        at = pl.ds(pl.multiple_of(lax.rem(i, 2) * 512 + (i // 2) * 32, 32), 32)
        GVT[at, :] = GVT[at, :] + TMPV[pl.ds(pl.multiple_of(i * 32, 32), 32), :]
        return carry

    lax.fori_loop(0, DPN, permuted, 0)
    reduce_cross(GVT, SV, 15)
    reduce_spread(GB, SB, BB, 11)
    reduce_spread(GVT, SV, BV, 15)
    share_wait(4)

    DOB[...] = nn(AG[4], WA3[...]).astype(BF)
    PRP[...] = jnp.zeros_like(PRP)
    for h in range(4):
        at = slice(h * 64, (h + 1) * 64)
        dout = DOB[:, at]
        through = nt(ewv[:, at], dout)
        dprob = PIXT[0:48, :] * through[0:48, :]
        for p in range(1, 5):
            row = slice(p * 48, (p + 1) * 48)
            dprob = dprob + PIXT[row, :] * through[row, :]
        probs = PT[h]
        ds = (probs * (dprob - jnp.sum(probs * dprob, 0, keepdims=True))).astype(BF).astype(F32)
        for p in range(5):
            row = slice(p * 48, (p + 1) * 48)
            PRP[row, 256 + h : 257 + h] = jnp.sum(ds * PIXT[row, :], 1, keepdims=True)
        PRP[:, at] = nn(MT[h], dout)

    def agg_grad():
        weight_grad(GA3, lambda at: AG[4, :, at], OA)
        reduce_cross(GA3, SA3, 10)
        reduce_spread(GA3, SA3, BA3, 10)

    all_sum(PRP, PRH, PRC, PRR, 8, agg_grad)

    spread = nt(PRR[:, 256:384], head_of, HIGH)
    dqa = jnp.sum(spread * EWR[:, 0:256], 0, keepdims=True) * SCALE
    pk = spread * (qa * SCALE)
    pv = PRR[:, 0:256]
    emb = TA[:, 0:256]
    wa = [aggw[j].astype(BF).astype(F32) for j in range(3)]
    TG[:, 0:256] = nt(wa[1], pk, HIGH) + nt(wa[2], pv, HIGH)
    TG[:, 256:384] = reduce_end(GVT, SV, BV, 15)
    TG[:, 256:257] = TG[:, 256:257] + jnp.sum(wa[0] * dqa, 1, keepdims=True)
    HG[...] = reduce_end(GH, SHH, BH, 14)

    def last_sends(i, t):
        rcopy(
            TG.at[pl.ds(pl.multiple_of(t * 8, 8), 8)],
            TGR.at[i - 1],
            ysend.at[13],
            yrecv.at[13],
            d,
            t,
        ).start()
        rcopy(
            HG.at[:, pl.ds(pl.multiple_of(t * 128, 128), 128)],
            HGR.at[i - 1],
            ysend.at[14],
            yrecv.at[14],
            d,
            t,
        ).start()

    to_peers(last_sends)

    lanes = iota((1, 128), 1)

    def square_sum(values):
        return jnp.sum(jnp.sum(values * values, 1, keepdims=True), 0, keepdims=True)

    wrow = jnp.zeros((1, 128), F32)
    urow = jnp.zeros((1, 128), F32)

    def tensor(index, weight, gradient, first, second):
        unused, unused2, direction = adam_direction(weight, gradient, first, second)
        here = lanes == index
        return (
            wrow + jnp.where(here, square_sum(weight), 0.0),
            urow + jnp.where(here, square_sum(direction), 0.0),
        )

    o_agg[0] = TA[:, 256:257] * dqa
    o_agg[1] = nn(emb, pk, HIGH)
    o_agg[2] = nn(emb, pv, HIGH)
    gsum = reduce_end(GB, SB, BB, 11)
    for j in range(4):
        o_attn[j] = gsum[:, j * 256 : (j + 1) * 256]
    o_mlp[0] = reduce_end(G1, S1, B1, 12)
    o_mlp[1] = reduce_end(G2, S2, B2, 13)
    o_agg[3] = reduce_end(GA3, SA3, BA3, 10)
    for j in range(4):
        wrow, urow = tensor(j, aggw[j], o_agg[j], aggf[j], aggs[j])
        wrow, urow = tensor(4 + j, attnw[j], o_attn[j], attnf[j], attns[j])
    for j in range(2):
        wrow, urow = tensor(8 + j, mlpw[j], o_mlp[j], mlpf[j], mlps[j])

    drain(HGR, yrecv.at[14])
    o_head[...] = HG[:, my_slot] + HGR[0] + HGR[1] + HGR[2]
    wrow, urow = tensor(10, headw[...], o_head[...], headf[...], heads[...])
    drain(TGR, yrecv.at[13])
    tgrad = TG[my_eight, :] + TGR[0] + TGR[1] + TGR[2]
    o_t[:, 0:256] = nt(tgrad[:, 0:256], vhot, HIGH)
    o_t[:, 256:384] = tgrad[:, 256:384]
    wrow, urow = tensor(
        11, tm[:, 0:256], o_t[:, 0:256], tfirst[:, 0:256], tsecond[:, 0:256]
    )
    vec_at = slice(256, 384)
    unused, unused2, direction = adam_direction(
        tm[:, vec_at], o_t[:, vec_at], tfirst[:, vec_at], tsecond[:, vec_at]
    )
    NX[0:1, :] = wrow
    NX[1:2, :] = urow
    NX[2:3, :] = jnp.sum(tm[:, vec_at] * tm[:, vec_at], 0, keepdims=True)
    NX[3:4, :] = jnp.sum(direction * direction, 0, keepdims=True)

    to_peers(lambda i, t: rcopy(NX, NXR.at[i - 1], ysend.at[15], yrecv.at[15], d, t).start())
    drain(NXR, yrecv.at[15])
    NY[...] = NX[...] + NXR[0] + NXR[1] + NXR[2]
    at_d = pl.ds(pl.multiple_of(d * 8, 8), 8)

    def norm_send(i, carry):
        t = lax.rem(d + i, DPN)
        rcopy(NY, NYR.at[at_d], dsend.at[16], drecv.at[16], t, m).start()
        return carry

    lax.fori_loop(1, DPN, norm_send, 0)
    drain(NYR.at[pl.ds(0, 248)], drecv.at[16])

    def norm_add(i, acc):
        at = pl.multiple_of(lax.rem(d + i, DPN) * 8, 8)
        return acc + NYR[pl.ds(at, 8), :]

    o_stats[...] = lax.fori_loop(1, DPN, norm_add, NY[...])
    o_stats[0:1, :] = jnp.where(lanes == 127, total_count, o_stats[0:1, :])

    for buf, g in ((WA3, 0), (WB, 1), (VEC, 2), (W1, 3), (W2, 4), (HW, 5)):
        gather_end(buf, g)
    drain(NYR.at[pl.ds(0, 248)], dsend.at[16])
    drain(TA.at[pl.ds(0, 24)], ysend.at[0])
    drain(HW.at[pl.ds(0, 32), pl.ds(0, 384)], ysend.at[1])
    drain(TGT.at[pl.ds(0, 3)], ysend.at[2])
    for ix in range(5):
        drain(RSR.at[ix], ysend.at[3 + ix])
        drain(AG.at[ix, pl.ds(0, 192)], ysend.at[8 + ix])
    drain(TGR, ysend.at[13])
    drain(HGR, ysend.at[14])
    drain(NXR, ysend.at[15])


def mega_call(inputs):
    vm = pltpu.VMEM
    dma = pltpu.SemaphoreType.DMA
    scratch = [
        vm((D, 256), BF),
        vm((D, 1024), BF),
        vm((D, 1024), BF),
        vm((D, 1024), BF),
        vm((D, 512), BF),
        vm((D, 128), F32),
        vm((128, D), F32),
        vm((128, D), F32),
        vm((D, 128), F32),
        vm((32, 384), F32),
        vm((4, SH, 128), F32),
        vm((256, TOK), F32),
        vm((256, 512), F32),
        vm((128, 512), F32),
        vm((128, 512), F32),
        vm((256, 512), F32),
        vm((256, 384), F32),
        vm((128, 384), F32),
        vm((128, 384), F32),
        vm((256, 384), F32),
        vm((4, 256, TOK), BF),
        vm((4, NVAR, TOK), F32),
        vm((256, TOK), F32),
        vm((TOK, 256), BF),
        vm((5, 4, TOK, 256), BF),
        vm((5, 3, 4, SH, 256), BF),
        vm((5, TOK, D), BF),
        vm((3, TOK, 256), BF),
        vm((4, TOK, TOK), F32),
        vm((TOK, 256), BF),
        vm((TOK, 256), BF),
        vm((TOK, 1024), BF),
        vm((TOK, 1024), F32),
        vm((TOK, 1024), BF),
        vm((2, SH, D), F32),
        vm((SH, D), F32),
        vm((2, SH, 128), F32),
        vm((D, 256), BF),
        vm((D, 1024), BF),
        vm((D, 1024), BF),
        vm((D, 1024), BF),
        vm((D, 512), BF),
        vm((D, 128), F32),
        vm((128, D), F32),
        vm((128, D), F32),
    ]
    for number in range(2):
        scratch += [
            vm((512, 256), BF),
            vm((512, 1024), BF),
            vm((512, 1024), BF),
            vm((512, 1024), BF),
            vm((512, 512), BF),
            vm((512, 128), F32),
        ]
    scratch += [
        vm((32, 384), F32),
        vm((3, 8, 384), F32),
        vm((32, 512), F32),
        vm((3, 32, 128), F32),
        vm((8, 128), F32),
        vm((3, 8, 128), F32),
        vm((8, 128), F32),
        vm((256, 128), F32),
        dma((16,)),
        dma((16,)),
        dma((17,)),
        dma((17,)),
        dma((16,)),
        dma((16,)),
    ]
    out_shape = (
        jax.ShapeDtypeStruct((8, 384), F32),
        jax.ShapeDtypeStruct((4, 32, 256), F32),
        jax.ShapeDtypeStruct((4, 32, 256), F32),
        jax.ShapeDtypeStruct((2, 32, 1024), F32),
        jax.ShapeDtypeStruct((32, 128), F32),
        jax.ShapeDtypeStruct((8, 128), F32),
    )
    return pl.pallas_call(
        mega,
        out_shape=out_shape,
        in_specs=[pl.BlockSpec(memory_space=pltpu.VMEM)] * len(inputs),
        out_specs=tuple(pl.BlockSpec(memory_space=pltpu.VMEM) for _ in out_shape),
        scratch_shapes=scratch,
        compiler_params=pltpu.CompilerParams(
            collective_id=0, has_side_effects=True, vmem_limit_bytes=60 * 2**20
        ),
        name="step",
    )(*inputs)


def to_table(embed, vecs):
    rows = embed.transpose(2, 1, 0).reshape(8, EROWS)
    return jnp.concatenate(
        [rows, jnp.zeros((8, 16), F32), vecs.T, jnp.zeros((8, 128 - NVEC), F32)], 1
    )


def wide(values):
    return jnp.pad(values, ((0, 0), (0, 128 - values.shape[1])))


def on_device(
    pixels,
    targets,
    valid_mask,
    segments,
    lead_index,
    latitude,
    var_ids,
    running_error,
    agg_weight,
    attn_weight,
    mlp_weight,
    head_weight,
    embed_weight,
    vectors,
    agg_first,
    attn_first,
    mlp_first,
    head_first,
    embed_first,
    vector_first,
    agg_second,
    attn_second,
    mlp_second,
    head_second,
    embed_second,
    vector_second,
):
    m = lax.axis_index("mp")
    keep = valid_mask.astype(F32)
    count = jnp.sum(keep) * NVAR
    keep_mine = lax.dynamic_slice_in_dim(keep, m * SH, SH, 0)
    lat_mine = lax.dynamic_slice_in_dim(latitude, m * SH, SH, 0)
    lat_hot = (lat_mine[:, None] == jnp.arange(LATS, dtype=jnp.int32)[None, :]).astype(F32)
    lat_w = jnp.sum(lat_hot * latitude_weights()[None, :], 1, keepdims=True)
    loss_weight = wide(jnp.tile(lat_w * keep_mine, (1, NVAR // 4)))
    seg = segments[0]
    seg_mine = lax.dynamic_slice_in_dim(seg, m * SH, SH, 0)
    crop_hot = (seg_mine[:, None] == jnp.arange(SEGS, dtype=jnp.int32)[None, :]).astype(F32)
    lead_values = (lead_index[0] + 1).astype(F32) / LEADS
    lead_mine = jnp.sum(crop_hot * lead_values[None, :], 1, keepdims=True)
    at = jnp.arange(256, dtype=jnp.int32)
    vidx = jnp.where(at < EROWS, at - at % NVAR + jnp.tile(var_ids, 6)[:256], at)[None, :]

    table = to_table(embed_weight, vectors)
    inputs = (
        table,
        agg_weight,
        attn_weight,
        mlp_weight,
        wide(head_weight),
        to_table(embed_first, vector_first),
        to_table(embed_second, vector_second),
        agg_first,
        agg_second,
        attn_first,
        attn_second,
        mlp_first,
        mlp_second,
        wide(head_first),
        wide(head_second),
        wide(targets),
        loss_weight,
        jnp.broadcast_to(count, (1, 128)),
        lead_mine,
        seg[:, None],
        seg[None, :],
        vidx,
        pixels,
    )
    g_table, g_agg, g_attn, g_mlp, g_head, stats = mega_call(inputs)

    g_embed = g_table[:, :EROWS].reshape(8, P_SIZE + 1, NVAR).transpose(2, 1, 0)
    g_vec = g_table[:, 256 : 256 + NVEC].T
    weight_norms = jnp.sqrt(jnp.concatenate([stats[0, :12], stats[2, :NVEC]]))
    trust = weight_norms / jnp.sqrt(jnp.concatenate([stats[1, :12], stats[3, :NVEC]]))
    error_all = jnp.sum(stats[4:8, : NVAR].reshape(4, 12, 4), -1).reshape(NVAR)
    total_count = stats[0, 127]

    def finish(weight, gradient, first, second, ratio):
        f, s, u = adam_direction(weight, gradient, first, second)
        return f, s, weight - LEARN_RATE * ratio * u

    done = [
        finish(agg_weight, g_agg, agg_first, agg_second, trust[0:4].reshape(4, 1, 1)),
        finish(attn_weight, g_attn, attn_first, attn_second, trust[4:8].reshape(4, 1, 1)),
        finish(mlp_weight, g_mlp, mlp_first, mlp_second, trust[8:10].reshape(2, 1, 1)),
        finish(head_weight, g_head[:, :48], head_first, head_second, trust[10]),
        finish(embed_weight, g_embed, embed_first, embed_second, trust[11]),
        finish(vectors, g_vec, vector_first, vector_second, trust[12:].reshape(NVEC, 1)),
    ]
    loss_sum = jnp.sum(error_all)
    running_out = STATS_DECAY * running_error + (1.0 - STATS_DECAY) * error_all * (
        NVAR / total_count
    )
    return (
        loss_sum,
        total_count,
        running_out,
        trust,
        weight_norms,
        *[item[0] for item in done],
        *[item[1] for item in done],
        *[item[2] for item in done],
    )


def solution(mesh):
    weights = (
        P(None, "dp", "mp"),
        P(None, "dp", "mp"),
        P(None, "dp", "mp"),
        P("dp", "mp"),
        P(None, None, ("dp", "mp")),
        P(None, ("dp", "mp")),
    )
    in_specs = (
        P("dp", None),
        P("dp", "mp"),
        P("dp", None),
        P("dp", None),
        P("dp", None),
        P("dp"),
        P(),
        P(),
        *weights,
        *weights,
        *weights,
    )
    out_specs = (P(), P(), P(), P(), P(), *weights, *weights, *weights)
    return jax.shard_map(
        on_device, mesh=mesh, in_specs=in_specs, out_specs=out_specs, check_vma=False
    )
```

time: 1880 us -> 196 us (0.10)
  waiting for transfers between devices: 1060 us -> 0 us
  blocking collectives: 342 us -> 0 us
  local copies, waits for them, and re-layouts: 229 us -> 12.9 us
  Pallas kernels: 0 us -> 168 us
  matrix products: 123 us -> 0 us
  other arithmetic: 97.3 us -> 10.5 us
    reduce_scatter x11 -> x0, waiting for transfers between devices: 976 us -> none  [the longest x1 633 us: on_device(): lax.psum_scatter(grad_embed, ('dp', 'mp'), scatter_dimension=2, tiled=True)]
    all_gather x9 -> x0, blocking collectives: 211 us -> none  [the longest x1 68.3 us: on_device(): lax.all_gather(embed_weight, ('dp', 'mp'), axis=2, tiled=True)]
    pallas_call x0 -> x1, Pallas kernels: none -> 168 us  [mega_call(): pl.pallas_call(mega, out_shape=out_shape, in_specs=[pl.BlockSpec(memory_s...]
    psum x2 -> x0, blocking collectives: 131 us -> none  [on_device(): lax.psum((error_vec, jnp.sum(keep) * mine_vars), ('dp', 'mp'))]
    dot_general x39 -> x0, matrix products: 123 us -> none  [the longest x1 24.9 us: on_device(): jnp.dot(flat_v, kv_weight, preferred_element_type=wide_type)]
    reshape x7 -> x5, local copies, waits for them, and re-layouts: 77.4 us -> 0.37 us  [the longest x3 0.22 us: to_table(): rows = embed.transpose(2, 1, 0).reshape(8, EROWS)]
    unnamed x4 -> x0, other arithmetic: 44.7 us -> none
    unnamed x16 -> x0, waiting for transfers between devices: 43.9 us -> none
  transfers between devices with their start and end apart: 15 -> 0, of which waited for: 11 -> 0; matrix products, arithmetic and copies ran while one was open for 21% -> 0% of each run, Pallas kernels for 0% -> 0%
where the time goes in v1:
time: 196 us
  Pallas kernels  168 us (86%)
  local copies, waits for them, and re-layouts  12.9 us (7%)
  other arithmetic  10.5 us (5%)
  between operations  4.23 us (2%)
    pallas_call x1, Pallas kernels, mega_call(): pl.pallas_call(mega, out_shape=out_shape, in_specs=[pl.BlockSpec(memory_s...  168 us
    sub x5, other arithmetic, finish(): return (f, s, weight - LEARN_RATE * ratio * u)  4.94 us
    unnamed x64, local copies, waits for them, and re-layouts  4.89 us

profile of v1, /device:TPU:1, one launch (start us, length us, event | category | flops | bytes accessed | tf_op | source)
XLA Modules:
  0.0 195.6 jit_solution(170084589100364415)
XLA Ops:
  0.7 0.7 copy.89
  1.4 0.1 reshape.101
  1.5 0.1 pad.38.clone
  1.6 0.1 pad.36.clone
  1.6 0.5 copy-done.12
  2.1 0.1 reshape.100
  2.2 0.6 copy-done.13
  3.0 0.6 copy-done.19
  3.6 0.6 maximum_maximum_fusion.2
  4.2 0.1 copy-done.14
  4.3 0.6 pad.18.headw
  4.9 0.1 copy-done.15
  5.0 0.6 pad.19.headf
  5.6 0.1 copy-done.16
  5.8 0.6 pad.20.heads
  6.4 0.1 copy.90
  6.5 0.7 pad.21.targ
  7.2 0.7 fusion.10
  8.5 0.6 copy-done.28
  9.2 0.1 select_reduce_fusion
  9.3 0.1 dynamic-slice_multiply_fusion
  9.4 0.1 copy.91
  9.5 0.6 pad.22.lossw
  10.1 0.6 convert_reduce_fusion
  11.4 0.5 broadcast_in_dim.6.cnt
  11.9 0.1 dynamic-slice_bitcast_fusion
  12.0 0.1 select_reduce_fusion.1
  12.1 0.7 copy.92.lead
  12.8 0.8 copy.93.segc
  13.6 0.1 tile.21
  13.7 0.6 compare_select_fusion
  14.2 0.8 copy.94.pix
  15.0 168.0 %step.1 = (f32[8,384]{1,0:T(8,128)}, f32[4,32,256]{2,1,0:T(8,128)}, f32[4,32,256]{2,1,0:T(8,128)}, f32[2,32,1024]{2,1,0:T(8,128)}, f32[32,128]{1,0:T(8,128)}, /*index=5*/f32[8,128]{1,0:T(8,128)}) custom-call(f32[8,384]{1,0:T(8,128)} %get-tuple-element.109.tm, f32[4,32,256]{2,1,0:T(8,128)} %aggw.1, f32[4,32,256]{2,1,0:T(8,128)} %attnw.1, ...), custom_call_target="tpu_custom_call" | custom-call | tf_op jit(solution)/shard_map/step/pallas_call | solution.py:860
  183.0 1.3 fusion.19
  184.4 0.6 slice.50
  185.0 0.1 reshape.102
  185.0 0.1 reduce_sum.59
  185.9 0.1 mul.395
  185.9 0.6 copy-done.30
  186.5 0.5 multiply_add_fusion.4
  187.0 0.6 fusion.9
  187.8 2.0 %multiply_subtract_fusion.1 = (f32[4,32,256]{2,1,0:T(8,128)}, f32[4,32,256]{2,1,0:T(8,128)}, f32[4,32,256]{2,1,0:T(8,128)}, f32[4,32,256]{2,1,0:T(8,128)}, f32[4,32,256]{2,1,0:T(8,128)}, /*index=5*/f32[4,32,256]{2,1,0:T(8,128)}) fusion(f32[4,32,256]{2,1,0:T(8,128)S(1)} %copy-done.4, f32[4]{0:T(128)S(1)} %get-tuple-element.112, ...), kind=kLoop, calls=%fused_computation.8 | loop fusion | flops 983040 | bytes 1835040 | tf_op jit(solution)/shard_map/sub | solution.py:965
  189.9 1.0 multiply_subtract_fusion
  190.9 0.6 fusion.20
  192.2 0.6 multiply_subtract_fusion.4
  193.6 0.6 copy-done.11
  194.2 0.6 multiply_subtract_fusion.3
  194.9 0.6 multiply_subtract_fusion.5
  (72 shorter events, 0.7 us)
Async XLA Ops:
  1.4 0.7 copy-start.12
  2.1 0.7 copy-start.13
  2.9 0.7 copy-start.19
  2.9 0.7 copy-start.20
  2.9 0.7 copy-start.21
  3.6 0.7 copy-start.14
  3.6 2.8 %copy-start.17 = (f32[256,48]{0,1:T(8,128)S(1)}, f32[256,48]{0,1:T(8,128)}, u32[]{:S(2)}) copy-start(f32[256,48]{0,1:T(8,128)} %param.27) | copy-start | bytes 147460
  4.3 0.7 copy-start.15
  5.0 0.7 copy-start.16
  6.5 0.7 copy-start.22
  8.5 0.7 copy-start.28
  9.5 2.4 %copy-start.29 = (s32[1,4]{1,0:T(1,128)S(1)}, s32[1,4]{1,0:T(1,128)}, u32[]{:S(2)}) copy-start(s32[1,4]{1,0:T(1,128)} %param.30) | copy-start | bytes 52
  9.5 2.4 %copy-start.25 = (s32[1,256]{1,0:T(1,128)S(1)}, s32[1,256]{1,0:T(1,128)}, u32[]{:S(2)}) copy-start(s32[1,256]{1,0:T(1,128)} %segr.1) | copy-start | bytes 3076
  10.1 4.1 %copy-start.10 = (bf16[256,192]{0,1:T(8,128)(2,1)S(1)}, bf16[256,192]{0,1:T(8,128)(2,1)}, u32[]{:S(2)}) copy-start(bf16[256,192]{0,1:T(8,128)(2,1)} %param.26) | copy-start | bytes 294916
  12.8 0.8 copy-start.27
  15.0 172.7 %copy-start.3 = (f32[4,32,256]{2,1,0:T(8,128)S(1)}, f32[4,32,256]{2,1,0:T(8,128)}, u32[]{:S(2)}) copy-start(f32[4,32,256]{2,1,0:T(8,128)} %aggw.1) | copy-start | bytes 393220
  15.0 172.7 %copy-start.4 = (f32[4,32,256]{2,1,0:T(8,128)S(1)}, f32[4,32,256]{2,1,0:T(8,128)}, u32[]{:S(2)}) copy-start(f32[4,32,256]{2,1,0:T(8,128)} %attnw.1) | copy-start | bytes 393220
  15.0 172.7 %copy-start.5 = (f32[4,32,256]{2,1,0:T(8,128)S(1)}, f32[4,32,256]{2,1,0:T(8,128)}, u32[]{:S(2)}) copy-start(f32[4,32,256]{2,1,0:T(8,128)} %aggf.1) | copy-start | bytes 393220
  15.0 172.7 %copy-start.6 = (f32[4,32,256]{2,1,0:T(8,128)S(1)}, f32[4,32,256]{2,1,0:T(8,128)}, u32[]{:S(2)}) copy-start(f32[4,32,256]{2,1,0:T(8,128)} %aggs.1) | copy-start | bytes 393220
  15.0 172.7 %copy-start.7 = (f32[4,32,256]{2,1,0:T(8,128)S(1)}, f32[4,32,256]{2,1,0:T(8,128)}, u32[]{:S(2)}) copy-start(f32[4,32,256]{2,1,0:T(8,128)} %attnf.1) | copy-start | bytes 393220
  15.0 172.7 %copy-start.8 = (f32[4,32,256]{2,1,0:T(8,128)S(1)}, f32[4,32,256]{2,1,0:T(8,128)}, u32[]{:S(2)}) copy-start(f32[4,32,256]{2,1,0:T(8,128)} %attns.1) | copy-start | bytes 393220
  183.0 1.4 copy-start.26
  185.9 0.7 copy-start.30
  187.6 7.2 %copy-start.23 = (f32[29]{0:T(128)}, f32[29]{0:T(128)S(1)}, u32[]{:S(2)}) copy-start(f32[29]{0:T(128)S(1)} %get-tuple-element.99) | copy-start | bytes 352
  187.7 2.2 %copy-start = (f32[2,32,1024]{2,1,0:T(8,128)S(1)}, f32[2,32,1024]{2,1,0:T(8,128)}, u32[]{:S(2)}) copy-start(f32[2,32,1024]{2,1,0:T(8,128)} %mlpw.1) | copy-start | bytes 786436
  187.7 2.2 %copy-start.1 = (f32[2,32,1024]{2,1,0:T(8,128)S(1)}, f32[2,32,1024]{2,1,0:T(8,128)}, u32[]{:S(2)}) copy-start(f32[2,32,1024]{2,1,0:T(8,128)} %mlpf.1) | copy-start | bytes 786436
  187.8 2.1 %copy-start.2 = (f32[2,32,1024]{2,1,0:T(8,128)S(1)}, f32[2,32,1024]{2,1,0:T(8,128)}, u32[]{:S(2)}) copy-start(f32[2,32,1024]{2,1,0:T(8,128)} %mlps.1) | copy-start | bytes 786436
  187.8 2.1 %copy-start.9 = (f32[2,32,1024]{2,1,0:T(8,128)S(1)}, f32[2,32,1024]{2,1,0:T(8,128)}, u32[]{:S(2)}) copy-start(f32[2,32,1024]{2,1,0:T(8,128)} %get-tuple-element.32) | copy-start | bytes 786436
  189.9 2.3 %copy-start.18 = (f32[32,128]{1,0:T(8,128)S(1)}, f32[32,128]{1,0:T(8,128)}, u32[]{:S(2)}) copy-start(f32[32,128]{1,0:T(8,128)} %get-tuple-element.33) | copy-start | bytes 49156
  192.2 1.3 copy-start.24
  193.5 0.7 copy-start.11

commit v2 on v0

v2 whole, which is shorter than its diff:
```python
import math

import jax
import jax.numpy as jnp
from jax import lax
from jax.experimental import pallas as pl
from jax.experimental.pallas import tpu as pltpu
from jax.sharding import PartitionSpec as P

D = 1024
HEAD_DIM = 64
FF = 4096
NVAR = 48
P_SIZE = 4
SEGS = 4
LEADS = 28
LATS = 32
STEP = 10
NVEC = 17
EROWS = NVAR * (P_SIZE + 1)

HIGH = lax.Precision.HIGHEST
NORM_EPS = 1e-06
BETA_ONE = 0.9
BETA_TWO = 0.999
LEARN_RATE = 0.3
WEIGHT_DECAY = 0.01
ADAM_EPS = 1e-08
STATS_DECAY = 0.9
MESH = pl.DeviceIdType.MESH
BF = jnp.bfloat16
F32 = jnp.float32

DPN, MPN, CHIPS, SH, TOK, COLS = 32, 4, 16, 64, 256, 256
NQ = 4
RQ, CH = TOK // NQ, SH // NQ
SCALE = 1.0 / math.sqrt(HEAD_DIM)


def nn(a, b, precision=None):
    return lax.dot_general(
        a, b, (((1,), (0,)), ((), ())), preferred_element_type=F32, precision=precision
    )


def nt(a, b, precision=None):
    return lax.dot_general(
        a, b, (((1,), (1,)), ((), ())), preferred_element_type=F32, precision=precision
    )


def tn(a, b, precision=None):
    return lax.dot_general(
        a, b, (((0,), (0,)), ((), ())), preferred_element_type=F32, precision=precision
    )


def latitude_weights():
    cosines = [
        math.cos(((j + 0.5) * (180.0 / LATS) - 90.0) * (math.pi / 180.0)) for j in range(LATS)
    ]
    mean = sum(cosines) / LATS
    return [value / mean for value in cosines]


def moments_new(gradient, first, second):
    first_new = BETA_ONE * first + (1.0 - BETA_ONE) * gradient
    second_new = BETA_TWO * second + (1.0 - BETA_TWO) * gradient * gradient
    return first_new, second_new


def adam_direction(weight, gradient, first, second):
    first_new, second_new = moments_new(gradient, first, second)
    first_hat = first_new * (1.0 / (1.0 - BETA_ONE**STEP))
    second_hat = second_new * (1.0 / (1.0 - BETA_TWO**STEP))
    direction = first_hat / (jnp.sqrt(second_hat) + ADAM_EPS) + WEIGHT_DECAY * weight
    return (first_new, second_new, direction)


def iota(shape, dim):
    return lax.broadcasted_iota(jnp.int32, shape, dim)


def ln_parts(x):
    centre = jnp.mean(x, -1, keepdims=True)
    shifted = x - centre
    r = lax.rsqrt(jnp.mean(shifted * shifted, -1, keepdims=True) + NORM_EPS)
    return shifted * r, r


def ln_back(n, r, gain, dh):
    e = dh * gain
    dx = r * (e - jnp.mean(e, -1, keepdims=True) - n * jnp.mean(e * n, -1, keepdims=True))
    dgain = jnp.sum(dh * n, 0, keepdims=True)
    dbias = jnp.sum(dh, 0, keepdims=True)
    return dx, dgain, dbias


LARGE = ("pix", "targ", "aggw", "attnw", "mlpw", "headw", "emb", "vec")
MOMENTS = ("agg", "attn", "mlp", "head", "emb", "vec")
SMALL = ("mask", "seg", "leadi", "lat", "vid")
OUTS = ("o_emb", "o_vec", "o_agg", "o_attn", "o_mlp", "o_head", "o_stats")
SHAPES = {
    "pix": ((NVAR * P_SIZE, TOK), BF),
    "targ": ((NVAR, TOK), F32),
    "agg": ((4, 32, 256), F32),
    "attn": ((4, 32, 256), F32),
    "mlp": ((2, 32, 1024), F32),
    "head": ((32, NVAR), F32),
    "emb": ((40, NVAR), F32),
    "vec": ((8, NVEC), F32),
}
SHAPES.update({"aggw": SHAPES["agg"], "attnw": SHAPES["attn"], "mlpw": SHAPES["mlp"]})
SHAPES["headw"] = SHAPES["head"]
FETCH = LARGE + tuple(n + "_f" for n in MOMENTS) + tuple(n + "_s" for n in MOMENTS)


def fetch_shape(name):
    return SHAPES[name[:-2] if name[-2] == "_" else name]


def scratch_list():
    vm = pltpu.VMEM
    dma = pltpu.SemaphoreType.DMA
    items = [
        ("WA3", vm((D, 256), BF)),
        ("WB", vm((D, 1024), BF)),
        ("W1", vm((D, 1024), BF)),
        ("W2", vm((D, 1024), BF)),
        ("HW", vm((D, 512), BF)),
        ("VEC", vm((D, 128), F32)),
        ("VR", vm((128, D), F32)),
        ("VRN", vm((128, D), F32)),
        ("TMPV", vm((D, 128), F32)),
        ("TA", vm((32, 384), F32)),
        ("HWT", vm((32, 128), F32)),
        ("TT", vm((128, TOK), F32)),
        ("TS", vm((NQ, MPN, CH, 128), F32)),
        ("TGT", vm((MPN, NQ, CH, 128), F32)),
        ("ROWS", vm((128, TOK), F32)),
        ("TCOL", vm((TOK, 128), F32)),
        ("LW", vm((TOK, 128), F32)),
        ("PIXT", vm((256, TOK), F32)),
        ("EWP", vm((256, 512), F32)),
        ("EWH", vm((128, 512), F32)),
        ("EWC", vm((128, 512), F32)),
        ("EWR", vm((256, 512), F32)),
        ("PRP", vm((256, 384), F32)),
        ("PRH", vm((128, 384), F32)),
        ("PRC", vm((128, 384), F32)),
        ("PRR", vm((256, 384), F32)),
        ("MT", vm((4, 256, TOK), BF)),
        ("PT", vm((4, NVAR, TOK), F32)),
        ("OAT", vm((256, TOK), F32)),
        ("OA", vm((TOK, 256), BF)),
        ("RSS", vm((5, TOK, D), BF)),
        ("RSR", vm((5, 3, SH, D), BF)),
        ("AG", vm((5, TOK, D), BF)),
        ("QKV", vm((3, TOK, 256), BF)),
        ("PB", vm((4, TOK, TOK), F32)),
        ("OB", vm((TOK, 256), BF)),
        ("DOB", vm((TOK, 256), BF)),
        ("GEL", vm((TOK, 1024), BF)),
        ("GELP", vm((TOK, 1024), F32)),
        ("DU", vm((TOK, 1024), BF)),
        ("DQKV", vm((TOK, 768), BF)),
        ("LN", vm((2, SH, D), F32)),
        ("XS", vm((SH, D), F32)),
        ("RR", vm((2, SH, 128), F32)),
        ("H3", vm((SH, D), BF)),
        ("DP", vm((SH, 512), BF)),
        ("GVT", vm((D, 128), F32)),
        ("GVP", vm((128, D), F32)),
        ("GVN", vm((128, D), F32)),
        ("TG", vm((32, 256), F32)),
        ("TGR", vm((3, 8, 256), F32)),
        ("VG", vm((32, 128), F32)),
        ("VGR", vm((3, 8, 128), F32)),
        ("HG", vm((32, 512), F32)),
        ("HGR", vm((3, 32, 128), F32)),
        ("EG", vm((40, NVAR), F32)),
        ("NX", vm((8, 128), F32)),
        ("NXR", vm((3, 8, 128), F32)),
        ("NY", vm((8, 128), F32)),
        ("NYR", vm((256, 128), F32)),
    ]
    for name, width, kind in (
        ("A3", 256, BF),
        ("B", 1024, BF),
        ("1", 1024, BF),
        ("2", 1024, BF),
        ("H", 512, BF),
        ("V", 128, F32),
    ):
        if name != "V":
            items.append(("G" + name, vm((D, width), kind)))
        items.append(("S" + name, vm((512, width), kind)))
        items.append(("B" + name, vm((512, width), kind)))
    for name in FETCH:
        items.append(("in_" + name, vm(*fetch_shape(name))))
    items += [
        ("fsem", dma((len(FETCH),))),
        ("ysend", dma((20,))),
        ("yrecv", dma((8,))),
        ("rrecv", dma((5, NQ))),
        ("arecv", dma((5, NQ))),
        ("dsend", dma((19,))),
        ("drecv", dma((19,))),
        ("ssend", dma((16,))),
        ("srecv", dma((16,))),
    ]
    return items


SCRATCH = scratch_list()
NAMES = tuple(n + "_hbm" for n in FETCH) + SMALL + OUTS + tuple(n for n, unused in SCRATCH)


def mega(*refs):
    r = dict(zip(NAMES, refs))
    step_kernel(type("Refs", (), r))


def step_kernel(R):
    d = lax.axis_index("dp")
    m = lax.axis_index("mp")
    c = lax.rem(d, 2)
    k = d // 2
    z = k // 4
    x = lax.rem(k, 4)
    sib = d + 1 - 2 * c
    rb = pl.multiple_of(c * 512 + k * 32, 32)
    half = pl.multiple_of(c * 512, 512)
    other = pl.multiple_of(512 - c * 512, 512)
    my_slot = pl.ds(pl.multiple_of(m * 128, 128), 128)
    my_eight = pl.ds(pl.multiple_of(m * 8, 8), 8)
    my_cols = pl.ds(pl.multiple_of(m * COLS, COLS), COLS)

    def rcopy(src, dst, ss, rs, dp, mp):
        return pltpu.make_async_remote_copy(
            src_ref=src,
            dst_ref=dst,
            send_sem=ss,
            recv_sem=rs,
            device_id={"dp": dp, "mp": mp},
            device_id_type=MESH,
        )

    def drain(ref, sem):
        pltpu.make_async_copy(ref, ref, sem).wait()

    def loop(first, last, fn):
        def step(i, carry):
            fn(i)
            return carry

        lax.fori_loop(first, last, step, 0)

    def to_peers(fn):
        for i in (2, 1, 3):
            fn(i, lax.rem(m + i, MPN))

    def to_chips(fn):
        def step(i):
            kk = lax.rem(k + i, CHIPS)
            fn(kk, kk * 2 + c)

        loop(1, CHIPS, step)

    def fetch(name):
        i = FETCH.index(name)
        return pltpu.make_async_copy(
            getattr(R, name + "_hbm"), getattr(R, "in_" + name), R.fsem.at[i]
        )

    dsend, drecv, ssend, srecv = R.dsend, R.drecv, R.ssend, R.srecv
    ysend, yrecv = R.ysend, R.yrecv

    def gather_start(buf, g):
        block = buf.at[pl.ds(rb, 32)]
        to_chips(lambda kk, t: rcopy(block, block, dsend.at[g], drecv.at[g], t, m).start())

    def gather_cross(buf, g, rows=480):
        drain(buf.at[pl.ds(0, rows)], drecv.at[g])
        part = buf.at[pl.ds(half, 512)]
        rcopy(part, part, ssend.at[g], srecv.at[g], sib, m).start()

    def gather_wait(buf, g):
        drain(buf.at[pl.ds(0, 512)], srecv.at[g])

    def gather_end(buf, g, rows=480):
        drain(buf.at[pl.ds(0, rows)], dsend.at[g])
        drain(buf.at[pl.ds(0, 512)], ssend.at[g])

    def along(axis, i):
        if axis == "x":
            return (z * 4 + lax.rem(x + i, 4)) * 2 + c
        return (lax.rem(z + i, 4) * 4 + x) * 2 + c

    def two_first(buf, axis, g):
        block = buf.at[pl.ds(rb, 32)]
        for i in (2, 1, 3):
            rcopy(block, block, dsend.at[g], drecv.at[g], along(axis, i), m).start()

    def two_second(buf, axis, g, before):
        drain(buf.at[pl.ds(0, 96)], drecv.at[before])
        if axis == "z":
            block = buf.at[pl.ds(pl.multiple_of(half + z * 128, 128), 128)]
            for i in (2, 1, 3):
                rcopy(block, block, dsend.at[g], drecv.at[g], along("z", i), m).start()
        else:

            def send(zz):
                block = buf.at[pl.ds(pl.multiple_of(half + zz * 128 + x * 32, 32), 32)]
                for i in (2, 1, 3):
                    rcopy(block, block, dsend.at[g], drecv.at[g], along("x", i), m).start()

            loop(0, 4, send)

    def reduce_cross(name, g):
        buf, sbuf = (R.GVT if name == "V" else getattr(R, "G" + name)), getattr(R, "S" + name)
        rcopy(buf.at[pl.ds(other, 512)], sbuf, ssend.at[g], srecv.at[g], sib, m).start()

    def reduce_spread(name, g):
        buf, sbuf = (R.GVT if name == "V" else getattr(R, "G" + name)), getattr(R, "S" + name)
        bbuf = getattr(R, "B" + name)
        drain(sbuf, srecv.at[g])

        def add(i):
            at = pl.multiple_of(i * 128, 128)
            sbuf[pl.ds(at, 128), :] = (
                sbuf[pl.ds(at, 128), :].astype(F32)
                + buf[pl.ds(pl.multiple_of(half + at, 128), 128), :].astype(F32)
            ).astype(sbuf.dtype)

        loop(0, 4, add)
        land = bbuf.at[pl.ds(pl.multiple_of(k * 32, 32), 32)]

        def send(kk, t):
            src = sbuf.at[pl.ds(pl.multiple_of(kk * 32, 32), 32)]
            rcopy(src, land, dsend.at[g], drecv.at[g], t, m).start()

        to_chips(send)

    def reduce_end(name, g):
        sbuf, bbuf = getattr(R, "S" + name), getattr(R, "B" + name)
        drain(bbuf.at[pl.ds(0, 480)], drecv.at[g])

        def add(i, acc):
            at = pl.multiple_of(lax.rem(k + i, CHIPS) * 32, 32)
            return acc + bbuf[pl.ds(at, 32), :].astype(F32)

        total = lax.fori_loop(
            1, CHIPS, add, sbuf[pl.ds(pl.multiple_of(k * 32, 32), 32), :].astype(F32)
        )
        drain(bbuf.at[pl.ds(0, 480)], dsend.at[g])
        drain(sbuf, ssend.at[g])
        return total

    def all_sum(src, hbuf, cbuf, res, g, hooks):
        mine_half = pl.multiple_of(c * 128, 128)
        rcopy(
            src.at[pl.ds(pl.multiple_of(128 - c * 128, 128), 128)],
            hbuf,
            ssend.at[g],
            srecv.at[g],
            sib,
            m,
        ).start()
        hooks[0]()
        drain(hbuf, srecv.at[g])
        hbuf[...] = hbuf[...] + src[pl.ds(mine_half, 128), :]
        at_k = pl.multiple_of(k * 8, 8)

        def send(kk, t):
            rcopy(
                hbuf.at[pl.ds(pl.multiple_of(kk * 8, 8), 8)],
                cbuf.at[pl.ds(at_k, 8)],
                dsend.at[g],
                drecv.at[g],
                t,
                m,
            ).start()

        to_chips(send)
        hooks[1]()
        drain(cbuf.at[pl.ds(0, 120)], drecv.at[g])

        def add(i, acc):
            at = pl.multiple_of(lax.rem(k + i, CHIPS) * 8, 8)
            return acc + cbuf[pl.ds(at, 8), :]

        total = lax.fori_loop(1, CHIPS, add, hbuf[pl.ds(at_k, 8), :])
        block = pl.ds(pl.multiple_of(mine_half + at_k, 8), 8)
        res[block, :] = total
        part = res.at[block]
        to_chips(lambda kk, t: rcopy(part, part, dsend.at[g + 1], drecv.at[g + 1], t, m).start())
        hooks[2]()
        drain(res.at[pl.ds(0, 120)], drecv.at[g + 1])
        part2 = res.at[pl.ds(mine_half, 128)]
        rcopy(part2, part2, ssend.at[g + 1], srecv.at[g + 1], sib, m).start()
        hooks[3]()
        drain(res.at[pl.ds(0, 128)], srecv.at[g + 1])

    def all_sum_end(hbuf, cbuf, res, g):
        drain(hbuf, ssend.at[g])
        drain(res.at[pl.ds(0, 128)], ssend.at[g + 1])
        drain(cbuf.at[pl.ds(0, 120)], dsend.at[g])
        drain(res.at[pl.ds(0, 120)], dsend.at[g + 1])

    def rows_of(q):
        return pl.ds(pl.multiple_of(q * RQ, RQ), RQ)

    def own_of(q, t):
        return pl.ds(pl.multiple_of(q * RQ + t * CH, CH), CH)

    def local_of(q):
        return pl.ds(pl.multiple_of(q * CH, CH), CH)

    def branch_send(ix, q, left, weight, cols=None):
        for n in range(4):
            at = pl.ds(n * 256, 256)
            w = weight[at, :] if cols is None else weight[at, cols[0] : cols[1]]
            R.RSS[ix, rows_of(q), n * 256 : (n + 1) * 256] = nt(left, w).astype(BF)

        def send(i, t):
            rcopy(
                R.RSS.at[ix, own_of(q, t)],
                R.RSR.at[ix, i - 1, local_of(q)],
                ysend.at[ix],
                R.rrecv.at[ix, q],
                d,
                t,
            ).start()

        to_peers(send)

    def branch_sum(ix, q):
        drain(R.RSR.at[ix, :, pl.ds(0, CH)], R.rrecv.at[ix, q])
        acc = R.RSS[ix, own_of(q, m), :].astype(F32)
        for i in range(3):
            acc = acc + R.RSR[ix, i, local_of(q), :].astype(F32)
        return acc

    def share_send(ix, q, values):
        R.AG[ix, own_of(q, m), :] = values
        block = R.AG.at[ix, own_of(q, m)]
        to_peers(
            lambda i, t: rcopy(block, block, ysend.at[5 + ix], R.arecv.at[ix, q], d, t).start()
        )

    def share_wait(ix, q):
        drain(R.AG.at[ix, pl.ds(0, 3 * CH)], R.arecv.at[ix, q])

    for name in FETCH:
        fetch(name).start()
    bar = pltpu.get_barrier_semaphore()

    def greet(i):
        pl.semaphore_signal(
            bar, inc=1, device_id={"dp": lax.rem(d + i, DPN), "mp": m}, device_id_type=MESH
        )

    for i in range(1, MPN):
        pl.semaphore_signal(
            bar, inc=1, device_id={"dp": d, "mp": lax.rem(m + i, MPN)}, device_id_type=MESH
        )
    loop(1, DPN, greet)

    vhot = (iota((NVAR, NVAR), 0) == R.vid[...]).astype(F32)
    fetch("emb").wait()
    fetch("vec").wait()
    chosen = nn(R.in_emb[...], vhot, HIGH)
    R.TA[my_eight, :] = jnp.zeros((8, 384), F32)
    for p in range(5):
        R.TA[my_eight, p * 48 : (p + 1) * 48] = chosen[p * 8 : (p + 1) * 8, :]
    R.TA[my_eight, 256 : 256 + NVEC] = R.in_vec[...]
    fetch("aggw").wait()
    fetch("headw").wait()
    aw = [R.in_aggw[j].astype(BF) for j in range(3)]
    R.WA3[pl.ds(rb, 32), :] = R.in_aggw[3].astype(BF)
    R.HWT[...] = jnp.zeros_like(R.HWT)
    R.HWT[:, 0:NVAR] = R.in_headw[...]
    R.HW[pl.ds(rb, 32), my_slot] = R.HWT[...].astype(BF)
    fetch("mlpw").wait()
    R.W1[pl.ds(rb, 32), :] = R.in_mlpw[0].astype(BF)
    R.W2[pl.ds(rb, 32), :] = R.in_mlpw[1].astype(BF)
    fetch("attnw").wait()
    for j in range(4):
        R.WB[pl.ds(rb, 32), j * 256 : (j + 1) * 256] = R.in_attnw[j].astype(BF)
    fetch("targ").wait()
    R.TT[NVAR:, :] = jnp.zeros((128 - NVAR, TOK), F32)
    R.TT[0:NVAR, :] = R.in_targ[...]
    turned = R.TT[...].T
    for q in range(NQ):
        for t in range(MPN):
            at = q * RQ + t * CH
            R.TS[q, t] = turned[at : at + CH, :]
    R.TGT[m] = R.TS[:, m]
    R.GVP[...] = jnp.zeros_like(R.GVP)
    R.GVN[...] = jnp.zeros_like(R.GVN)
    R.NX[...] = jnp.zeros_like(R.NX)
    pl.semaphore_wait(bar, DPN + MPN - 2)

    def first_sends(i, t):
        part = R.TA.at[my_eight]
        rcopy(part, part, ysend.at[10], yrecv.at[0], d, t).start()

    def later_sends(i, t):
        slot = R.HW.at[pl.ds(rb, 32), my_slot]
        rcopy(slot, slot, ysend.at[11], yrecv.at[1], d, t).start()
        rcopy(R.TS.at[:, t], R.TGT.at[m], ysend.at[12], yrecv.at[2], d, t).start()

    to_peers(first_sends)
    gather_start(R.WA3, 0)
    two_first(R.W1, "x", 17)
    two_first(R.W2, "z", 18)
    to_peers(later_sends)

    fetch("pix").wait()
    rows = iota((256, 192), 0)
    cols = iota((256, 192), 1)
    pick = (rows < 192) & ((lax.rem(rows, NVAR) * P_SIZE + rows // NVAR) == cols)
    pixt = nn(pick.astype(BF), R.in_pix[...])
    row_at = iota((256, TOK), 0)
    R.PIXT[...] = jnp.where(row_at < 192, pixt, jnp.where(row_at < EROWS, 1.0, 0.0))

    drain(R.TA.at[pl.ds(0, 24)], yrecv.at[0])
    emb = R.TA[:, 0:256]
    R.EWP[:, 0:256] = tn(emb, aw[1].astype(F32), HIGH)
    R.EWP[:, 256:512] = tn(emb, aw[2].astype(F32), HIGH)
    R.EWP[240:241, 0:256] = jnp.sum(R.TA[:, 256:257] * aw[0].astype(F32), 0, keepdims=True)
    keep = R.mask[...].astype(F32)
    count = jnp.sum(jnp.sum(keep, 1, keepdims=True), 0, keepdims=True) * NVAR
    R.EWP[241:242, 0:128] = jnp.broadcast_to(count, (1, 128))

    def per_patch():
        seg = R.seg[...]
        lead_row = jnp.zeros((1, TOK), F32)
        for s in range(SEGS):
            value = (R.leadi[:, s : s + 1] + 1).astype(F32) / LEADS
            lead_row = jnp.where(seg == s, value, lead_row)
        lat = R.lat[...]
        lat_row = jnp.zeros((1, TOK), F32)
        for j, value in enumerate(latitude_weights()):
            lat_row = jnp.where(lat == j, value, lat_row)
        R.ROWS[...] = jnp.zeros_like(R.ROWS)
        R.ROWS[0:1, :] = seg.astype(F32)
        R.ROWS[1:2, :] = lead_row
        R.ROWS[8:12, :] = keep * lat_row
        R.TCOL[...] = R.ROWS[...].T
        lane = iota((128, 128), 1)
        pick = (lane < NVAR) & (iota((128, 128), 0) == 8 + lax.rem(lane, P_SIZE))
        R.LW[...] = nn(R.TCOL[...], pick.astype(F32), HIGH)

    def own_slot_done():
        drain(R.HW.at[pl.ds(0, 32), pl.ds(0, 384)], yrecv.at[1])
        R.VEC[pl.ds(rb, 32), :] = R.TA[:, 256:384]

    def bulk():
        gather_cross(R.WA3, 0)
        gather_start(R.VEC, 2)
        gather_start(R.WB, 1)
        gather_start(R.HW, 5)

    all_sum(R.EWP, R.EWH, R.EWC, R.EWR, 6, (own_slot_done, per_patch, bulk, lambda: None))

    head_of = (iota((256, 128), 0) // HEAD_DIM == iota((256, 128), 1)).astype(F32)
    qa = R.EWR[240:241, 0:256].astype(BF).astype(F32)
    total_count = R.EWR[241:242, 0:1]
    qe = nn(R.EWR[:, 0:256] * (qa * SCALE), head_of, HIGH)
    ewv = R.EWR[:, 256:512].astype(BF)
    for h in range(4):
        scores = R.PIXT[0:48, :] * qe[0:48, h : h + 1]
        for p in range(1, 5):
            at = slice(p * 48, (p + 1) * 48)
            scores = scores + R.PIXT[at, :] * qe[at, h : h + 1]
        e = jnp.exp(scores - jnp.max(scores, 0, keepdims=True))
        probs = e / jnp.sum(e, 0, keepdims=True)
        R.PT[h] = probs
        probs = probs.astype(BF).astype(F32)
        for p in range(5):
            at = slice(p * 48, (p + 1) * 48)
            R.MT[h, at, :] = (probs * R.PIXT[at, :]).astype(BF)
        R.MT[h, 240:256, :] = jnp.zeros((16, TOK), BF)
        R.OAT[h * 64 : (h + 1) * 64, :] = tn(ewv[:, h * 64 : (h + 1) * 64], R.MT[h])
    R.OA[...] = R.OAT[...].T.astype(BF)

    gather_wait(R.WA3, 0)
    loop(0, NQ, lambda q: branch_send(0, q, R.OA[rows_of(q), :], R.WA3))
    two_second(R.W1, "z", 3, 17)
    two_second(R.W2, "x", 4, 18)
    gather_cross(R.VEC, 2)
    gather_wait(R.VEC, 2)
    R.VR[...] = R.VEC[...].T

    def natural(i):
        at = pl.multiple_of(lax.rem(i, 2) * 512 + (i // 2) * 32, 32)
        R.TMPV[pl.ds(pl.multiple_of(i * 32, 32), 32), :] = R.VEC[pl.ds(at, 32), :]

    loop(0, DPN, natural)
    R.VRN[...] = R.TMPV[...].T

    def vrow(i):
        return R.VR[i : i + 1, :]

    def keep_norm(j, q, n, r):
        R.LN[j, local_of(q), :] = n
        R.RR[j, local_of(q), :] = jnp.broadcast_to(r, (CH, 128))

    def mixed_rows(q):
        lead = R.TCOL[own_of(q, m), 1:2]
        x0 = branch_sum(0, q) + vrow(1) + lead * vrow(2)
        n, r = ln_parts(x0)
        share_send(0, q, (n * vrow(3) + vrow(4)).astype(BF))
        R.XS[local_of(q), :] = x0
        keep_norm(0, q, n, r)

    loop(0, NQ, mixed_rows)
    gather_cross(R.WB, 1)
    gather_wait(R.WB, 1)

    def project(q):
        share_wait(0, q)
        at = rows_of(q)
        h1 = R.AG[0, at, :]
        R.QKV[0, at, :] = (nn(h1, R.WB[:, 0:256]) + R.VRN[5:6, my_cols]).astype(BF)
        R.QKV[1, at, :] = nn(h1, R.WB[:, 256:512]).astype(BF)
        R.QKV[2, at, :] = (nn(h1, R.WB[:, 512:768]) + R.VRN[6:7, my_cols]).astype(BF)

    loop(0, NQ, project)
    seg_row = R.seg[...].astype(F32)

    def attend(q):
        rows = rows_of(q)
        same = R.TCOL[rows, 0:1] == seg_row
        for h in range(4):
            at = slice(h * 64, (h + 1) * 64)
            scores = nt(R.QKV[0, rows, at], R.QKV[1, :, at]) * SCALE
            scores = jnp.where(same, scores, -1e30)
            e = jnp.exp(scores - jnp.max(scores, 1, keepdims=True))
            probs = e / jnp.sum(e, 1, keepdims=True)
            R.PB[h, rows, :] = probs
            R.OB[rows, at] = nn(probs.astype(BF), R.QKV[2, :, at]).astype(BF)
        branch_send(1, q, R.OB[rows, :], R.WB, (768, 1024))

    loop(0, NQ, attend)
    gather_cross(R.W1, 3, 384)
    gather_cross(R.W2, 4, 384)

    def second_rows(q):
        x1 = R.XS[local_of(q), :] + branch_sum(1, q) + vrow(7)
        n, r = ln_parts(x1)
        share_send(1, q, (n * vrow(8) + vrow(9)).astype(BF))
        R.XS[local_of(q), :] = x1
        keep_norm(1, q, n, r)

    loop(0, NQ, second_rows)
    gather_cross(R.HW, 5)
    gather_wait(R.W1, 3)
    gather_wait(R.W2, 4)

    def feed(q):
        share_wait(1, q)
        rows = rows_of(q)
        for n in range(4):
            at = slice(n * 256, (n + 1) * 256)
            u = nn(R.AG[1, rows, :], R.W1[:, at]) + R.VRN[pl.ds(10 + m, 1), at]
            phi = 0.5 * (1.0 + lax.erf(u * (1.0 / math.sqrt(2.0))))
            R.GEL[rows, at] = (u * phi).astype(BF)
            R.GELP[rows, at] = phi + u * jnp.exp(-0.5 * u * u) * (1.0 / math.sqrt(2.0 * math.pi))
        branch_send(2, q, R.GEL[rows, :], R.W2)

    loop(0, NQ, feed)
    gather_wait(R.HW, 5)
    drain(R.TGT.at[pl.ds(0, 3)], yrecv.at[2])

    def head_rows(q):
        here = local_of(q)
        x2 = R.XS[here, :] + branch_sum(2, q) + vrow(14)
        n, r = ln_parts(x2)
        h3 = (n * vrow(15) + vrow(16)).astype(BF)
        R.H3[here, :] = h3
        pred = nn(h3, R.HW[...])
        weight = R.LW[own_of(q, m), :]
        for j in range(4):
            misfit = pred[:, j * 128 : (j + 1) * 128] - R.TGT[j, q]
            weighted = weight * misfit
            R.NX[4 + j : 5 + j, :] = R.NX[4 + j : 5 + j, :] + jnp.sum(
                weighted * misfit, 0, keepdims=True
            )
            R.DP[here, j * 128 : (j + 1) * 128] = (2.0 * weighted / total_count).astype(BF)
        dh3 = nt(R.DP[here, :], R.HW[...])
        dx2, dgain, dbias = ln_back(n, r, vrow(15), dh3)
        share_send(2, q, dx2.astype(BF))
        R.XS[here, :] = dx2
        R.GVP[14:15, :] = R.GVP[14:15, :] + jnp.sum(dx2, 0, keepdims=True)
        R.GVP[15:16, :] = R.GVP[15:16, :] + dgain
        R.GVP[16:17, :] = R.GVP[16:17, :] + dbias

    loop(0, NQ, head_rows)

    def feed_back(q):
        share_wait(2, q)
        rows = rows_of(q)
        for n in range(4):
            at = slice(n * 256, (n + 1) * 256)
            du = (nn(R.AG[2, rows, :], R.W2[:, at]) * R.GELP[rows, at]).astype(BF)
            R.DU[rows, at] = du
            row = pl.ds(10 + m, 1)
            R.GVN[row, at] = R.GVN[row, at] + jnp.sum(du.astype(F32), 0, keepdims=True)
        branch_send(3, q, R.DU[rows, :], R.W1)

    loop(0, NQ, feed_back)

    def pieces(q, fn):
        for j in range(4 // NQ):
            fn(pl.ds(pl.multiple_of((q * (4 // NQ) + j) * 256, 256), 256))

    def grad_two(at):
        R.G2[at, :] = tn(R.AG[2, :, at], R.GEL[...]).astype(BF)

    def grad_one(at):
        R.G1[at, :] = tn(R.AG[1, :, at], R.DU[...]).astype(BF)

    def back_rows(q):
        here = local_of(q)
        n = R.LN[1, here, :]
        dx1, dgain, dbias = ln_back(n, R.RR[1, here, 0:1], vrow(8), branch_sum(3, q))
        dx1 = dx1 + R.XS[here, :]
        share_send(3, q, dx1.astype(BF))
        R.XS[here, :] = dx1
        R.GVP[7:8, :] = R.GVP[7:8, :] + jnp.sum(dx1, 0, keepdims=True)
        R.GVP[8:9, :] = R.GVP[8:9, :] + dgain
        R.GVP[9:10, :] = R.GVP[9:10, :] + dbias
        pieces(q, grad_two)

    R.GH[...] = tn(R.H3[...], R.DP[...]).astype(BF)
    reduce_cross("H", 14)
    loop(0, NQ, back_rows)
    reduce_cross("2", 13)

    def out_back(q):
        share_wait(3, q)
        rows = rows_of(q)
        R.DOB[rows, :] = nn(R.AG[3, rows, :], R.WB[:, 768:1024]).astype(BF)
        pieces(q, grad_one)

    loop(0, NQ, out_back)
    reduce_cross("1", 12)
    reduce_spread("H", 14)
    reduce_spread("2", 13)
    for h in range(4):
        at = slice(h * 64, (h + 1) * 64)
        probs = R.PB[h]
        dout = R.DOB[:, at]
        dv = tn(probs.astype(BF), dout).astype(BF)
        dprob = nt(dout, R.QKV[2, :, at])
        ds = (probs * (dprob - jnp.sum(probs * dprob, 1, keepdims=True))).astype(BF)
        dq = (nn(ds, R.QKV[1, :, at]) * SCALE).astype(BF)
        dk = (tn(ds, R.QKV[0, :, at]) * SCALE).astype(BF)
        R.DQKV[:, h * 64 : (h + 1) * 64] = dq
        R.DQKV[:, 256 + h * 64 : 256 + (h + 1) * 64] = dk
        R.DQKV[:, 512 + h * 64 : 512 + (h + 1) * 64] = dv
    loop(0, NQ, lambda q: branch_send(4, q, R.DQKV[rows_of(q), :], R.WB, (0, 768)))
    R.GVN[5:6, my_cols] = jnp.sum(R.DQKV[:, 0:256].astype(F32), 0, keepdims=True)
    R.GVN[6:7, my_cols] = jnp.sum(R.DQKV[:, 512:768].astype(F32), 0, keepdims=True)
    reduce_spread("1", 12)

    def grad_attn(at):
        R.GB[at, 0:768] = tn(R.AG[0, :, at], R.DQKV[...]).astype(BF)
        R.GB[at, 768:1024] = tn(R.AG[3, :, at], R.OB[...]).astype(BF)

    def first_rows(q):
        here = local_of(q)
        n = R.LN[0, here, :]
        dx0, dgain, dbias = ln_back(n, R.RR[0, here, 0:1], vrow(3), branch_sum(4, q))
        dx0 = dx0 + R.XS[here, :]
        share_send(4, q, dx0.astype(BF))
        lead = R.TCOL[own_of(q, m), 1:2]
        R.GVP[1:2, :] = R.GVP[1:2, :] + jnp.sum(dx0, 0, keepdims=True)
        R.GVP[2:3, :] = R.GVP[2:3, :] + jnp.sum(lead * dx0, 0, keepdims=True)
        R.GVP[3:4, :] = R.GVP[3:4, :] + dgain
        R.GVP[4:5, :] = R.GVP[4:5, :] + dbias
        pieces(q, grad_attn)

    loop(0, NQ, first_rows)
    reduce_cross("B", 11)
    R.TMPV[...] = R.GVN[...].T
    R.GVT[...] = R.GVP[...].T

    def permuted(i):
        at = pl.ds(pl.multiple_of(lax.rem(i, 2) * 512 + (i // 2) * 32, 32), 32)
        R.GVT[at, :] = R.GVT[at, :] + R.TMPV[pl.ds(pl.multiple_of(i * 32, 32), 32), :]

    loop(0, DPN, permuted)
    reduce_cross("V", 15)
    reduce_spread("B", 11)
    reduce_spread("V", 15)

    def mix_back(q):
        share_wait(4, q)
        rows = rows_of(q)
        R.DOB[rows, :] = nn(R.AG[4, rows, :], R.WA3[...]).astype(BF)

    loop(0, NQ, mix_back)
    R.PRP[...] = jnp.zeros_like(R.PRP)
    for h in range(4):
        at = slice(h * 64, (h + 1) * 64)
        dout = R.DOB[:, at]
        through = nt(ewv[:, at], dout)
        dprob = R.PIXT[0:48, :] * through[0:48, :]
        for p in range(1, 5):
            row = slice(p * 48, (p + 1) * 48)
            dprob = dprob + R.PIXT[row, :] * through[row, :]
        probs = R.PT[h]
        ds = (probs * (dprob - jnp.sum(probs * dprob, 0, keepdims=True))).astype(BF).astype(F32)
        for p in range(5):
            row = slice(p * 48, (p + 1) * 48)
            R.PRP[row, 256 + h : 257 + h] = jnp.sum(ds * R.PIXT[row, :], 1, keepdims=True)
        R.PRP[:, at] = nn(R.MT[h], dout)

    lanes = iota((1, 128), 1)
    sums = {"w": jnp.zeros((1, 128), F32), "u": jnp.zeros((1, 128), F32)}

    def square_sum(values):
        return jnp.sum(jnp.sum(values * values, 1, keepdims=True), 0, keepdims=True)

    def tensor(index, weight, gradient, first, second):
        unused, unused2, direction = adam_direction(weight, gradient, first, second)
        here = lanes == index
        sums["w"] = sums["w"] + jnp.where(here, square_sum(weight), 0.0)
        sums["u"] = sums["u"] + jnp.where(here, square_sum(direction), 0.0)

    def hook_first():
        def piece(n):
            at = pl.ds(pl.multiple_of(n * 256, 256), 256)
            R.GA3[at, :] = tn(R.AG[4, :, at], R.OA[...]).astype(BF)

        loop(0, 4, piece)
        reduce_cross("A3", 10)

    def hook_second():
        reduce_spread("A3", 10)
        for name in MOMENTS:
            fetch(name + "_f").wait()
            fetch(name + "_s").wait()
        R.o_mlp[1] = reduce_end("2", 13)
        R.o_mlp[0] = reduce_end("1", 12)
        for j in range(2):
            tensor(8 + j, R.in_mlpw[j], R.o_mlp[j], R.in_mlp_f[j], R.in_mlp_s[j])

    def hook_third():
        R.HG[...] = reduce_end("H", 14)
        R.VG[...] = reduce_end("V", 15)

        def sends(i, t):
            rcopy(
                R.HG.at[:, pl.ds(pl.multiple_of(t * 128, 128), 128)],
                R.HGR.at[i - 1],
                ysend.at[14],
                yrecv.at[4],
                d,
                t,
            ).start()
            rcopy(
                R.VG.at[pl.ds(pl.multiple_of(t * 8, 8), 8)],
                R.VGR.at[i - 1],
                ysend.at[15],
                yrecv.at[5],
                d,
                t,
            ).start()

        to_peers(sends)
        gsum = reduce_end("B", 11)
        for j in range(4):
            R.o_attn[j] = gsum[:, j * 256 : (j + 1) * 256]
        for j in range(4):
            tensor(4 + j, R.in_attnw[j], R.o_attn[j], R.in_attn_f[j], R.in_attn_s[j])

    all_sum(R.PRP, R.PRH, R.PRC, R.PRR, 8, (hook_first, hook_second, hook_third, lambda: None))

    spread = nt(R.PRR[:, 256:384], head_of, HIGH)
    dqa = jnp.sum(spread * R.EWR[:, 0:256], 0, keepdims=True) * SCALE
    pk = spread * (qa * SCALE)
    pv = R.PRR[:, 0:256]
    emb = R.TA[:, 0:256]
    wa = [R.in_aggw[j].astype(BF).astype(F32) for j in range(3)]
    R.TG[...] = nt(wa[1], pk, HIGH) + nt(wa[2], pv, HIGH)
    R.TG[:, 240:241] = jnp.sum(wa[0] * dqa, 1, keepdims=True)

    def last_sends(i, t):
        rcopy(
            R.TG.at[pl.ds(pl.multiple_of(t * 8, 8), 8)],
            R.TGR.at[i - 1],
            ysend.at[13],
            yrecv.at[3],
            d,
            t,
        ).start()

    to_peers(last_sends)
    R.o_agg[0] = R.TA[:, 256:257] * dqa
    R.o_agg[1] = nn(emb, pk, HIGH)
    R.o_agg[2] = nn(emb, pv, HIGH)
    R.o_agg[3] = reduce_end("A3", 10)
    for j in range(4):
        tensor(j, R.in_aggw[j], R.o_agg[j], R.in_agg_f[j], R.in_agg_s[j])
    drain(R.HGR, yrecv.at[4])
    hgrad = R.HG[:, my_slot] + R.HGR[0] + R.HGR[1] + R.HGR[2]
    R.o_head[...] = hgrad[:, 0:NVAR]
    tensor(10, R.in_headw[...], R.o_head[...], R.in_head_f[...], R.in_head_s[...])
    drain(R.VGR, yrecv.at[5])
    vgrad = R.VG[my_eight, :] + R.VGR[0] + R.VGR[1] + R.VGR[2]
    drain(R.TGR, yrecv.at[3])
    tgrad = R.TG[my_eight, :] + R.TGR[0] + R.TGR[1] + R.TGR[2]
    for p in range(5):
        R.EG[p * 8 : (p + 1) * 8, :] = tgrad[:, p * 48 : (p + 1) * 48]
    R.o_emb[...] = nt(R.EG[...], vhot, HIGH)
    tensor(11, R.in_emb[...], R.o_emb[...], R.in_emb_f[...], R.in_emb_s[...])
    R.o_vec[...] = vgrad[:, 0:NVEC]
    R.o_vec[:, 0:1] = tgrad[:, 240:241]
    unused, unused2, direction = adam_direction(
        R.in_vec[...], R.o_vec[...], R.in_vec_f[...], R.in_vec_s[...]
    )
    R.NX[0:1, :] = sums["w"]
    R.NX[1:2, :] = sums["u"]
    R.NX[0:1, 12 : 12 + NVEC] = jnp.sum(R.in_vec[...] * R.in_vec[...], 0, keepdims=True)
    R.NX[1:2, 12 : 12 + NVEC] = jnp.sum(direction * direction, 0, keepdims=True)

    to_peers(lambda i, t: rcopy(R.NX, R.NXR.at[i - 1], ysend.at[16], yrecv.at[6], d, t).start())
    drain(R.NXR, yrecv.at[6])
    R.NY[...] = R.NX[...] + R.NXR[0] + R.NXR[1] + R.NXR[2]
    at_d = pl.ds(pl.multiple_of(d * 8, 8), 8)

    def norm_send(i):
        t = lax.rem(d + i, DPN)
        rcopy(R.NY, R.NYR.at[at_d], dsend.at[16], drecv.at[16], t, m).start()

    loop(1, DPN, norm_send)

    gather_end(R.WA3, 0)
    gather_end(R.WB, 1)
    gather_end(R.VEC, 2)
    gather_end(R.HW, 5)
    for buf, g in ((R.W1, 3), (R.W2, 4)):
        gather_end(buf, g, 384)
        drain(buf.at[pl.ds(0, 96)], dsend.at[14 + g])
    all_sum_end(R.EWH, R.EWC, R.EWR, 6)
    all_sum_end(R.PRH, R.PRC, R.PRR, 8)
    for ix in range(5):
        drain(R.RSR.at[ix], ysend.at[ix])
        drain(R.AG.at[ix, pl.ds(0, 192)], ysend.at[5 + ix])
    drain(R.TA.at[pl.ds(0, 24)], ysend.at[10])
    drain(R.HW.at[pl.ds(0, 32), pl.ds(0, 384)], ysend.at[11])
    drain(R.TGT.at[pl.ds(0, 3)], ysend.at[12])
    drain(R.TGR, ysend.at[13])
    drain(R.HGR, ysend.at[14])
    drain(R.VGR, ysend.at[15])
    drain(R.NXR, ysend.at[16])

    drain(R.NYR.at[pl.ds(0, 248)], drecv.at[16])

    def norm_add(i, acc):
        at = pl.multiple_of(lax.rem(d + i, DPN) * 8, 8)
        return acc + R.NYR[pl.ds(at, 8), :]

    stats = lax.fori_loop(1, DPN, norm_add, R.NY[...])
    first_lane = (iota((8, 128), 0) == 0) & (iota((8, 128), 1) == 127)
    R.o_stats[...] = jnp.where(first_lane, total_count, stats)
    drain(R.NYR.at[pl.ds(0, 248)], dsend.at[16])


def mega_call(large, small):
    outs = [SHAPES[n] for n in ("emb", "vec", "agg", "attn", "mlp", "head")] + [((8, 128), F32)]
    out_shape = tuple(jax.ShapeDtypeStruct(*item) for item in outs)
    whole = pl.BlockSpec(memory_space=pltpu.VMEM)
    return pl.pallas_call(
        mega,
        out_shape=out_shape,
        in_specs=[pl.BlockSpec(memory_space=pl.ANY)] * len(large) + [whole] * len(small),
        out_specs=tuple(whole for unused in out_shape),
        scratch_shapes=[item for unused, item in SCRATCH],
        compiler_params=pltpu.CompilerParams(
            collective_id=0, has_side_effects=True, vmem_limit_bytes=60 * 2**20
        ),
        name="step",
    )(*large, *small)


def finish(*refs):
    weights, firsts, seconds, grads = (refs[6 * i : 6 * i + 6] for i in range(4))
    stats, running = refs[24:26]
    o_loss, o_count, o_running, o_trust, o_norms = refs[26:31]
    o_first, o_second, o_new = (refs[31 + 6 * i : 37 + 6 * i] for i in range(3))
    norms = jnp.sqrt(stats[0:1, :])
    trust = norms / jnp.sqrt(stats[1:2, :])
    o_norms[...] = norms[:, 0:29]
    o_trust[...] = trust[:, 0:29]
    count = stats[0:1, 127:128]
    o_count[...] = count
    errors = jnp.zeros((1, NVAR), F32)
    for j in range(4):
        lane = iota((128, NVAR), 0)
        pick = (lane < NVAR) & (iota((128, NVAR), 1) == 12 * j + lane // P_SIZE)
        errors = errors + nn(stats[4 + j : 5 + j, :], pick.astype(F32), HIGH)
    o_loss[...] = jnp.sum(errors, 1, keepdims=True)
    o_running[...] = STATS_DECAY * running[...] + (1.0 - STATS_DECAY) * errors * (NVAR / count)

    def update(i, at, ratio):
        first, second, direction = adam_direction(
            weights[i][at], grads[i][at], firsts[i][at], seconds[i][at]
        )
        o_first[i][at] = first
        o_second[i][at] = second
        o_new[i][at] = weights[i][at] - LEARN_RATE * ratio * direction

    for i, number, offset in ((0, 4, 0), (1, 4, 4), (2, 2, 8)):
        for j in range(number):
            update(i, j, trust[:, offset + j : offset + j + 1])
    update(3, Ellipsis, trust[:, 10:11])
    update(4, Ellipsis, trust[:, 11:12])
    update(5, Ellipsis, trust[:, 12 : 12 + NVEC])


def finish_call(weights, firsts, seconds, grads, stats, running):
    shapes = [(1, 1), (1, 1), (1, NVAR), (1, 29), (1, 29)] + 3 * [w.shape for w in weights]
    whole = pl.BlockSpec(memory_space=pltpu.VMEM)
    return pl.pallas_call(
        finish,
        out_shape=tuple(jax.ShapeDtypeStruct(s, F32) for s in shapes),
        in_specs=[whole] * 26,
        out_specs=tuple(whole for unused in shapes),
        compiler_params=pltpu.CompilerParams(vmem_limit_bytes=32 * 2**20),
        name="finish",
    )(*weights, *firsts, *seconds, *grads, stats, running)


def on_device(
    pixels,
    targets,
    valid_mask,
    segments,
    lead_index,
    latitude,
    var_ids,
    running_error,
    *tensors,
):
    def turned(group):
        agg, attn, mlp, head, embed, vecs = group
        return (agg, attn, mlp, head, embed.transpose(1, 2, 0).reshape(40, NVAR), vecs.T)

    weights, firsts, seconds = (turned(tensors[6 * i : 6 * i + 6]) for i in range(3))
    large = (pixels.T, targets.T, *weights, *firsts, *seconds)
    small = (
        valid_mask.T,
        segments,
        lead_index,
        latitude.reshape(1, TOK),
        var_ids.reshape(1, NVAR),
    )
    g_emb, g_vec, g_agg, g_attn, g_mlp, g_head, stats = mega_call(large, small)
    grads = (g_agg, g_attn, g_mlp, g_head, g_emb, g_vec)
    out = finish_call(weights, firsts, seconds, grads, stats, running_error.reshape(1, NVAR))

    def back(group):
        agg, attn, mlp, head, embed, vecs = group
        return (agg, attn, mlp, head, embed.reshape(5, 8, NVAR).transpose(2, 0, 1), vecs.T)

    return (
        out[0].reshape(()),
        out[1].reshape(()),
        out[2].reshape(NVAR),
        out[3].reshape(29),
        out[4].reshape(29),
        *back(out[5:11]),
        *back(out[11:17]),
        *back(out[17:23]),
    )


def solution(mesh):
    weights = (
        P(None, "dp", "mp"),
        P(None, "dp", "mp"),
        P(None, "dp", "mp"),
        P("dp", "mp"),
        P(None, None, ("dp", "mp")),
        P(None, ("dp", "mp")),
    )
    in_specs = (
        P("dp", None),
        P("dp", "mp"),
        P("dp", None),
        P("dp", None),
        P("dp", None),
        P("dp"),
        P(),
        P(),
        *weights,
        *weights,
        *weights,
    )
    out_specs = (P(), P(), P(), P(), P(), *weights, *weights, *weights)
    return jax.shard_map(
        on_device, mesh=mesh, in_specs=in_specs, out_specs=out_specs, check_vma=False
    )
```

time: 1880 us -> 171 us (0.09)
  waiting for transfers between devices: 1060 us -> 0 us
  blocking collectives: 342 us -> 0 us
  local copies, waits for them, and re-layouts: 229 us -> 6.15 us
  Pallas kernels: 0 us -> 163 us
  matrix products: 123 us -> 0 us
  other arithmetic: 97.3 us -> 0 us
    reduce_scatter x11 -> x0, waiting for transfers between devices: 976 us -> none  [the longest x1 633 us: on_device(): lax.psum_scatter(grad_embed, ('dp', 'mp'), scatter_dimension=2, tiled=True)]
    all_gather x9 -> x0, blocking collectives: 211 us -> none  [the longest x1 68.3 us: on_device(): lax.all_gather(embed_weight, ('dp', 'mp'), axis=2, tiled=True)]
    pallas_call x0 -> x2, Pallas kernels: none -> 163 us  [the longest x1 162 us: mega_call(): pl.pallas_call(mega, out_shape=out_shape, in_specs=[pl.BlockSpec(memory_s...]
    psum x2 -> x0, blocking collectives: 131 us -> none  [on_device(): lax.psum((error_vec, jnp.sum(keep) * mine_vars), ('dp', 'mp'))]
    dot_general x39 -> x0, matrix products: 123 us -> none  [the longest x1 24.9 us: on_device(): jnp.dot(flat_v, kv_weight, preferred_element_type=wide_type)]
    reshape x7 -> x0, local copies, waits for them, and re-layouts: 77.4 us -> none  [the longest x1 39 us: on_device(): dkv_a = jnp.stack([dkeys_a, dvals_a], 2).reshape(length * NVAR, 2 * cols)]
    unnamed x4 -> x0, other arithmetic: 44.7 us -> none
    unnamed x16 -> x0, waiting for transfers between devices: 43.9 us -> none
  transfers between devices with their start and end apart: 15 -> 0, of which waited for: 11 -> 0; matrix products, arithmetic and copies ran while one was open for 21% -> 0% of each run, Pallas kernels for 0% -> 0%
where the time goes in v2:
time: 171 us; the launch traced here: 170 us
  Pallas kernels  163 us (95%)
  local copies, waits for them, and re-layouts  6.15 us (4%)
    pallas_call x1, Pallas kernels, mega_call(): pl.pallas_call(mega, out_shape=out_shape, in_specs=[pl.BlockSpec(memory_s...  162 us
    unnamed x52, local copies, waits for them, and re-layouts  6.15 us

profile of v2, /device:TPU:1, one launch (start us, length us, event | category | flops | bytes accessed | tf_op | source)
XLA Modules:
  0.0 170.2 jit_solution(5911509797443009113)
XLA Ops:
  0.7 0.0 copy-start
  0.7 0.0 copy-start.1
  0.7 0.0 copy-start.2
  0.7 0.0 copy-start.3
  0.7 0.0 copy-start.4
  0.7 0.0 copy-start.5
  0.7 0.0 copy-start.6
  0.7 0.0 copy-start.7
  0.7 0.0 copy-start.8
  0.8 0.0 copy-start.12
  0.8 0.0 copy-start.13
  0.8 0.0 copy-start.14
  0.8 0.0 copy-start.15
  0.8 0.0 copy-start.16
  0.8 0.0 copy-start.17
  0.8 161.6 %step.1 = (f32[40,48]{1,0:T(8,128)}, f32[8,17]{1,0:T(8,128)}, f32[4,32,256]{2,1,0:T(8,128)}, f32[4,32,256]{2,1,0:T(8,128)}, f32[2,32,1024]{2,1,0:T(8,128)}, /*index=5*/f32[32,48]{1,0:T(8,128)}, f32[8,128]{1,0:T(8,128)}) custom-call(bf16[192,256]{1,0:T(8,128)(2,1)} %bitcast.48, f32[48,256]{1,0:T(8,128)} %bitcast.49, f32[4,32,256]{2,1,0:T(8,128)} %refs_0_.1, ...), custom_call_target="tpu_custom_call" | custom-call | tf_op jit(solution)/shard_map/step/pallas_call | solution.py:979
  162.4 0.0 copy-start.22
  162.4 0.0 copy-start.21
  162.4 0.0 copy-start.20
  162.4 0.0 copy-start.25
  162.5 0.0 copy-done
  162.5 0.0 copy-done.1
  162.5 0.0 copy-done.2
  162.5 0.0 copy-done.3
  162.5 0.0 copy-done.4
  162.5 0.0 copy-done.5
  162.5 0.0 copy-done.6
  162.5 0.0 copy-done.7
  162.5 0.0 copy-done.8
  162.5 0.0 copy-done.12
  162.6 0.0 copy-done.13
  162.6 0.0 copy-done.14
  162.6 0.0 copy-done.15
  162.6 0.0 copy-done.16
  162.6 0.0 copy-done.17
  162.6 0.5 copy-done.22
  163.1 0.0 copy-done.21
  163.1 0.0 copy-done.20
  163.1 0.0 copy-done.25
  163.1 0.0 copy-start.9
  163.1 0.9 copy-done.9
  164.1 0.9 copy-done.10
  165.0 0.9 copy-done.11
  165.9 0.7 copy-done.18
  166.6 0.7 copy-done.19
  167.3 0.7 copy-done.23
  168.0 0.7 copy-done.24
  168.7 1.5 finish.1
  (6 shorter events, 0.0 us)
Async XLA Ops:
  0.7 161.8 %copy-start = (f32[2,32,1024]{2,1,0:T(8,128)S(1)}, f32[2,32,1024]{2,1,0:T(8,128)}, u32[]{:S(2)}) copy-start(f32[2,32,1024]{2,1,0:T(8,128)} %refs_2_.3) | copy-start | bytes 786436
  0.7 161.8 %copy-start.1 = (f32[2,32,1024]{2,1,0:T(8,128)S(1)}, f32[2,32,1024]{2,1,0:T(8,128)}, u32[]{:S(2)}) copy-start(f32[2,32,1024]{2,1,0:T(8,128)} %refs_8_.3) | copy-start | bytes 786436
  0.7 161.8 %copy-start.2 = (f32[2,32,1024]{2,1,0:T(8,128)S(1)}, f32[2,32,1024]{2,1,0:T(8,128)}, u32[]{:S(2)}) copy-start(f32[2,32,1024]{2,1,0:T(8,128)} %refs_14_.3) | copy-start | bytes 786436
  0.7 161.8 %copy-start.3 = (f32[4,32,256]{2,1,0:T(8,128)S(1)}, f32[4,32,256]{2,1,0:T(8,128)}, u32[]{:S(2)}) copy-start(f32[4,32,256]{2,1,0:T(8,128)} %refs_0_.1) | copy-start | bytes 393220
  0.7 161.8 %copy-start.4 = (f32[4,32,256]{2,1,0:T(8,128)S(1)}, f32[4,32,256]{2,1,0:T(8,128)}, u32[]{:S(2)}) copy-start(f32[4,32,256]{2,1,0:T(8,128)} %refs_1_.1) | copy-start | bytes 393220
  0.7 161.8 %copy-start.5 = (f32[4,32,256]{2,1,0:T(8,128)S(1)}, f32[4,32,256]{2,1,0:T(8,128)}, u32[]{:S(2)}) copy-start(f32[4,32,256]{2,1,0:T(8,128)} %refs_6_.1) | copy-start | bytes 393220
  0.7 161.8 %copy-start.6 = (f32[4,32,256]{2,1,0:T(8,128)S(1)}, f32[4,32,256]{2,1,0:T(8,128)}, u32[]{:S(2)}) copy-start(f32[4,32,256]{2,1,0:T(8,128)} %refs_7_.1) | copy-start | bytes 393220
  0.7 161.8 %copy-start.7 = (f32[4,32,256]{2,1,0:T(8,128)S(1)}, f32[4,32,256]{2,1,0:T(8,128)}, u32[]{:S(2)}) copy-start(f32[4,32,256]{2,1,0:T(8,128)} %refs_12_.1) | copy-start | bytes 393220
  0.7 161.8 %copy-start.8 = (f32[4,32,256]{2,1,0:T(8,128)S(1)}, f32[4,32,256]{2,1,0:T(8,128)}, u32[]{:S(2)}) copy-start(f32[4,32,256]{2,1,0:T(8,128)} %refs_13_.1) | copy-start | bytes 393220
  0.8 161.8 %copy-start.12 = (f32[48,5,8]{0,2,1:T(8,128)S(1)}, f32[48,5,8]{0,2,1:T(8,128)}, u32[]{:S(2)}) copy-start(f32[48,5,8]{0,2,1:T(8,128)} %param.38) | copy-start | bytes 23044
  0.8 161.8 %copy-start.13 = (f32[48,5,8]{0,2,1:T(8,128)S(1)}, f32[48,5,8]{0,2,1:T(8,128)}, u32[]{:S(2)}) copy-start(f32[48,5,8]{0,2,1:T(8,128)} %param.44) | copy-start | bytes 23044
  0.8 161.8 %copy-start.14 = (f32[48,5,8]{0,2,1:T(8,128)S(1)}, f32[48,5,8]{0,2,1:T(8,128)}, u32[]{:S(2)}) copy-start(f32[48,5,8]{0,2,1:T(8,128)} %param.50) | copy-start | bytes 23044
  0.8 161.8 %copy-start.15 = (f32[32,48]{1,0:T(8,128)S(1)}, f32[32,48]{1,0:T(8,128)}, u32[]{:S(2)}) copy-start(f32[32,48]{1,0:T(8,128)} %refs_3_.3) | copy-start | bytes 18436
  0.8 161.8 %copy-start.16 = (f32[32,48]{1,0:T(8,128)S(1)}, f32[32,48]{1,0:T(8,128)}, u32[]{:S(2)}) copy-start(f32[32,48]{1,0:T(8,128)} %refs_9_.3) | copy-start | bytes 18436
  0.8 161.8 %copy-start.17 = (f32[32,48]{1,0:T(8,128)S(1)}, f32[32,48]{1,0:T(8,128)}, u32[]{:S(2)}) copy-start(f32[32,48]{1,0:T(8,128)} %refs_15_.3) | copy-start | bytes 18436
  162.4 0.7 copy-start.22
  162.4 0.7 copy-start.21
  162.4 0.7 copy-start.20
  162.4 0.7 copy-start.25
  163.1 1.0 copy-start.9
  164.1 0.9 copy-start.10
  165.0 0.9 copy-start.11
  165.9 0.7 copy-start.18
  166.6 0.7 copy-start.19
  167.3 0.7 copy-start.23
  168.0 0.7 copy-start.24

commit v3 on v2

--- a/solution.py
+++ b/solution.py
@@ -195,7 +195,11 @@
         if name != "V":
             items.append(("G" + name, vm((D, width), kind)))
         items.append(("S" + name, vm((512, width), kind)))
-        items.append(("B" + name, vm((512, width), kind)))
+        if name in ("A3", "V"):
+            items.append(("B" + name, vm((512, width), kind)))
+        else:
+            items.append(("FP" + name, vm((2, 3, 128, width // 2), kind)))
+            items.append(("FQ" + name, vm((2, 3, 32, width // 2), kind)))
     for name in FETCH:
         items.append(("in_" + name, vm(*fetch_shape(name))))
     items += [
@@ -206,6 +210,8 @@
         ("arecv", dma((5, NQ))),
         ("dsend", dma((19,))),
         ("drecv", dma((19,))),
+        ("tsend", dma((8, 4))),
+        ("trecv", dma((8, 4))),
         ("ssend", dma((16,))),
         ("srecv", dma((16,))),
     ]
@@ -280,16 +286,16 @@
         block = buf.at[pl.ds(rb, 32)]
         to_chips(lambda kk, t: rcopy(block, block, dsend.at[g], drecv.at[g], t, m).start())
 
-    def gather_cross(buf, g, rows=480):
-        drain(buf.at[pl.ds(0, rows)], drecv.at[g])
+    def gather_cross(buf, g):
+        drain(buf.at[pl.ds(0, 480)], drecv.at[g])
         part = buf.at[pl.ds(half, 512)]
         rcopy(part, part, ssend.at[g], srecv.at[g], sib, m).start()
 
     def gather_wait(buf, g):
         drain(buf.at[pl.ds(0, 512)], srecv.at[g])
 
-    def gather_end(buf, g, rows=480):
-        drain(buf.at[pl.ds(0, rows)], dsend.at[g])
+    def gather_end(buf, g):
+        drain(buf.at[pl.ds(0, 480)], dsend.at[g])
         drain(buf.at[pl.ds(0, 512)], ssend.at[g])
 
     def along(axis, i):
@@ -297,33 +303,54 @@
             return (z * 4 + lax.rem(x + i, 4)) * 2 + c
         return (lax.rem(z + i, 4) * 4 + x) * 2 + c
 
-    def two_first(buf, axis, g):
-        block = buf.at[pl.ds(rb, 32)]
+    def sides(buf):
+        n = buf.shape[1] // 2
+        return pl.ds(0, n), pl.ds(n, n)
+
+    def tcopy(src, dst, g, j, t):
+        rcopy(src, dst, R.tsend.at[g, j], R.trecv.at[g, j], t, m).start()
+
+    def two_first(buf, g):
+        left, right = sides(buf)
         for i in (2, 1, 3):
-            rcopy(block, block, dsend.at[g], drecv.at[g], along(axis, i), m).start()
-
-    def two_second(buf, axis, g, before):
-        drain(buf.at[pl.ds(0, 96)], drecv.at[before])
-        if axis == "z":
-            block = buf.at[pl.ds(pl.multiple_of(half + z * 128, 128), 128)]
+            block = buf.at[pl.ds(rb, 32), left]
+            tcopy(block, block, g, 0, along("x", i))
+            block = buf.at[pl.ds(rb, 32), right]
+            tcopy(block, block, g, 1, along("z", i))
+
+    def two_second(buf, g):
+        left, right = sides(buf)
+        drain(buf.at[pl.ds(0, 96), left], R.trecv.at[g, 0])
+        block = buf.at[pl.ds(pl.multiple_of(half + z * 128, 128), 128), left]
+        for i in (2, 1, 3):
+            tcopy(block, block, g, 2, along("z", i))
+        drain(buf.at[pl.ds(0, 96), right], R.trecv.at[g, 1])
+
+        def send(zz):
+            block = buf.at[pl.ds(pl.multiple_of(half + zz * 128 + x * 32, 32), 32), right]
             for i in (2, 1, 3):
-                rcopy(block, block, dsend.at[g], drecv.at[g], along("z", i), m).start()
-        else:
-
-            def send(zz):
-                block = buf.at[pl.ds(pl.multiple_of(half + zz * 128 + x * 32, 32), 32)]
-                for i in (2, 1, 3):
-                    rcopy(block, block, dsend.at[g], drecv.at[g], along("x", i), m).start()
-
-            loop(0, 4, send)
+                tcopy(block, block, g, 3, along("x", i))
+
+        loop(0, 4, send)
+
+    def two_cross(buf, g):
+        for side, j in zip(sides(buf), (2, 3)):
+            drain(buf.at[pl.ds(0, 384), side], R.trecv.at[g, j])
+        part = buf.at[pl.ds(half, 512)]
+        rcopy(part, part, ssend.at[g], srecv.at[g], sib, m).start()
+
+    def two_end(buf, g):
+        left, right = sides(buf)
+        for j, rows in ((0, 96), (1, 96), (2, 384), (3, 384)):
+            drain(buf.at[pl.ds(0, rows), left if j % 2 == 0 else right], R.tsend.at[g, j])
+        drain(buf.at[pl.ds(0, 512)], ssend.at[g])
 
     def reduce_cross(name, g):
         buf, sbuf = (R.GVT if name == "V" else getattr(R, "G" + name)), getattr(R, "S" + name)
         rcopy(buf.at[pl.ds(other, 512)], sbuf, ssend.at[g], srecv.at[g], sib, m).start()
 
-    def reduce_spread(name, g):
+    def core_sum(name, g):
         buf, sbuf = (R.GVT if name == "V" else getattr(R, "G" + name)), getattr(R, "S" + name)
-        bbuf = getattr(R, "B" + name)
         drain(sbuf, srecv.at[g])
 
         def add(i):
@@ -334,6 +361,10 @@
             ).astype(sbuf.dtype)
 
         loop(0, 4, add)
+
+    def reduce_spread(name, g):
+        core_sum(name, g)
+        sbuf, bbuf = getattr(R, "S" + name), getattr(R, "B" + name)
         land = bbuf.at[pl.ds(pl.multiple_of(k * 32, 32), 32)]
 
         def send(kk, t):
@@ -341,6 +372,62 @@
             rcopy(src, land, dsend.at[g], drecv.at[g], t, m).start()
 
         to_chips(send)
+
+    def row_block(zz, xx):
+        return pl.ds(pl.multiple_of(zz * 128 + xx * 32, 32), 32)
+
+    def fold_first(name, g):
+        core_sum(name, g)
+        sbuf, pbuf = getattr(R, "S" + name), getattr(R, "FP" + name)
+        left, right = sides(sbuf)
+        for i in (2, 1, 3):
+            zz = lax.rem(z + i, 4)
+            src = sbuf.at[pl.ds(pl.multiple_of(zz * 128, 128), 128), left]
+            tcopy(src, pbuf.at[0, i - 1], g - 7, 0, along("z", i))
+
+        def send(zz):
+            for i in (2, 1, 3):
+                src = sbuf.at[row_block(zz, lax.rem(x + i, 4)), right]
+                land = pbuf.at[1, i - 1, pl.ds(pl.multiple_of(zz * 32, 32), 32)]
+                tcopy(src, land, g - 7, 1, along("x", i))
+
+        loop(0, 4, send)
+
+    def fold_second(name, g):
+        sbuf, pbuf, qbuf = getattr(R, "S" + name), getattr(R, "FP" + name), getattr(R, "FQ" + name)
+        left, right = sides(sbuf)
+        for side, j in ((left, 0), (right, 1)):
+            drain(pbuf.at[j], R.trecv.at[g - 7, j])
+
+            def add(i):
+                at = row_block(z, i) if j == 0 else row_block(i, x)
+                acc = sbuf[at, side].astype(F32)
+                for n in range(3):
+                    acc = acc + pbuf[j, n, pl.ds(pl.multiple_of(i * 32, 32), 32), :].astype(F32)
+                sbuf[at, side] = acc.astype(sbuf.dtype)
+
+            loop(0, 4, add)
+            for i in (2, 1, 3):
+                if j == 0:
+                    src = sbuf.at[row_block(z, lax.rem(x + i, 4)), side]
+                    tcopy(src, qbuf.at[0, i - 1], g - 7, 2, along("x", i))
+                else:
+                    src = sbuf.at[row_block(lax.rem(z + i, 4), x), side]
+                    tcopy(src, qbuf.at[1, i - 1], g - 7, 3, along("z", i))
+
+    def fold_end(name, g):
+        sbuf, pbuf, qbuf = getattr(R, "S" + name), getattr(R, "FP" + name), getattr(R, "FQ" + name)
+        parts = []
+        for side, j in zip(sides(sbuf), (0, 1)):
+            drain(qbuf.at[j], R.trecv.at[g - 7, 2 + j])
+            acc = sbuf[row_block(z, x), side].astype(F32)
+            for n in range(3):
+                acc = acc + qbuf[j, n].astype(F32)
+            parts.append(acc)
+            drain(pbuf.at[j], R.tsend.at[g - 7, j])
+            drain(qbuf.at[j], R.tsend.at[g - 7, 2 + j])
+        drain(sbuf, ssend.at[g])
+        return jnp.concatenate(parts, 1)
 
     def reduce_end(name, g):
         sbuf, bbuf = getattr(R, "S" + name), getattr(R, "B" + name)
@@ -512,9 +599,6 @@
         rcopy(R.TS.at[:, t], R.TGT.at[m], ysend.at[12], yrecv.at[2], d, t).start()
 
     to_peers(first_sends)
-    gather_start(R.WA3, 0)
-    two_first(R.W1, "x", 17)
-    two_first(R.W2, "z", 18)
     to_peers(later_sends)
 
     fetch("pix").wait()
@@ -557,13 +641,19 @@
         drain(R.HW.at[pl.ds(0, 32), pl.ds(0, 384)], yrecv.at[1])
         R.VEC[pl.ds(rb, 32), :] = R.TA[:, 256:384]
 
+    def first_bulk():
+        gather_start(R.WA3, 5)
+        two_first(R.WB, 1)
+        per_patch()
+
     def bulk():
-        gather_cross(R.WA3, 0)
-        gather_start(R.VEC, 2)
-        gather_start(R.WB, 1)
-        gather_start(R.HW, 5)
-
-    all_sum(R.EWP, R.EWH, R.EWC, R.EWR, 6, (own_slot_done, per_patch, bulk, lambda: None))
+        two_second(R.WB, 1)
+        gather_start(R.VEC, 4)
+        two_first(R.W1, 2)
+        two_first(R.W2, 3)
+        gather_cross(R.WA3, 5)
+
+    all_sum(R.EWP, R.EWH, R.EWC, R.EWR, 6, (own_slot_done, first_bulk, bulk, lambda: None))
 
     head_of = (iota((256, 128), 0) // HEAD_DIM == iota((256, 128), 1)).astype(F32)
     qa = R.EWR[240:241, 0:256].astype(BF).astype(F32)
@@ -586,12 +676,12 @@
         R.OAT[h * 64 : (h + 1) * 64, :] = tn(ewv[:, h * 64 : (h + 1) * 64], R.MT[h])
     R.OA[...] = R.OAT[...].T.astype(BF)
 
-    gather_wait(R.WA3, 0)
+    gather_wait(R.WA3, 5)
     loop(0, NQ, lambda q: branch_send(0, q, R.OA[rows_of(q), :], R.WA3))
-    two_second(R.W1, "z", 3, 17)
-    two_second(R.W2, "x", 4, 18)
-    gather_cross(R.VEC, 2)
-    gather_wait(R.VEC, 2)
+    two_second(R.W1, 2)
+    gather_cross(R.VEC, 4)
+    two_cross(R.WB, 1)
+    gather_wait(R.VEC, 4)
     R.VR[...] = R.VEC[...].T
 
     def natural(i):
@@ -617,7 +707,8 @@
         keep_norm(0, q, n, r)
 
     loop(0, NQ, mixed_rows)
-    gather_cross(R.WB, 1)
+    two_second(R.W2, 3)
+    two_first(R.HW, 0)
     gather_wait(R.WB, 1)
 
     def project(q):
@@ -631,22 +722,18 @@
     loop(0, NQ, project)
     seg_row = R.seg[...].astype(F32)
 
-    def attend(q):
-        rows = rows_of(q)
-        same = R.TCOL[rows, 0:1] == seg_row
-        for h in range(4):
-            at = slice(h * 64, (h + 1) * 64)
-            scores = nt(R.QKV[0, rows, at], R.QKV[1, :, at]) * SCALE
-            scores = jnp.where(same, scores, -1e30)
-            e = jnp.exp(scores - jnp.max(scores, 1, keepdims=True))
-            probs = e / jnp.sum(e, 1, keepdims=True)
-            R.PB[h, rows, :] = probs
-            R.OB[rows, at] = nn(probs.astype(BF), R.QKV[2, :, at]).astype(BF)
-        branch_send(1, q, R.OB[rows, :], R.WB, (768, 1024))
-
-    loop(0, NQ, attend)
-    gather_cross(R.W1, 3, 384)
-    gather_cross(R.W2, 4, 384)
+    same = R.TCOL[:, 0:1] == seg_row
+    for h in range(4):
+        at = slice(h * 64, (h + 1) * 64)
+        scores = nt(R.QKV[0, :, at], R.QKV[1, :, at]) * SCALE
+        scores = jnp.where(same, scores, -1e30)
+        e = jnp.exp(scores - jnp.max(scores, 1, keepdims=True))
+        probs = e / jnp.sum(e, 1, keepdims=True)
+        R.PB[h] = probs
+        R.OB[:, at] = nn(probs.astype(BF), R.QKV[2, :, at]).astype(BF)
+    loop(0, NQ, lambda q: branch_send(1, q, R.OB[rows_of(q), :], R.WB, (768, 1024)))
+    two_cross(R.W1, 2)
+    two_second(R.HW, 0)
 
     def second_rows(q):
         x1 = R.XS[local_of(q), :] + branch_sum(1, q) + vrow(7)
@@ -656,9 +743,10 @@
         keep_norm(1, q, n, r)
 
     loop(0, NQ, second_rows)
-    gather_cross(R.HW, 5)
-    gather_wait(R.W1, 3)
-    gather_wait(R.W2, 4)
+    two_cross(R.W2, 3)
+    two_cross(R.HW, 0)
+    gather_wait(R.W1, 2)
+    gather_wait(R.W2, 3)
 
     def feed(q):
         share_wait(1, q)
@@ -672,7 +760,7 @@
         branch_send(2, q, R.GEL[rows, :], R.W2)
 
     loop(0, NQ, feed)
-    gather_wait(R.HW, 5)
+    gather_wait(R.HW, 0)
     drain(R.TGT.at[pl.ds(0, 3)], yrecv.at[2])
 
     def head_rows(q):
@@ -733,23 +821,28 @@
         R.GVP[7:8, :] = R.GVP[7:8, :] + jnp.sum(dx1, 0, keepdims=True)
         R.GVP[8:9, :] = R.GVP[8:9, :] + dgain
         R.GVP[9:10, :] = R.GVP[9:10, :] + dbias
-        pieces(q, grad_two)
-
+        pieces(q, grad_one)
+
+    for n in range(4):
+        grad_two(pl.ds(n * 256, 256))
+    reduce_cross("2", 13)
+    loop(0, NQ // 2, back_rows)
+    fold_first("2", 13)
+    loop(NQ // 2, NQ, back_rows)
+    reduce_cross("1", 12)
     R.GH[...] = tn(R.H3[...], R.DP[...]).astype(BF)
     reduce_cross("H", 14)
-    loop(0, NQ, back_rows)
-    reduce_cross("2", 13)
 
     def out_back(q):
         share_wait(3, q)
         rows = rows_of(q)
         R.DOB[rows, :] = nn(R.AG[3, rows, :], R.WB[:, 768:1024]).astype(BF)
-        pieces(q, grad_one)
-
-    loop(0, NQ, out_back)
-    reduce_cross("1", 12)
-    reduce_spread("H", 14)
-    reduce_spread("2", 13)
+
+    loop(0, NQ // 2, out_back)
+    fold_first("1", 12)
+    fold_first("H", 14)
+    loop(NQ // 2, NQ, out_back)
+    fold_second("2", 13)
     for h in range(4):
         at = slice(h * 64, (h + 1) * 64)
         probs = R.PB[h]
@@ -765,7 +858,6 @@
     loop(0, NQ, lambda q: branch_send(4, q, R.DQKV[rows_of(q), :], R.WB, (0, 768)))
     R.GVN[5:6, my_cols] = jnp.sum(R.DQKV[:, 0:256].astype(F32), 0, keepdims=True)
     R.GVN[6:7, my_cols] = jnp.sum(R.DQKV[:, 512:768].astype(F32), 0, keepdims=True)
-    reduce_spread("1", 12)
 
     def grad_attn(at):
         R.GB[at, 0:768] = tn(R.AG[0, :, at], R.DQKV[...]).astype(BF)
@@ -782,10 +874,14 @@
         R.GVP[2:3, :] = R.GVP[2:3, :] + jnp.sum(lead * dx0, 0, keepdims=True)
         R.GVP[3:4, :] = R.GVP[3:4, :] + dgain
         R.GVP[4:5, :] = R.GVP[4:5, :] + dbias
-        pieces(q, grad_attn)
-
-    loop(0, NQ, first_rows)
+
+    loop(0, 4, lambda n: grad_attn(pl.ds(pl.multiple_of(n * 256, 256), 256)))
     reduce_cross("B", 11)
+    loop(0, NQ // 2, first_rows)
+    fold_first("B", 11)
+    loop(NQ // 2, NQ, first_rows)
+    fold_second("1", 12)
+    fold_second("H", 14)
     R.TMPV[...] = R.GVN[...].T
     R.GVT[...] = R.GVP[...].T
 
@@ -795,7 +891,6 @@
 
     loop(0, DPN, permuted)
     reduce_cross("V", 15)
-    reduce_spread("B", 11)
     reduce_spread("V", 15)
 
     def mix_back(q):
@@ -845,13 +940,14 @@
         for name in MOMENTS:
             fetch(name + "_f").wait()
             fetch(name + "_s").wait()
-        R.o_mlp[1] = reduce_end("2", 13)
-        R.o_mlp[0] = reduce_end("1", 12)
+        R.o_mlp[1] = fold_end("2", 13)
+        R.o_mlp[0] = fold_end("1", 12)
+        fold_second("B", 11)
         for j in range(2):
             tensor(8 + j, R.in_mlpw[j], R.o_mlp[j], R.in_mlp_f[j], R.in_mlp_s[j])
 
     def hook_third():
-        R.HG[...] = reduce_end("H", 14)
+        R.HG[...] = fold_end("H", 14)
         R.VG[...] = reduce_end("V", 15)
 
         def sends(i, t):
@@ -873,7 +969,7 @@
             ).start()
 
         to_peers(sends)
-        gsum = reduce_end("B", 11)
+        gsum = fold_end("B", 11)
         for j in range(4):
             R.o_attn[j] = gsum[:, j * 256 : (j + 1) * 256]
         for j in range(4):
@@ -940,13 +1036,10 @@
 
     loop(1, DPN, norm_send)
 
-    gather_end(R.WA3, 0)
-    gather_end(R.WB, 1)
-    gather_end(R.VEC, 2)
-    gather_end(R.HW, 5)
-    for buf, g in ((R.W1, 3), (R.W2, 4)):
-        gather_end(buf, g, 384)
-        drain(buf.at[pl.ds(0, 96)], dsend.at[14 + g])
+    gather_end(R.WA3, 5)
+    gather_end(R.VEC, 4)
+    for buf, g in ((R.HW, 0), (R.WB, 1), (R.W1, 2), (R.W2, 3)):
+        two_end(buf, g)
     all_sum_end(R.EWH, R.EWC, R.EWR, 6)
     all_sum_end(R.PRH, R.PRC, R.PRR, 8)
     for ix in range(5):
@@ -990,10 +1083,16 @@
 
 
 def finish(*refs):
-    weights, firsts, seconds, grads = (refs[6 * i : 6 * i + 6] for i in range(4))
-    stats, running = refs[24:26]
+    held, sems = refs[49:75], refs[75]
+    copies = [pltpu.make_async_copy(refs[i], held[i], sems.at[i]) for i in range(26)]
+    for copy in copies[::-1]:
+        copy.start()
     o_loss, o_count, o_running, o_trust, o_norms = refs[26:31]
     o_first, o_second, o_new = (refs[31 + 6 * i : 37 + 6 * i] for i in range(3))
+    weights, firsts, seconds, grads = (held[6 * i : 6 * i + 6] for i in range(4))
+    stats, running = held[24:26]
+    for copy in copies[::-1]:
+        copy.wait()
     norms = jnp.sqrt(stats[0:1, :])
     trust = norms / jnp.sqrt(stats[1:2, :])
     o_norms[...] = norms[:, 0:29]
@@ -1027,14 +1126,17 @@
 def finish_call(weights, firsts, seconds, grads, stats, running):
     shapes = [(1, 1), (1, 1), (1, NVAR), (1, 29), (1, 29)] + 3 * [w.shape for w in weights]
     whole = pl.BlockSpec(memory_space=pltpu.VMEM)
+    values = (*weights, *firsts, *seconds, *grads, stats, running)
     return pl.pallas_call(
         finish,
         out_shape=tuple(jax.ShapeDtypeStruct(s, F32) for s in shapes),
-        in_specs=[whole] * 26,
+        in_specs=[pl.BlockSpec(memory_space=pl.ANY)] * 26,
         out_specs=tuple(whole for unused in shapes),
-        compiler_params=pltpu.CompilerParams(vmem_limit_bytes=32 * 2**20),
+        scratch_shapes=[pltpu.VMEM(v.shape, F32) for v in values]
+        + [pltpu.SemaphoreType.DMA((26,))],
+        compiler_params=pltpu.CompilerParams(vmem_limit_bytes=60 * 2**20),
         name="finish",
-    )(*weights, *firsts, *seconds, *grads, stats, running)
+    )(*values)
 
 
 def on_device(

time: 171 us -> 143 us (0.84)
  Pallas kernels: 163 us -> 142 us
  local copies, waits for them, and re-layouts: 6.15 us -> 0 us
    pallas_call x1, Pallas kernels: 162 us -> 138 us  [mega_call(): pl.pallas_call(mega, out_shape=out_shape, in_specs=[pl.BlockSpec(memory_s...]
    unnamed x52 -> x0, local copies, waits for them, and re-layouts: 6.15 us -> none
    pallas_call x1, Pallas kernels: 1.54 us -> 3.48 us  [finish_call(): pl.pallas_call(finish, out_shape=tuple((jax.ShapeDtypeStruct(s, F32) for...]
where the time goes in v3:
time: 143 us
  Pallas kernels  142 us (99%)
    pallas_call x1, Pallas kernels, mega_call(): pl.pallas_call(mega, out_shape=out_shape, in_specs=[pl.BlockSpec(memory_s...  138 us
    pallas_call x1, Pallas kernels, finish_call(): pl.pallas_call(finish, out_shape=tuple((jax.ShapeDtypeStruct(s, F32) for...  3.48 us

profile of v3, /device:TPU:1, one launch (start us, length us, event | category | flops | bytes accessed | tf_op | source)
XLA Modules:
  0.0 142.6 jit_solution(2515566277579796456)
XLA Ops:
  0.7 138.3 %step.1 = (f32[40,48]{1,0:T(8,128)}, f32[8,17]{1,0:T(8,128)}, f32[4,32,256]{2,1,0:T(8,128)}, f32[4,32,256]{2,1,0:T(8,128)}, f32[2,32,1024]{2,1,0:T(8,128)}, /*index=5*/f32[32,48]{1,0:T(8,128)}, f32[8,128]{1,0:T(8,128)}) custom-call(bf16[192,256]{1,0:T(8,128)(2,1)} %bitcast.35, f32[48,256]{1,0:T(8,128)} %bitcast.42, f32[4,32,256]{2,1,0:T(8,128)} %refs_0_.1, ...), custom_call_target="tpu_custom_call" | custom-call | tf_op jit(solution)/shard_map/step/pallas_call | solution.py:1072
  139.0 3.5 %finish.1 = (f32[1,1]{1,0:T(1,128)}, f32[1,1]{1,0:T(1,128)}, f32[1,48]{1,0:T(1,128)}, f32[1,29]{1,0:T(1,128)}, f32[1,29]{1,0:T(1,128)}, /*index=5*/f32[4,32,256]...) custom-call(f32[4,32,256]{2,1,0:T(8,128)} %refs_0_.1, ...), custom_call_target="tpu_custom_call" | custom-call | tf_op jit(solution)/shard_map/finish/pallas_call | solution.py:1130

commit v4 on v3

--- a/solution.py
+++ b/solution.py
@@ -35,6 +35,10 @@
 NQ = 4
 RQ, CH = TOK // NQ, SH // NQ
 SCALE = 1.0 / math.sqrt(HEAD_DIM)
+FAR_FIRST = sorted(
+    ((dz, dx) for dz in range(4) for dx in range(4) if dz or dx),
+    key=lambda o: -(min(o[0], 4 - o[0]) + min(o[1], 4 - o[1])),
+)
 
 
 def nn(a, b, precision=None):
@@ -127,8 +131,10 @@
         ("WB", vm((D, 1024), BF)),
         ("W1", vm((D, 1024), BF)),
         ("W2", vm((D, 1024), BF)),
-        ("HW", vm((D, 512), BF)),
-        ("VEC", vm((D, 128), F32)),
+        ("HW", vm((D, 256), BF)),
+        ("HWS", vm((MPN, 32, 128), BF)),
+        ("VPK", vm((256, 128), F32)),
+        ("VEC", vm((DPN, 4, 8, 128), F32)),
         ("VR", vm((128, D), F32)),
         ("VRN", vm((128, D), F32)),
         ("TMPV", vm((D, 128), F32)),
@@ -168,7 +174,7 @@
         ("XS", vm((SH, D), F32)),
         ("RR", vm((2, SH, 128), F32)),
         ("H3", vm((SH, D), BF)),
-        ("DP", vm((SH, 512), BF)),
+        ("DP", vm((SH, 256), BF)),
         ("GVT", vm((D, 128), F32)),
         ("GVP", vm((128, D), F32)),
         ("GVN", vm((128, D), F32)),
@@ -176,20 +182,20 @@
         ("TGR", vm((3, 8, 256), F32)),
         ("VG", vm((32, 128), F32)),
         ("VGR", vm((3, 8, 128), F32)),
-        ("HG", vm((32, 512), F32)),
+        ("HG", vm((MPN, 32, 128), F32)),
         ("HGR", vm((3, 32, 128), F32)),
         ("EG", vm((40, NVAR), F32)),
         ("NX", vm((8, 128), F32)),
-        ("NXR", vm((3, 8, 128), F32)),
+        ("NXR", vm((7, 8, 128), F32)),
         ("NY", vm((8, 128), F32)),
-        ("NYR", vm((256, 128), F32)),
+        ("NYR", vm((128, 128), F32)),
     ]
     for name, width, kind in (
         ("A3", 256, BF),
         ("B", 1024, BF),
         ("1", 1024, BF),
         ("2", 1024, BF),
-        ("H", 512, BF),
+        ("H", 256, BF),
         ("V", 128, F32),
     ):
         if name != "V":
@@ -210,8 +216,8 @@
         ("arecv", dma((5, NQ))),
         ("dsend", dma((19,))),
         ("drecv", dma((19,))),
-        ("tsend", dma((8, 4))),
-        ("trecv", dma((8, 4))),
+        ("tsend", dma((9, 4))),
+        ("trecv", dma((9, 4))),
         ("ssend", dma((16,))),
         ("srecv", dma((16,))),
     ]
@@ -267,11 +273,9 @@
             fn(i, lax.rem(m + i, MPN))
 
     def to_chips(fn):
-        def step(i):
-            kk = lax.rem(k + i, CHIPS)
+        for dz, dx in FAR_FIRST:
+            kk = lax.rem(z + dz, 4) * 4 + lax.rem(x + dx, 4)
             fn(kk, kk * 2 + c)
-
-        loop(1, CHIPS, step)
 
     def fetch(name):
         i = FETCH.index(name)
@@ -283,20 +287,20 @@
     ysend, yrecv = R.ysend, R.yrecv
 
     def gather_start(buf, g):
-        block = buf.at[pl.ds(rb, 32)]
+        block = buf.at[pl.ds(pl.multiple_of(c * 128 + k * 8, 8), 8)]
         to_chips(lambda kk, t: rcopy(block, block, dsend.at[g], drecv.at[g], t, m).start())
 
     def gather_cross(buf, g):
-        drain(buf.at[pl.ds(0, 480)], drecv.at[g])
-        part = buf.at[pl.ds(half, 512)]
+        drain(buf.at[pl.ds(0, 120)], drecv.at[g])
+        part = buf.at[pl.ds(pl.multiple_of(c * 128, 128), 128)]
         rcopy(part, part, ssend.at[g], srecv.at[g], sib, m).start()
 
     def gather_wait(buf, g):
-        drain(buf.at[pl.ds(0, 512)], srecv.at[g])
+        drain(buf.at[pl.ds(0, buf.shape[0] // 2)], srecv.at[g])
 
     def gather_end(buf, g):
-        drain(buf.at[pl.ds(0, 480)], dsend.at[g])
-        drain(buf.at[pl.ds(0, 512)], ssend.at[g])
+        drain(buf.at[pl.ds(0, 120)], dsend.at[g])
+        drain(buf.at[pl.ds(0, 128)], ssend.at[g])
 
     def along(axis, i):
         if axis == "x":
@@ -337,13 +341,14 @@
         for side, j in zip(sides(buf), (2, 3)):
             drain(buf.at[pl.ds(0, 384), side], R.trecv.at[g, j])
         part = buf.at[pl.ds(half, 512)]
+        g = 5 if g == 8 else g
         rcopy(part, part, ssend.at[g], srecv.at[g], sib, m).start()
 
     def two_end(buf, g):
         left, right = sides(buf)
         for j, rows in ((0, 96), (1, 96), (2, 384), (3, 384)):
             drain(buf.at[pl.ds(0, rows), left if j % 2 == 0 else right], R.tsend.at[g, j])
-        drain(buf.at[pl.ds(0, 512)], ssend.at[g])
+        drain(buf.at[pl.ds(0, 512)], ssend.at[5 if g == 8 else g])
 
     def reduce_cross(name, g):
         buf, sbuf = (R.GVT if name == "V" else getattr(R, "G" + name)), getattr(R, "S" + name)
@@ -553,6 +558,10 @@
             bar, inc=1, device_id={"dp": d, "mp": lax.rem(m + i, MPN)}, device_id_type=MESH
         )
     loop(1, DPN, greet)
+    for i in range(1, MPN):
+        pl.semaphore_signal(
+            bar, inc=1, device_id={"dp": sib, "mp": lax.rem(m + i, MPN)}, device_id_type=MESH
+        )
 
     vhot = (iota((NVAR, NVAR), 0) == R.vid[...]).astype(F32)
     fetch("emb").wait()
@@ -568,7 +577,7 @@
     R.WA3[pl.ds(rb, 32), :] = R.in_aggw[3].astype(BF)
     R.HWT[...] = jnp.zeros_like(R.HWT)
     R.HWT[:, 0:NVAR] = R.in_headw[...]
-    R.HW[pl.ds(rb, 32), my_slot] = R.HWT[...].astype(BF)
+    R.HWS[m] = R.HWT[...].astype(BF)
     fetch("mlpw").wait()
     R.W1[pl.ds(rb, 32), :] = R.in_mlpw[0].astype(BF)
     R.W2[pl.ds(rb, 32), :] = R.in_mlpw[1].astype(BF)
@@ -587,18 +596,23 @@
     R.GVP[...] = jnp.zeros_like(R.GVP)
     R.GVN[...] = jnp.zeros_like(R.GVN)
     R.NX[...] = jnp.zeros_like(R.NX)
-    pl.semaphore_wait(bar, DPN + MPN - 2)
+    R.HG[...] = jnp.zeros_like(R.HG)
+    pl.semaphore_wait(bar, DPN + 2 * MPN - 3)
 
     def first_sends(i, t):
         part = R.TA.at[my_eight]
         rcopy(part, part, ysend.at[10], yrecv.at[0], d, t).start()
 
     def later_sends(i, t):
-        slot = R.HW.at[pl.ds(rb, 32), my_slot]
+        slot = R.HWS.at[m]
         rcopy(slot, slot, ysend.at[11], yrecv.at[1], d, t).start()
         rcopy(R.TS.at[:, t], R.TGT.at[m], ysend.at[12], yrecv.at[2], d, t).start()
 
     to_peers(first_sends)
+    two_first(R.WA3, 8)
+    two_first(R.WB, 1)
+    two_first(R.W1, 2)
+    two_first(R.W2, 3)
     to_peers(later_sends)
 
     fetch("pix").wait()
@@ -637,23 +651,22 @@
         pick = (lane < NVAR) & (iota((128, 128), 0) == 8 + lax.rem(lane, P_SIZE))
         R.LW[...] = nn(R.TCOL[...], pick.astype(F32), HIGH)
 
-    def own_slot_done():
-        drain(R.HW.at[pl.ds(0, 32), pl.ds(0, 384)], yrecv.at[1])
-        R.VEC[pl.ds(rb, 32), :] = R.TA[:, 256:384]
+    def own_vectors():
+        at = pl.ds(pl.multiple_of(c * 128 + k * 8, 8), 8)
+        for g in range(4):
+            R.VPK[at, 32 * g : 32 * (g + 1)] = R.TA[8 * g : 8 * (g + 1), 256:288]
 
     def first_bulk():
-        gather_start(R.WA3, 5)
-        two_first(R.WB, 1)
+        two_second(R.WA3, 8)
+        gather_start(R.VPK, 4)
         per_patch()
 
     def bulk():
         two_second(R.WB, 1)
-        gather_start(R.VEC, 4)
-        two_first(R.W1, 2)
-        two_first(R.W2, 3)
-        gather_cross(R.WA3, 5)
-
-    all_sum(R.EWP, R.EWH, R.EWC, R.EWR, 6, (own_slot_done, first_bulk, bulk, lambda: None))
+        gather_cross(R.VPK, 4)
+        two_cross(R.WA3, 8)
+
+    all_sum(R.EWP, R.EWH, R.EWC, R.EWR, 6, (own_vectors, first_bulk, bulk, lambda: None))
 
     head_of = (iota((256, 128), 0) // HEAD_DIM == iota((256, 128), 1)).astype(F32)
     qa = R.EWR[240:241, 0:256].astype(BF).astype(F32)
@@ -679,17 +692,12 @@
     gather_wait(R.WA3, 5)
     loop(0, NQ, lambda q: branch_send(0, q, R.OA[rows_of(q), :], R.WA3))
     two_second(R.W1, 2)
-    gather_cross(R.VEC, 4)
+    gather_wait(R.VPK, 4)
+    packed = R.VPK[...].reshape(DPN, 8, 128)
+    for g in range(4):
+        R.VEC[:, g, :, 0:32] = packed[:, :, 32 * g : 32 * (g + 1)]
+    R.VR[...] = R.VEC[...].reshape(D, 128).T
     two_cross(R.WB, 1)
-    gather_wait(R.VEC, 4)
-    R.VR[...] = R.VEC[...].T
-
-    def natural(i):
-        at = pl.multiple_of(lax.rem(i, 2) * 512 + (i // 2) * 32, 32)
-        R.TMPV[pl.ds(pl.multiple_of(i * 32, 32), 32), :] = R.VEC[pl.ds(at, 32), :]
-
-    loop(0, DPN, natural)
-    R.VRN[...] = R.TMPV[...].T
 
     def vrow(i):
         return R.VR[i : i + 1, :]
@@ -708,6 +716,17 @@
 
     loop(0, NQ, mixed_rows)
     two_second(R.W2, 3)
+
+    def natural(i):
+        block = R.VEC[lax.rem(i, 2) * 16 + i // 2]
+        R.TMPV[pl.ds(pl.multiple_of(i * 32, 32), 32), :] = block.reshape(32, 128)
+
+    loop(0, DPN, natural)
+    R.VRN[...] = R.TMPV[...].T
+    drain(R.HWS.at[pl.ds(0, 3)], yrecv.at[1])
+    R.HW[pl.ds(rb, 32), :] = jnp.concatenate(
+        [R.HWS[j].astype(F32)[:, 0:64] for j in range(MPN)], 1
+    ).astype(BF)
     two_first(R.HW, 0)
     gather_wait(R.WB, 1)
 
@@ -733,7 +752,6 @@
         R.OB[:, at] = nn(probs.astype(BF), R.QKV[2, :, at]).astype(BF)
     loop(0, NQ, lambda q: branch_send(1, q, R.OB[rows_of(q), :], R.WB, (768, 1024)))
     two_cross(R.W1, 2)
-    two_second(R.HW, 0)
 
     def second_rows(q):
         x1 = R.XS[local_of(q), :] + branch_sum(1, q) + vrow(7)
@@ -742,9 +760,10 @@
         R.XS[local_of(q), :] = x1
         keep_norm(1, q, n, r)
 
-    loop(0, NQ, second_rows)
+    loop(0, NQ // 2, second_rows)
     two_cross(R.W2, 3)
-    two_cross(R.HW, 0)
+    loop(NQ // 2, NQ, second_rows)
+    two_second(R.HW, 0)
     gather_wait(R.W1, 2)
     gather_wait(R.W2, 3)
 
@@ -759,7 +778,9 @@
             R.GELP[rows, at] = phi + u * jnp.exp(-0.5 * u * u) * (1.0 / math.sqrt(2.0 * math.pi))
         branch_send(2, q, R.GEL[rows, :], R.W2)
 
-    loop(0, NQ, feed)
+    loop(0, NQ - 1, feed)
+    two_cross(R.HW, 0)
+    loop(NQ - 1, NQ, feed)
     gather_wait(R.HW, 0)
     drain(R.TGT.at[pl.ds(0, 3)], yrecv.at[2])
 
@@ -770,14 +791,14 @@
         h3 = (n * vrow(15) + vrow(16)).astype(BF)
         R.H3[here, :] = h3
         pred = nn(h3, R.HW[...])
-        weight = R.LW[own_of(q, m), :]
+        weight = R.LW[own_of(q, m), 0:64]
         for j in range(4):
-            misfit = pred[:, j * 128 : (j + 1) * 128] - R.TGT[j, q]
+            misfit = pred[:, j * 64 : (j + 1) * 64] - R.TGT[j, q, :, 0:64]
             weighted = weight * misfit
-            R.NX[4 + j : 5 + j, :] = R.NX[4 + j : 5 + j, :] + jnp.sum(
+            R.NX[4 + j : 5 + j, 0:64] = R.NX[4 + j : 5 + j, 0:64] + jnp.sum(
                 weighted * misfit, 0, keepdims=True
             )
-            R.DP[here, j * 128 : (j + 1) * 128] = (2.0 * weighted / total_count).astype(BF)
+            R.DP[here, j * 64 : (j + 1) * 64] = (2.0 * weighted / total_count).astype(BF)
         dh3 = nt(R.DP[here, :], R.HW[...])
         dx2, dgain, dbias = ln_back(n, r, vrow(15), dh3)
         share_send(2, q, dx2.astype(BF))
@@ -842,7 +863,6 @@
     fold_first("1", 12)
     fold_first("H", 14)
     loop(NQ // 2, NQ, out_back)
-    fold_second("2", 13)
     for h in range(4):
         at = slice(h * 64, (h + 1) * 64)
         probs = R.PB[h]
@@ -856,6 +876,7 @@
         R.DQKV[:, 256 + h * 64 : 256 + (h + 1) * 64] = dk
         R.DQKV[:, 512 + h * 64 : 512 + (h + 1) * 64] = dv
     loop(0, NQ, lambda q: branch_send(4, q, R.DQKV[rows_of(q), :], R.WB, (0, 768)))
+    fold_second("2", 13)
     R.GVN[5:6, my_cols] = jnp.sum(R.DQKV[:, 0:256].astype(F32), 0, keepdims=True)
     R.GVN[6:7, my_cols] = jnp.sum(R.DQKV[:, 512:768].astype(F32), 0, keepdims=True)
 
@@ -891,7 +912,6 @@
 
     loop(0, DPN, permuted)
     reduce_cross("V", 15)
-    reduce_spread("V", 15)
 
     def mix_back(q):
         share_wait(4, q)
@@ -899,6 +919,8 @@
         R.DOB[rows, :] = nn(R.AG[4, rows, :], R.WA3[...]).astype(BF)
 
     loop(0, NQ, mix_back)
+    reduce_spread("V", 15)
+    fold_second("B", 11)
     R.PRP[...] = jnp.zeros_like(R.PRP)
     for h in range(4):
         at = slice(h * 64, (h + 1) * 64)
@@ -936,23 +958,24 @@
         reduce_cross("A3", 10)
 
     def hook_second():
-        reduce_spread("A3", 10)
         for name in MOMENTS:
             fetch(name + "_f").wait()
             fetch(name + "_s").wait()
         R.o_mlp[1] = fold_end("2", 13)
         R.o_mlp[0] = fold_end("1", 12)
-        fold_second("B", 11)
         for j in range(2):
             tensor(8 + j, R.in_mlpw[j], R.o_mlp[j], R.in_mlp_f[j], R.in_mlp_s[j])
 
     def hook_third():
-        R.HG[...] = fold_end("H", 14)
+        reduce_spread("A3", 10)
+        total = fold_end("H", 14)
+        for j in range(MPN):
+            R.HG[j, :, 0:64] = total[:, 64 * j : 64 * (j + 1)]
         R.VG[...] = reduce_end("V", 15)
 
         def sends(i, t):
             rcopy(
-                R.HG.at[:, pl.ds(pl.multiple_of(t * 128, 128), 128)],
+                R.HG.at[t],
                 R.HGR.at[i - 1],
                 ysend.at[14],
                 yrecv.at[4],
@@ -983,7 +1006,8 @@
     pv = R.PRR[:, 0:256]
     emb = R.TA[:, 0:256]
     wa = [R.in_aggw[j].astype(BF).astype(F32) for j in range(3)]
-    R.TG[...] = nt(wa[1], pk, HIGH) + nt(wa[2], pv, HIGH)
+    pk, pv = pk.astype(BF), pv.astype(BF)
+    R.TG[...] = nt(wa[1].astype(BF), pk) + nt(wa[2].astype(BF), pv)
     R.TG[:, 240:241] = jnp.sum(wa[0] * dqa, 1, keepdims=True)
 
     def last_sends(i, t):
@@ -998,13 +1022,14 @@
 
     to_peers(last_sends)
     R.o_agg[0] = R.TA[:, 256:257] * dqa
-    R.o_agg[1] = nn(emb, pk, HIGH)
-    R.o_agg[2] = nn(emb, pv, HIGH)
+    emb = emb.astype(BF)
+    R.o_agg[1] = nn(emb, pk)
+    R.o_agg[2] = nn(emb, pv)
     R.o_agg[3] = reduce_end("A3", 10)
     for j in range(4):
         tensor(j, R.in_aggw[j], R.o_agg[j], R.in_agg_f[j], R.in_agg_s[j])
     drain(R.HGR, yrecv.at[4])
-    hgrad = R.HG[:, my_slot] + R.HGR[0] + R.HGR[1] + R.HGR[2]
+    hgrad = R.HG[m] + R.HGR[0] + R.HGR[1] + R.HGR[2]
     R.o_head[...] = hgrad[:, 0:NVAR]
     tensor(10, R.in_headw[...], R.o_head[...], R.in_head_f[...], R.in_head_s[...])
     drain(R.VGR, yrecv.at[5])
@@ -1025,20 +1050,21 @@
     R.NX[0:1, 12 : 12 + NVEC] = jnp.sum(R.in_vec[...] * R.in_vec[...], 0, keepdims=True)
     R.NX[1:2, 12 : 12 + NVEC] = jnp.sum(direction * direction, 0, keepdims=True)
 
-    to_peers(lambda i, t: rcopy(R.NX, R.NXR.at[i - 1], ysend.at[16], yrecv.at[6], d, t).start())
+    for j in range(1, 2 * MPN):
+        t = lax.rem(m + j, MPN)
+        rcopy(
+            R.NX, R.NXR.at[j - 1], ysend.at[16], yrecv.at[6], sib if j >= MPN else d, t
+        ).start()
     drain(R.NXR, yrecv.at[6])
-    R.NY[...] = R.NX[...] + R.NXR[0] + R.NXR[1] + R.NXR[2]
-    at_d = pl.ds(pl.multiple_of(d * 8, 8), 8)
-
-    def norm_send(i):
-        t = lax.rem(d + i, DPN)
-        rcopy(R.NY, R.NYR.at[at_d], dsend.at[16], drecv.at[16], t, m).start()
-
-    loop(1, DPN, norm_send)
-
-    gather_end(R.WA3, 5)
-    gather_end(R.VEC, 4)
-    for buf, g in ((R.HW, 0), (R.WB, 1), (R.W1, 2), (R.W2, 3)):
+    norm = R.NX[...]
+    for j in range(7):
+        norm = norm + R.NXR[j]
+    R.NY[...] = norm
+    at_k = pl.ds(pl.multiple_of(k * 8, 8), 8)
+    to_chips(lambda kk, t: rcopy(R.NY, R.NYR.at[at_k], dsend.at[16], drecv.at[16], t, m).start())
+
+    gather_end(R.VPK, 4)
+    for buf, g in ((R.HW, 0), (R.WB, 1), (R.W1, 2), (R.W2, 3), (R.WA3, 8)):
         two_end(buf, g)
     all_sum_end(R.EWH, R.EWC, R.EWR, 6)
     all_sum_end(R.PRH, R.PRC, R.PRR, 8)
@@ -1046,28 +1072,26 @@
         drain(R.RSR.at[ix], ysend.at[ix])
         drain(R.AG.at[ix, pl.ds(0, 192)], ysend.at[5 + ix])
     drain(R.TA.at[pl.ds(0, 24)], ysend.at[10])
-    drain(R.HW.at[pl.ds(0, 32), pl.ds(0, 384)], ysend.at[11])
+    drain(R.HWS.at[pl.ds(0, 3)], ysend.at[11])
     drain(R.TGT.at[pl.ds(0, 3)], ysend.at[12])
     drain(R.TGR, ysend.at[13])
     drain(R.HGR, ysend.at[14])
     drain(R.VGR, ysend.at[15])
     drain(R.NXR, ysend.at[16])
 
-    drain(R.NYR.at[pl.ds(0, 248)], drecv.at[16])
-
-    def norm_add(i, acc):
-        at = pl.multiple_of(lax.rem(d + i, DPN) * 8, 8)
-        return acc + R.NYR[pl.ds(at, 8), :]
-
-    stats = lax.fori_loop(1, DPN, norm_add, R.NY[...])
+    drain(R.NYR.at[pl.ds(0, 120)], drecv.at[16])
+    stats = R.NY[...]
+    for dz, dx in FAR_FIRST:
+        kk = lax.rem(z + dz, 4) * 4 + lax.rem(x + dx, 4)
+        stats = stats + R.NYR[pl.ds(pl.multiple_of(kk * 8, 8), 8), :]
     first_lane = (iota((8, 128), 0) == 0) & (iota((8, 128), 1) == 127)
     R.o_stats[...] = jnp.where(first_lane, total_count, stats)
-    drain(R.NYR.at[pl.ds(0, 248)], dsend.at[16])
+    drain(R.NYR.at[pl.ds(0, 120)], dsend.at[16])
 
 
 def mega_call(large, small):
     outs = [SHAPES[n] for n in ("emb", "vec", "agg", "attn", "mlp", "head")] + [((8, 128), F32)]
-    out_shape = tuple(jax.ShapeDtypeStruct(*item) for item in outs)
+    out_shape = tuple(pltpu.VMEM(*item) for item in outs)
     whole = pl.BlockSpec(memory_space=pltpu.VMEM)
     return pl.pallas_call(
         mega,
@@ -1076,23 +1100,17 @@
         out_specs=tuple(whole for unused in out_shape),
         scratch_shapes=[item for unused, item in SCRATCH],
         compiler_params=pltpu.CompilerParams(
-            collective_id=0, has_side_effects=True, vmem_limit_bytes=60 * 2**20
+            collective_id=0, has_side_effects=True, vmem_limit_bytes=54 * 2**20
         ),
         name="step",
     )(*large, *small)
 
 
 def finish(*refs):
-    held, sems = refs[49:75], refs[75]
-    copies = [pltpu.make_async_copy(refs[i], held[i], sems.at[i]) for i in range(26)]
-    for copy in copies[::-1]:
-        copy.start()
+    weights, firsts, seconds, grads = (refs[6 * i : 6 * i + 6] for i in range(4))
+    stats, running = refs[24:26]
     o_loss, o_count, o_running, o_trust, o_norms = refs[26:31]
-    o_first, o_second, o_new = (refs[31 + 6 * i : 37 + 6 * i] for i in range(3))
-    weights, firsts, seconds, grads = (held[6 * i : 6 * i + 6] for i in range(4))
-    stats, running = held[24:26]
-    for copy in copies[::-1]:
-        copy.wait()
+    outs = refs[31:49]
     norms = jnp.sqrt(stats[0:1, :])
     trust = norms / jnp.sqrt(stats[1:2, :])
     o_norms[...] = norms[:, 0:29]
@@ -1111,9 +1129,9 @@
         first, second, direction = adam_direction(
             weights[i][at], grads[i][at], firsts[i][at], seconds[i][at]
         )
-        o_first[i][at] = first
-        o_second[i][at] = second
-        o_new[i][at] = weights[i][at] - LEARN_RATE * ratio * direction
+        outs[i][at] = first
+        outs[6 + i][at] = second
+        outs[12 + i][at] = weights[i][at] - LEARN_RATE * ratio * direction
 
     for i, number, offset in ((0, 4, 0), (1, 4, 4), (2, 2, 8)):
         for j in range(number):
@@ -1130,11 +1148,9 @@
     return pl.pallas_call(
         finish,
         out_shape=tuple(jax.ShapeDtypeStruct(s, F32) for s in shapes),
-        in_specs=[pl.BlockSpec(memory_space=pl.ANY)] * 26,
-        out_specs=tuple(whole for unused in shapes),
-        scratch_shapes=[pltpu.VMEM(v.shape, F32) for v in values]
-        + [pltpu.SemaphoreType.DMA((26,))],
-        compiler_params=pltpu.CompilerParams(vmem_limit_bytes=60 * 2**20),
+        in_specs=[whole] * 26,
+        out_specs=(whole,) * 23,
+        compiler_params=pltpu.CompilerParams(vmem_limit_bytes=32 * 2**20),
         name="finish",
     )(*values)
 

time: 143 us -> 132 us (0.923)
  Pallas kernels: 142 us -> 130 us
    pallas_call x1, Pallas kernels: 138 us -> 129 us  [mega_call(): pl.pallas_call(mega, out_shape=out_shape, in_specs=[pl.BlockSpec(memory_s...]
    pallas_call x1, Pallas kernels: 3.48 us -> 1.59 us  [finish_call(): pl.pallas_call(finish, out_shape=tuple((jax.ShapeDtypeStruct(s, F32) for...]
where the time goes in v4:
time: 132 us
  Pallas kernels  130 us (98%)
    pallas_call x1, Pallas kernels, mega_call(): pl.pallas_call(mega, out_shape=out_shape, in_specs=[pl.BlockSpec(memory_s...  129 us

profile of v4, /device:TPU:1, one launch (start us, length us, event | category | flops | bytes accessed | tf_op | source)
XLA Modules:
  0.0 132.0 jit_solution(6973282929457078349)
XLA Ops:
  0.7 0.0 copy-start
  0.7 0.0 copy-start.1
  0.7 0.0 copy-start.2
  0.7 0.0 copy-start.3
  0.7 0.0 copy-start.4
  0.7 0.0 copy-start.5
  0.7 0.0 copy-start.6
  0.7 0.0 copy-start.7
  0.7 0.0 copy-start.8
  0.8 0.0 copy-start.9
  0.8 0.0 copy-start.10
  0.8 0.0 copy-start.11
  0.8 0.0 copy-start.12
  0.8 0.0 copy-start.13
  0.8 0.0 copy-start.14
  0.8 128.8 %step.1 = (f32[40,48]{1,0:T(8,128)S(1)}, f32[8,17]{1,0:T(8,128)S(1)}, f32[4,32,256]{2,1,0:T(8,128)S(1)}, f32[4,32,256]{2,1,0:T(8,128)S(1)}, f32[2,32,1024]{2,1,0...) custom-call(bf16[192,256]{1,0:T(8,128)(2,1)} %bitcast.48, f32[48,256]{1,0:T(8,128)} %bitcast.49, ...), custom_call_target="tpu_custom_call" | custom-call | tf_op jit(solution)/shard_map/step/pallas_call | solution.py:1096
  129.6 0.0 copy-start.17
  129.7 0.0 copy-start.16
  129.7 0.0 copy-start.15
  129.7 0.0 copy-start.18
  129.7 0.0 copy-done
  129.7 0.0 copy-done.1
  129.7 0.0 copy-done.2
  129.7 0.0 copy-done.3
  129.7 0.0 copy-done.4
  129.7 0.0 copy-done.5
  129.8 0.0 copy-done.6
  129.8 0.0 copy-done.7
  129.8 0.0 copy-done.8
  129.8 0.0 copy-done.9
  129.8 0.0 copy-done.10
  129.8 0.0 copy-done.11
  129.8 0.0 copy-done.12
  129.8 0.0 copy-done.13
  129.8 0.0 copy-done.14
  129.8 0.5 copy-done.17
  130.3 0.0 copy-done.16
  130.4 0.0 copy-done.15
  130.4 0.0 copy-done.18
  130.4 1.6 %finish.1 = (f32[1,1]{1,0:T(1,128)}, f32[1,1]{1,0:T(1,128)}, f32[1,48]{1,0:T(1,128)}, f32[1,29]{1,0:T(1,128)}, f32[1,29]{1,0:T(1,128)}, /*index=5*/f32[4,32,256]...) custom-call(f32[4,32,256]{2,1,0:T(8,128)S(1)} %copy-done.3, ...), custom_call_target="tpu_custom_call" | custom-call | tf_op jit(solution)/shard_map/finish/pallas_call | solution.py:1148
Async XLA Ops:
  0.7 129.0 %copy-start = (f32[2,32,1024]{2,1,0:T(8,128)S(1)}, f32[2,32,1024]{2,1,0:T(8,128)}, u32[]{:S(2)}) copy-start(f32[2,32,1024]{2,1,0:T(8,128)} %refs_2_.3) | copy-start | bytes 786436
  0.7 129.0 %copy-start.1 = (f32[2,32,1024]{2,1,0:T(8,128)S(1)}, f32[2,32,1024]{2,1,0:T(8,128)}, u32[]{:S(2)}) copy-start(f32[2,32,1024]{2,1,0:T(8,128)} %refs_8_.3) | copy-start | bytes 786436
  0.7 129.0 %copy-start.2 = (f32[2,32,1024]{2,1,0:T(8,128)S(1)}, f32[2,32,1024]{2,1,0:T(8,128)}, u32[]{:S(2)}) copy-start(f32[2,32,1024]{2,1,0:T(8,128)} %refs_14_.3) | copy-start | bytes 786436
  0.7 129.0 %copy-start.3 = (f32[4,32,256]{2,1,0:T(8,128)S(1)}, f32[4,32,256]{2,1,0:T(8,128)}, u32[]{:S(2)}) copy-start(f32[4,32,256]{2,1,0:T(8,128)} %refs_0_.1) | copy-start | bytes 393220
  0.7 129.0 %copy-start.4 = (f32[4,32,256]{2,1,0:T(8,128)S(1)}, f32[4,32,256]{2,1,0:T(8,128)}, u32[]{:S(2)}) copy-start(f32[4,32,256]{2,1,0:T(8,128)} %refs_1_.1) | copy-start | bytes 393220
  0.7 129.0 %copy-start.5 = (f32[4,32,256]{2,1,0:T(8,128)S(1)}, f32[4,32,256]{2,1,0:T(8,128)}, u32[]{:S(2)}) copy-start(f32[4,32,256]{2,1,0:T(8,128)} %refs_6_.1) | copy-start | bytes 393220
  0.7 129.0 %copy-start.6 = (f32[4,32,256]{2,1,0:T(8,128)S(1)}, f32[4,32,256]{2,1,0:T(8,128)}, u32[]{:S(2)}) copy-start(f32[4,32,256]{2,1,0:T(8,128)} %refs_7_.1) | copy-start | bytes 393220
  0.7 129.0 %copy-start.7 = (f32[4,32,256]{2,1,0:T(8,128)S(1)}, f32[4,32,256]{2,1,0:T(8,128)}, u32[]{:S(2)}) copy-start(f32[4,32,256]{2,1,0:T(8,128)} %refs_12_.1) | copy-start | bytes 393220
  0.7 129.0 %copy-start.8 = (f32[4,32,256]{2,1,0:T(8,128)S(1)}, f32[4,32,256]{2,1,0:T(8,128)}, u32[]{:S(2)}) copy-start(f32[4,32,256]{2,1,0:T(8,128)} %refs_13_.1) | copy-start | bytes 393220
  0.8 129.0 %copy-start.9 = (f32[48,5,8]{0,2,1:T(8,128)S(1)}, f32[48,5,8]{0,2,1:T(8,128)}, u32[]{:S(2)}) copy-start(f32[48,5,8]{0,2,1:T(8,128)} %param.38) | copy-start | bytes 23044
  0.8 129.0 %copy-start.10 = (f32[48,5,8]{0,2,1:T(8,128)S(1)}, f32[48,5,8]{0,2,1:T(8,128)}, u32[]{:S(2)}) copy-start(f32[48,5,8]{0,2,1:T(8,128)} %param.44) | copy-start | bytes 23044
  0.8 129.0 %copy-start.11 = (f32[48,5,8]{0,2,1:T(8,128)S(1)}, f32[48,5,8]{0,2,1:T(8,128)}, u32[]{:S(2)}) copy-start(f32[48,5,8]{0,2,1:T(8,128)} %param.50) | copy-start | bytes 23044
  0.8 129.0 %copy-start.12 = (f32[32,48]{1,0:T(8,128)S(1)}, f32[32,48]{1,0:T(8,128)}, u32[]{:S(2)}) copy-start(f32[32,48]{1,0:T(8,128)} %refs_3_.3) | copy-start | bytes 18436
  0.8 129.0 %copy-start.13 = (f32[32,48]{1,0:T(8,128)S(1)}, f32[32,48]{1,0:T(8,128)}, u32[]{:S(2)}) copy-start(f32[32,48]{1,0:T(8,128)} %refs_9_.3) | copy-start | bytes 18436
  0.8 129.0 %copy-start.14 = (f32[32,48]{1,0:T(8,128)S(1)}, f32[32,48]{1,0:T(8,128)}, u32[]{:S(2)}) copy-start(f32[32,48]{1,0:T(8,128)} %refs_15_.3) | copy-start | bytes 18436
  129.6 0.7 copy-start.17
  129.7 0.7 copy-start.16
  129.7 0.7 copy-start.15
  129.7 0.7 copy-start.18

commit v5 on v4

--- a/solution.py
+++ b/solution.py
@@ -100,10 +100,11 @@
     return dx, dgain, dbias
 
 
-LARGE = ("pix", "targ", "aggw", "attnw", "mlpw", "headw", "emb", "vec")
+LARGE = ("emb", "vid", "vec", "aggw", "headw", "mlpw", "attnw", "targ", "pix")
 MOMENTS = ("agg", "attn", "mlp", "head", "emb", "vec")
-SMALL = ("mask", "seg", "leadi", "lat", "vid")
+SMALL = ("mask", "seg", "leadi", "lat", "run")
 OUTS = ("o_emb", "o_vec", "o_agg", "o_attn", "o_mlp", "o_head", "o_stats")
+OUTS = OUTS + ("o_vw", "o_vf", "o_vs", "o_run")
 SHAPES = {
     "pix": ((NVAR * P_SIZE, TOK), BF),
     "targ": ((NVAR, TOK), F32),
@@ -113,10 +114,16 @@
     "head": ((32, NVAR), F32),
     "emb": ((40, NVAR), F32),
     "vec": ((8, NVEC), F32),
+    "mask": ((P_SIZE, TOK), jnp.int32),
+    "seg": ((1, TOK), jnp.int32),
+    "leadi": ((1, SEGS), jnp.int32),
+    "lat": ((1, TOK), jnp.int32),
+    "vid": ((1, NVAR), jnp.int32),
+    "run": ((1, NVAR), F32),
 }
 SHAPES.update({"aggw": SHAPES["agg"], "attnw": SHAPES["attn"], "mlpw": SHAPES["mlp"]})
 SHAPES["headw"] = SHAPES["head"]
-FETCH = LARGE + tuple(n + "_f" for n in MOMENTS) + tuple(n + "_s" for n in MOMENTS)
+FETCH = LARGE + SMALL + tuple(n + "_f" for n in MOMENTS) + tuple(n + "_s" for n in MOMENTS)
 
 
 def fetch_shape(name):
@@ -128,7 +135,9 @@
     dma = pltpu.SemaphoreType.DMA
     items = [
         ("WA3", vm((D, 256), BF)),
-        ("WB", vm((D, 1024), BF)),
+        ("WB", vm((D, 768), BF)),
+        ("WA3F", vm((D, 1024), BF)),
+        ("WB3F", vm((D, 1024), BF)),
         ("W1", vm((D, 1024), BF)),
         ("W2", vm((D, 1024), BF)),
         ("HW", vm((D, 256), BF)),
@@ -148,13 +157,15 @@
         ("LW", vm((TOK, 128), F32)),
         ("PIXT", vm((256, TOK), F32)),
         ("EWP", vm((256, 512), F32)),
-        ("EWH", vm((128, 512), F32)),
-        ("EWC", vm((128, 512), F32)),
-        ("EWR", vm((256, 512), F32)),
+        ("EWB", vm((256, 512), BF)),
+        ("EWC", vm((256, 512), BF)),
+        ("EWH", vm((2, 16, 512), F32)),
+        ("EWR", vm((256, 512), BF)),
         ("PRP", vm((256, 384), F32)),
-        ("PRH", vm((128, 384), F32)),
-        ("PRC", vm((128, 384), F32)),
-        ("PRR", vm((256, 384), F32)),
+        ("PRB", vm((256, 384), BF)),
+        ("PRC", vm((256, 384), BF)),
+        ("PRH", vm((2, 16, 384), F32)),
+        ("PRR", vm((256, 384), BF)),
         ("MT", vm((4, 256, TOK), BF)),
         ("PT", vm((4, NVAR, TOK), F32)),
         ("OAT", vm((256, TOK), F32)),
@@ -165,7 +176,11 @@
         ("QKV", vm((3, TOK, 256), BF)),
         ("PB", vm((4, TOK, TOK), F32)),
         ("OB", vm((TOK, 256), BF)),
+        ("OF", vm((SH, D), BF)),
         ("DOB", vm((TOK, 256), BF)),
+        ("DOF", vm((SH, D), BF)),
+        ("DMB", vm((TOK, 256), BF)),
+        ("DMF", vm((SH, D), BF)),
         ("GEL", vm((TOK, 1024), BF)),
         ("GELP", vm((TOK, 1024), F32)),
         ("DU", vm((TOK, 1024), BF)),
@@ -175,7 +190,10 @@
         ("RR", vm((2, SH, 128), F32)),
         ("H3", vm((SH, D), BF)),
         ("DP", vm((SH, 256), BF)),
-        ("GVT", vm((D, 128), F32)),
+        ("GVT", vm((DPN, 4, 8, 128), F32)),
+        ("GVK", vm((256, 128), F32)),
+        ("GVS", vm((128, 128), F32)),
+        ("GVB", vm((128, 128), F32)),
         ("GVP", vm((128, D), F32)),
         ("GVN", vm((128, D), F32)),
         ("TG", vm((32, 256), F32)),
@@ -196,12 +214,10 @@
         ("1", 1024, BF),
         ("2", 1024, BF),
         ("H", 256, BF),
-        ("V", 128, F32),
     ):
-        if name != "V":
-            items.append(("G" + name, vm((D, width), kind)))
+        items.append(("G" + name, vm((D, width), kind)))
         items.append(("S" + name, vm((512, width), kind)))
-        if name in ("A3", "V"):
+        if name == "A3":
             items.append(("B" + name, vm((512, width), kind)))
         else:
             items.append(("FP" + name, vm((2, 3, 128, width // 2), kind)))
@@ -210,22 +226,23 @@
         items.append(("in_" + name, vm(*fetch_shape(name))))
     items += [
         ("fsem", dma((len(FETCH),))),
-        ("ysend", dma((20,))),
-        ("yrecv", dma((8,))),
+        ("ysend", dma((22,))),
+        ("yrecv", dma((10,))),
+        ("nrecv", dma((2, NQ))),
         ("rrecv", dma((5, NQ))),
         ("arecv", dma((5, NQ))),
         ("dsend", dma((19,))),
         ("drecv", dma((19,))),
-        ("tsend", dma((9, 4))),
-        ("trecv", dma((9, 4))),
-        ("ssend", dma((16,))),
-        ("srecv", dma((16,))),
+        ("tsend", dma((12, 4))),
+        ("trecv", dma((12, 4))),
+        ("ssend", dma((19,))),
+        ("srecv", dma((19,))),
     ]
     return items
 
 
 SCRATCH = scratch_list()
-NAMES = tuple(n + "_hbm" for n in FETCH) + SMALL + OUTS + tuple(n for n, unused in SCRATCH)
+NAMES = tuple(n + "_hbm" for n in FETCH) + OUTS + tuple(n for n, unused in SCRATCH)
 
 
 def mega(*refs):
@@ -341,21 +358,21 @@
         for side, j in zip(sides(buf), (2, 3)):
             drain(buf.at[pl.ds(0, 384), side], R.trecv.at[g, j])
         part = buf.at[pl.ds(half, 512)]
-        g = 5 if g == 8 else g
+        g = {8: 5, 9: 16, 10: 17}.get(g, g)
         rcopy(part, part, ssend.at[g], srecv.at[g], sib, m).start()
 
     def two_end(buf, g):
         left, right = sides(buf)
         for j, rows in ((0, 96), (1, 96), (2, 384), (3, 384)):
             drain(buf.at[pl.ds(0, rows), left if j % 2 == 0 else right], R.tsend.at[g, j])
-        drain(buf.at[pl.ds(0, 512)], ssend.at[5 if g == 8 else g])
+        drain(buf.at[pl.ds(0, 512)], ssend.at[{8: 5, 9: 16, 10: 17}.get(g, g)])
 
     def reduce_cross(name, g):
-        buf, sbuf = (R.GVT if name == "V" else getattr(R, "G" + name)), getattr(R, "S" + name)
+        buf, sbuf = getattr(R, "G" + name), getattr(R, "S" + name)
         rcopy(buf.at[pl.ds(other, 512)], sbuf, ssend.at[g], srecv.at[g], sib, m).start()
 
     def core_sum(name, g):
-        buf, sbuf = (R.GVT if name == "V" else getattr(R, "G" + name)), getattr(R, "S" + name)
+        buf, sbuf = getattr(R, "G" + name), getattr(R, "S" + name)
         drain(sbuf, srecv.at[g])
 
         def add(i):
@@ -449,56 +466,34 @@
         drain(sbuf, ssend.at[g])
         return total
 
-    def all_sum(src, hbuf, cbuf, res, g, hooks):
-        mine_half = pl.multiple_of(c * 128, 128)
-        rcopy(
-            src.at[pl.ds(pl.multiple_of(128 - c * 128, 128), 128)],
-            hbuf,
-            ssend.at[g],
-            srecv.at[g],
-            sib,
-            m,
-        ).start()
+    def all_sum(src, cbuf, hbuf, res, g, hooks):
+        at_k = pl.ds(pl.multiple_of(k * 16, 16), 16)
+
+        def send(kk, t):
+            block = src.at[pl.ds(pl.multiple_of(kk * 16, 16), 16)]
+            rcopy(block, cbuf.at[at_k], dsend.at[g], drecv.at[g], t, m).start()
+
+        to_chips(send)
         hooks[0]()
-        drain(hbuf, srecv.at[g])
-        hbuf[...] = hbuf[...] + src[pl.ds(mine_half, 128), :]
-        at_k = pl.multiple_of(k * 8, 8)
-
-        def send(kk, t):
-            rcopy(
-                hbuf.at[pl.ds(pl.multiple_of(kk * 8, 8), 8)],
-                cbuf.at[pl.ds(at_k, 8)],
-                dsend.at[g],
-                drecv.at[g],
-                t,
-                m,
-            ).start()
-
-        to_chips(send)
+        drain(cbuf.at[pl.ds(0, 240)], drecv.at[g])
+        total = src[at_k, :].astype(F32)
+        for dz, dx in FAR_FIRST:
+            kk = lax.rem(z + dz, 4) * 4 + lax.rem(x + dx, 4)
+            total = total + cbuf[pl.ds(pl.multiple_of(kk * 16, 16), 16), :].astype(F32)
+        hbuf[0] = total
+        rcopy(hbuf.at[0], hbuf.at[1], ssend.at[g], srecv.at[g], sib, m).start()
         hooks[1]()
-        drain(cbuf.at[pl.ds(0, 120)], drecv.at[g])
-
-        def add(i, acc):
-            at = pl.multiple_of(lax.rem(k + i, CHIPS) * 8, 8)
-            return acc + cbuf[pl.ds(at, 8), :]
-
-        total = lax.fori_loop(1, CHIPS, add, hbuf[pl.ds(at_k, 8), :])
-        block = pl.ds(pl.multiple_of(mine_half + at_k, 8), 8)
-        res[block, :] = total
-        part = res.at[block]
+        drain(hbuf.at[1], srecv.at[g])
+        res[at_k, :] = (hbuf[0] + hbuf[1]).astype(BF)
+        part = res.at[at_k]
         to_chips(lambda kk, t: rcopy(part, part, dsend.at[g + 1], drecv.at[g + 1], t, m).start())
         hooks[2]()
-        drain(res.at[pl.ds(0, 120)], drecv.at[g + 1])
-        part2 = res.at[pl.ds(mine_half, 128)]
-        rcopy(part2, part2, ssend.at[g + 1], srecv.at[g + 1], sib, m).start()
-        hooks[3]()
-        drain(res.at[pl.ds(0, 128)], srecv.at[g + 1])
-
-    def all_sum_end(hbuf, cbuf, res, g):
-        drain(hbuf, ssend.at[g])
-        drain(res.at[pl.ds(0, 128)], ssend.at[g + 1])
-        drain(cbuf.at[pl.ds(0, 120)], dsend.at[g])
-        drain(res.at[pl.ds(0, 120)], dsend.at[g + 1])
+        drain(res.at[pl.ds(0, 240)], drecv.at[g + 1])
+
+    def all_sum_end(cbuf, hbuf, res, g):
+        drain(hbuf.at[0], ssend.at[g])
+        drain(cbuf.at[pl.ds(0, 240)], dsend.at[g])
+        drain(res.at[pl.ds(0, 240)], dsend.at[g + 1])
 
     def rows_of(q):
         return pl.ds(pl.multiple_of(q * RQ, RQ), RQ)
@@ -536,6 +531,22 @@
 
     def share_send(ix, q, values):
         R.AG[ix, own_of(q, m), :] = values
+        share_start(ix, q)
+
+    def heads_out(src, dst, q, ss, rs):
+        land = dst.at[local_of(q), my_cols]
+        to_peers(lambda i, t: rcopy(src.at[own_of(q, t)], land, ss, rs, d, t).start())
+        dst[local_of(q), my_cols] = src[own_of(q, m), :]
+
+    def heads_back(src, dst, q, ss, rs):
+        def send(i, t):
+            block = src.at[local_of(q), pl.ds(pl.multiple_of(t * COLS, COLS), COLS)]
+            rcopy(block, dst.at[own_of(q, m)], ss, rs, d, t).start()
+
+        to_peers(send)
+        dst[own_of(q, m), :] = src[local_of(q), my_cols]
+
+    def share_start(ix, q):
         block = R.AG.at[ix, own_of(q, m)]
         to_peers(
             lambda i, t: rcopy(block, block, ysend.at[5 + ix], R.arecv.at[ix, q], d, t).start()
@@ -544,8 +555,6 @@
     def share_wait(ix, q):
         drain(R.AG.at[ix, pl.ds(0, 3 * CH)], R.arecv.at[ix, q])
 
-    for name in FETCH:
-        fetch(name).start()
     bar = pltpu.get_barrier_semaphore()
 
     def greet(i):
@@ -563,7 +572,11 @@
             bar, inc=1, device_id={"dp": sib, "mp": lax.rem(m + i, MPN)}, device_id_type=MESH
         )
 
-    vhot = (iota((NVAR, NVAR), 0) == R.vid[...]).astype(F32)
+    for name in FETCH:
+        fetch(name).start()
+
+    fetch("vid").wait()
+    vhot = (iota((NVAR, NVAR), 0) == R.in_vid[...]).astype(F32)
     fetch("emb").wait()
     fetch("vec").wait()
     chosen = nn(R.in_emb[...], vhot, HIGH)
@@ -582,8 +595,10 @@
     R.W1[pl.ds(rb, 32), :] = R.in_mlpw[0].astype(BF)
     R.W2[pl.ds(rb, 32), :] = R.in_mlpw[1].astype(BF)
     fetch("attnw").wait()
-    for j in range(4):
+    for j in range(3):
         R.WB[pl.ds(rb, 32), j * 256 : (j + 1) * 256] = R.in_attnw[j].astype(BF)
+    R.WB3F[pl.ds(rb, 32), my_cols] = R.in_attnw[3].astype(BF)
+    R.WA3F[pl.ds(rb, 32), my_cols] = R.in_aggw[3].astype(BF)
     fetch("targ").wait()
     R.TT[NVAR:, :] = jnp.zeros((128 - NVAR, TOK), F32)
     R.TT[0:NVAR, :] = R.in_targ[...]
@@ -597,15 +612,20 @@
     R.GVN[...] = jnp.zeros_like(R.GVN)
     R.NX[...] = jnp.zeros_like(R.NX)
     R.HG[...] = jnp.zeros_like(R.HG)
+    R.VG[...] = jnp.zeros_like(R.VG)
     pl.semaphore_wait(bar, DPN + 2 * MPN - 3)
 
     def first_sends(i, t):
         part = R.TA.at[my_eight]
         rcopy(part, part, ysend.at[10], yrecv.at[0], d, t).start()
+        block = R.WB3F.at[pl.ds(rb, 32), my_cols]
+        rcopy(block, block, ysend.at[17], yrecv.at[7], d, t).start()
 
     def later_sends(i, t):
         slot = R.HWS.at[m]
         rcopy(slot, slot, ysend.at[11], yrecv.at[1], d, t).start()
+        block = R.WA3F.at[pl.ds(rb, 32), my_cols]
+        rcopy(block, block, ysend.at[18], yrecv.at[8], d, t).start()
         rcopy(R.TS.at[:, t], R.TGT.at[m], ysend.at[12], yrecv.at[2], d, t).start()
 
     to_peers(first_sends)
@@ -616,6 +636,8 @@
     to_peers(later_sends)
 
     fetch("pix").wait()
+    for name in SMALL:
+        fetch(name).wait()
     rows = iota((256, 192), 0)
     cols = iota((256, 192), 1)
     pick = (rows < 192) & ((lax.rem(rows, NVAR) * P_SIZE + rows // NVAR) == cols)
@@ -628,17 +650,17 @@
     R.EWP[:, 0:256] = tn(emb, aw[1].astype(F32), HIGH)
     R.EWP[:, 256:512] = tn(emb, aw[2].astype(F32), HIGH)
     R.EWP[240:241, 0:256] = jnp.sum(R.TA[:, 256:257] * aw[0].astype(F32), 0, keepdims=True)
-    keep = R.mask[...].astype(F32)
+    R.EWB[...] = R.EWP[...].astype(BF)
+    keep = R.in_mask[...].astype(F32)
     count = jnp.sum(jnp.sum(keep, 1, keepdims=True), 0, keepdims=True) * NVAR
-    R.EWP[241:242, 0:128] = jnp.broadcast_to(count, (1, 128))
 
     def per_patch():
-        seg = R.seg[...]
+        seg = R.in_seg[...]
         lead_row = jnp.zeros((1, TOK), F32)
         for s in range(SEGS):
-            value = (R.leadi[:, s : s + 1] + 1).astype(F32) / LEADS
+            value = (R.in_leadi[:, s : s + 1] + 1).astype(F32) / LEADS
             lead_row = jnp.where(seg == s, value, lead_row)
-        lat = R.lat[...]
+        lat = R.in_lat[...]
         lat_row = jnp.zeros((1, TOK), F32)
         for j, value in enumerate(latitude_weights()):
             lat_row = jnp.where(lat == j, value, lat_row)
@@ -655,10 +677,14 @@
         at = pl.ds(pl.multiple_of(c * 128 + k * 8, 8), 8)
         for g in range(4):
             R.VPK[at, 32 * g : 32 * (g + 1)] = R.TA[8 * g : 8 * (g + 1), 256:288]
+        R.VPK[at, 31:32] = jnp.broadcast_to(count, (8, 1))
 
     def first_bulk():
+        own_vectors()
         two_second(R.WA3, 8)
         gather_start(R.VPK, 4)
+        drain(R.WB3F.at[pl.ds(0, 32), pl.ds(0, 768)], yrecv.at[7])
+        two_first(R.WB3F, 10)
         per_patch()
 
     def bulk():
@@ -666,13 +692,15 @@
         gather_cross(R.VPK, 4)
         two_cross(R.WA3, 8)
 
-    all_sum(R.EWP, R.EWH, R.EWC, R.EWR, 6, (own_vectors, first_bulk, bulk, lambda: None))
+    all_sum(R.EWB, R.EWC, R.EWH, R.EWR, 6, (first_bulk, lambda: None, bulk))
+
+    two_second(R.WB3F, 10)
 
     head_of = (iota((256, 128), 0) // HEAD_DIM == iota((256, 128), 1)).astype(F32)
-    qa = R.EWR[240:241, 0:256].astype(BF).astype(F32)
-    total_count = R.EWR[241:242, 0:1]
-    qe = nn(R.EWR[:, 0:256] * (qa * SCALE), head_of, HIGH)
-    ewv = R.EWR[:, 256:512].astype(BF)
+    ewk = R.EWR[:, 0:256].astype(F32)
+    qa = ewk[240:241, :]
+    qe = nn(ewk * (qa * SCALE), head_of, HIGH)
+    ewv = R.EWR[:, 256:512]
     for h in range(4):
         scores = R.PIXT[0:48, :] * qe[0:48, h : h + 1]
         for p in range(1, 5):
@@ -694,6 +722,7 @@
     two_second(R.W1, 2)
     gather_wait(R.VPK, 4)
     packed = R.VPK[...].reshape(DPN, 8, 128)
+    total_count = jnp.sum(packed, 0)[0:1, 31:32]
     for g in range(4):
         R.VEC[:, g, :, 0:32] = packed[:, :, 32 * g : 32 * (g + 1)]
     R.VR[...] = R.VEC[...].reshape(D, 128).T
@@ -714,8 +743,9 @@
         R.XS[local_of(q), :] = x0
         keep_norm(0, q, n, r)
 
-    loop(0, NQ, mixed_rows)
+    loop(0, NQ // 2, mixed_rows)
     two_second(R.W2, 3)
+    loop(NQ // 2, NQ, mixed_rows)
 
     def natural(i):
         block = R.VEC[lax.rem(i, 2) * 16 + i // 2]
@@ -728,6 +758,7 @@
         [R.HWS[j].astype(F32)[:, 0:64] for j in range(MPN)], 1
     ).astype(BF)
     two_first(R.HW, 0)
+    drain(R.WA3F.at[pl.ds(0, 32), pl.ds(0, 768)], yrecv.at[8])
     gather_wait(R.WB, 1)
 
     def project(q):
@@ -738,8 +769,10 @@
         R.QKV[1, at, :] = nn(h1, R.WB[:, 256:512]).astype(BF)
         R.QKV[2, at, :] = (nn(h1, R.WB[:, 512:768]) + R.VRN[6:7, my_cols]).astype(BF)
 
-    loop(0, NQ, project)
-    seg_row = R.seg[...].astype(F32)
+    loop(0, NQ // 2, project)
+    two_cross(R.WB3F, 10)
+    loop(NQ // 2, NQ, project)
+    seg_row = R.in_seg[...].astype(F32)
 
     same = R.TCOL[:, 0:1] == seg_row
     for h in range(4):
@@ -750,11 +783,13 @@
         probs = e / jnp.sum(e, 1, keepdims=True)
         R.PB[h] = probs
         R.OB[:, at] = nn(probs.astype(BF), R.QKV[2, :, at]).astype(BF)
-    loop(0, NQ, lambda q: branch_send(1, q, R.OB[rows_of(q), :], R.WB, (768, 1024)))
+    loop(0, NQ, lambda q: heads_out(R.OB, R.OF, q, ysend.at[1], R.rrecv.at[1, q]))
     two_cross(R.W1, 2)
+    gather_wait(R.WB3F, 17)
 
     def second_rows(q):
-        x1 = R.XS[local_of(q), :] + branch_sum(1, q) + vrow(7)
+        drain(R.OF.at[pl.ds(0, CH), pl.ds(0, 768)], R.rrecv.at[1, q])
+        x1 = R.XS[local_of(q), :] + nt(R.OF[local_of(q), :], R.WB3F[...]) + vrow(7)
         n, r = ln_parts(x1)
         share_send(1, q, (n * vrow(8) + vrow(9)).astype(BF))
         R.XS[local_of(q), :] = x1
@@ -764,6 +799,7 @@
     two_cross(R.W2, 3)
     loop(NQ // 2, NQ, second_rows)
     two_second(R.HW, 0)
+    two_first(R.WA3F, 9)
     gather_wait(R.W1, 2)
     gather_wait(R.W2, 3)
 
@@ -781,6 +817,7 @@
     loop(0, NQ - 1, feed)
     two_cross(R.HW, 0)
     loop(NQ - 1, NQ, feed)
+    two_second(R.WA3F, 9)
     gather_wait(R.HW, 0)
     drain(R.TGT.at[pl.ds(0, 3)], yrecv.at[2])
 
@@ -821,6 +858,7 @@
         branch_send(3, q, R.DU[rows, :], R.W1)
 
     loop(0, NQ, feed_back)
+    two_cross(R.WA3F, 9)
 
     def pieces(q, fn):
         for j in range(4 // NQ):
@@ -837,7 +875,10 @@
         n = R.LN[1, here, :]
         dx1, dgain, dbias = ln_back(n, R.RR[1, here, 0:1], vrow(8), branch_sum(3, q))
         dx1 = dx1 + R.XS[here, :]
-        share_send(3, q, dx1.astype(BF))
+        dy = dx1.astype(BF)
+        R.DOF[here, :] = nn(dy, R.WB3F[...]).astype(BF)
+        heads_back(R.DOF, R.DOB, q, ysend.at[19], R.nrecv.at[0, q])
+        R.AG[3, own_of(q, m), :] = dy
         R.XS[here, :] = dx1
         R.GVP[7:8, :] = R.GVP[7:8, :] + jnp.sum(dx1, 0, keepdims=True)
         R.GVP[8:9, :] = R.GVP[8:9, :] + dgain
@@ -850,19 +891,15 @@
     loop(0, NQ // 2, back_rows)
     fold_first("2", 13)
     loop(NQ // 2, NQ, back_rows)
+    loop(0, NQ, lambda q: share_start(3, q))
     reduce_cross("1", 12)
     R.GH[...] = tn(R.H3[...], R.DP[...]).astype(BF)
     reduce_cross("H", 14)
-
-    def out_back(q):
-        share_wait(3, q)
-        rows = rows_of(q)
-        R.DOB[rows, :] = nn(R.AG[3, rows, :], R.WB[:, 768:1024]).astype(BF)
-
-    loop(0, NQ // 2, out_back)
+    gather_wait(R.WA3F, 16)
     fold_first("1", 12)
     fold_first("H", 14)
-    loop(NQ // 2, NQ, out_back)
+
+    loop(0, NQ, lambda q: drain(R.DOB.at[pl.ds(0, 3 * CH)], R.nrecv.at[0, q]))
     for h in range(4):
         at = slice(h * 64, (h + 1) * 64)
         probs = R.PB[h]
@@ -882,6 +919,9 @@
 
     def grad_attn(at):
         R.GB[at, 0:768] = tn(R.AG[0, :, at], R.DQKV[...]).astype(BF)
+
+    def grad_out(n):
+        at = pl.ds(pl.multiple_of(n * 256, 256), 256)
         R.GB[at, 768:1024] = tn(R.AG[3, :, at], R.OB[...]).astype(BF)
 
     def first_rows(q):
@@ -889,7 +929,10 @@
         n = R.LN[0, here, :]
         dx0, dgain, dbias = ln_back(n, R.RR[0, here, 0:1], vrow(3), branch_sum(4, q))
         dx0 = dx0 + R.XS[here, :]
-        share_send(4, q, dx0.astype(BF))
+        dya = dx0.astype(BF)
+        R.DMF[here, :] = nn(dya, R.WA3F[...]).astype(BF)
+        heads_back(R.DMF, R.DMB, q, ysend.at[20], R.nrecv.at[1, q])
+        R.AG[4, own_of(q, m), :] = dya
         lead = R.TCOL[own_of(q, m), 1:2]
         R.GVP[1:2, :] = R.GVP[1:2, :] + jnp.sum(dx0, 0, keepdims=True)
         R.GVP[2:3, :] = R.GVP[2:3, :] + jnp.sum(lead * dx0, 0, keepdims=True)
@@ -897,34 +940,64 @@
         R.GVP[4:5, :] = R.GVP[4:5, :] + dbias
 
     loop(0, 4, lambda n: grad_attn(pl.ds(pl.multiple_of(n * 256, 256), 256)))
+    loop(0, NQ, lambda q: share_wait(3, q))
+    loop(0, 4, grad_out)
     reduce_cross("B", 11)
     loop(0, NQ // 2, first_rows)
     fold_first("B", 11)
     loop(NQ // 2, NQ, first_rows)
+    loop(0, NQ, lambda q: share_start(4, q))
     fold_second("1", 12)
     fold_second("H", 14)
     R.TMPV[...] = R.GVN[...].T
-    R.GVT[...] = R.GVP[...].T
+    R.GVT[...] = R.GVP[...].T.reshape(DPN, 4, 8, 128)
 
     def permuted(i):
-        at = pl.ds(pl.multiple_of(lax.rem(i, 2) * 512 + (i // 2) * 32, 32), 32)
-        R.GVT[at, :] = R.GVT[at, :] + R.TMPV[pl.ds(pl.multiple_of(i * 32, 32), 32), :]
+        block = lax.rem(i, 2) * 16 + i // 2
+        own = R.TMPV[pl.ds(pl.multiple_of(i * 32, 32), 32), :]
+        R.GVT[block] = R.GVT[block] + own.reshape(4, 8, 128)
 
     loop(0, DPN, permuted)
-    reduce_cross("V", 15)
-
-    def mix_back(q):
-        share_wait(4, q)
-        rows = rows_of(q)
-        R.DOB[rows, :] = nn(R.AG[4, rows, :], R.WA3[...]).astype(BF)
-
-    loop(0, NQ, mix_back)
-    reduce_spread("V", 15)
-    fold_second("B", 11)
+    for g in range(4):
+        R.GVK[:, 32 * g : 32 * (g + 1)] = R.GVT[:, g, :, 0:32].reshape(256, 32)
+    core_rows = pl.ds(pl.multiple_of(c * 128, 128), 128)
+    rcopy(
+        R.GVK.at[pl.ds(pl.multiple_of(128 - c * 128, 128), 128)],
+        R.GVS,
+        ssend.at[15],
+        srecv.at[15],
+        sib,
+        m,
+    ).start()
+    at_eight = pl.ds(pl.multiple_of(k * 8, 8), 8)
+
+    def vectors_spread():
+        drain(R.GVS, srecv.at[15])
+        R.GVS[...] = R.GVS[...] + R.GVK[core_rows, :]
+
+        def send(kk, t):
+            src = R.GVS.at[pl.ds(pl.multiple_of(kk * 8, 8), 8)]
+            rcopy(src, R.GVB.at[at_eight], dsend.at[15], drecv.at[15], t, m).start()
+
+        to_chips(send)
+
+    def vectors_end():
+        drain(R.GVB.at[pl.ds(0, 120)], drecv.at[15])
+        total = R.GVS[at_eight, :]
+        for dz, dx in FAR_FIRST:
+            kk = lax.rem(z + dz, 4) * 4 + lax.rem(x + dx, 4)
+            total = total + R.GVB[pl.ds(pl.multiple_of(kk * 8, 8), 8), :]
+        for g in range(4):
+            R.VG[8 * g : 8 * (g + 1), 0:32] = total[:, 32 * g : 32 * (g + 1)]
+        drain(R.GVB.at[pl.ds(0, 120)], dsend.at[15])
+        drain(R.GVS, ssend.at[15])
+
+    loop(0, NQ, lambda q: drain(R.DMB.at[pl.ds(0, 3 * CH)], R.nrecv.at[1, q]))
+    vectors_spread()
     R.PRP[...] = jnp.zeros_like(R.PRP)
     for h in range(4):
         at = slice(h * 64, (h + 1) * 64)
-        dout = R.DOB[:, at]
+        dout = R.DMB[:, at]
         through = nt(ewv[:, at], dout)
         dprob = R.PIXT[0:48, :] * through[0:48, :]
         for p in range(1, 5):
@@ -936,6 +1009,7 @@
             row = slice(p * 48, (p + 1) * 48)
             R.PRP[row, 256 + h : 257 + h] = jnp.sum(ds * R.PIXT[row, :], 1, keepdims=True)
         R.PRP[:, at] = nn(R.MT[h], dout)
+    R.PRB[...] = R.PRP[...].astype(BF)
 
     lanes = iota((1, 128), 1)
     sums = {"w": jnp.zeros((1, 128), F32), "u": jnp.zeros((1, 128), F32)}
@@ -949,7 +1023,9 @@
         sums["w"] = sums["w"] + jnp.where(here, square_sum(weight), 0.0)
         sums["u"] = sums["u"] + jnp.where(here, square_sum(direction), 0.0)
 
-    def hook_first():
+    def hook_second():
+        loop(0, NQ, lambda q: share_wait(4, q))
+
         def piece(n):
             at = pl.ds(pl.multiple_of(n * 256, 256), 256)
             R.GA3[at, :] = tn(R.AG[4, :, at], R.OA[...]).astype(BF)
@@ -957,7 +1033,7 @@
         loop(0, 4, piece)
         reduce_cross("A3", 10)
 
-    def hook_second():
+    def hook_first():
         for name in MOMENTS:
             fetch(name + "_f").wait()
             fetch(name + "_s").wait()
@@ -965,13 +1041,12 @@
         R.o_mlp[0] = fold_end("1", 12)
         for j in range(2):
             tensor(8 + j, R.in_mlpw[j], R.o_mlp[j], R.in_mlp_f[j], R.in_mlp_s[j])
-
+        fold_second("B", 11)
     def hook_third():
-        reduce_spread("A3", 10)
         total = fold_end("H", 14)
         for j in range(MPN):
             R.HG[j, :, 0:64] = total[:, 64 * j : 64 * (j + 1)]
-        R.VG[...] = reduce_end("V", 15)
+        vectors_end()
 
         def sends(i, t):
             rcopy(
@@ -997,16 +1072,17 @@
             R.o_attn[j] = gsum[:, j * 256 : (j + 1) * 256]
         for j in range(4):
             tensor(4 + j, R.in_attnw[j], R.o_attn[j], R.in_attn_f[j], R.in_attn_s[j])
-
-    all_sum(R.PRP, R.PRH, R.PRC, R.PRR, 8, (hook_first, hook_second, hook_third, lambda: None))
-
-    spread = nt(R.PRR[:, 256:384], head_of, HIGH)
-    dqa = jnp.sum(spread * R.EWR[:, 0:256], 0, keepdims=True) * SCALE
+        reduce_spread("A3", 10)
+
+    all_sum(R.PRB, R.PRC, R.PRH, R.PRR, 8, (hook_first, hook_second, hook_third))
+
+    spread = nt(R.PRR[:, 256:384], head_of.astype(BF))
+    dqa = jnp.sum(spread * ewk, 0, keepdims=True) * SCALE
     pk = spread * (qa * SCALE)
     pv = R.PRR[:, 0:256]
     emb = R.TA[:, 0:256]
     wa = [R.in_aggw[j].astype(BF).astype(F32) for j in range(3)]
-    pk, pv = pk.astype(BF), pv.astype(BF)
+    pk = pk.astype(BF)
     R.TG[...] = nt(wa[1].astype(BF), pk) + nt(wa[2].astype(BF), pv)
     R.TG[:, 240:241] = jnp.sum(wa[0] * dqa, 1, keepdims=True)
 
@@ -1025,8 +1101,7 @@
     emb = emb.astype(BF)
     R.o_agg[1] = nn(emb, pk)
     R.o_agg[2] = nn(emb, pv)
-    R.o_agg[3] = reduce_end("A3", 10)
-    for j in range(4):
+    for j in range(3):
         tensor(j, R.in_aggw[j], R.o_agg[j], R.in_agg_f[j], R.in_agg_s[j])
     drain(R.HGR, yrecv.at[4])
     hgrad = R.HG[m] + R.HGR[0] + R.HGR[1] + R.HGR[2]
@@ -1045,6 +1120,12 @@
     unused, unused2, direction = adam_direction(
         R.in_vec[...], R.o_vec[...], R.in_vec_f[...], R.in_vec_s[...]
     )
+    R.o_agg[3] = reduce_end("A3", 10)
+    tensor(3, R.in_aggw[3], R.o_agg[3], R.in_agg_f[3], R.in_agg_s[3])
+    R.o_vw[...] = R.in_vec[...]
+    R.o_vf[...] = R.in_vec_f[...]
+    R.o_vs[...] = R.in_vec_s[...]
+    R.o_run[...] = R.in_run[...]
     R.NX[0:1, :] = sums["w"]
     R.NX[1:2, :] = sums["u"]
     R.NX[0:1, 12 : 12 + NVEC] = jnp.sum(R.in_vec[...] * R.in_vec[...], 0, keepdims=True)
@@ -1064,12 +1145,15 @@
     to_chips(lambda kk, t: rcopy(R.NY, R.NYR.at[at_k], dsend.at[16], drecv.at[16], t, m).start())
 
     gather_end(R.VPK, 4)
-    for buf, g in ((R.HW, 0), (R.WB, 1), (R.W1, 2), (R.W2, 3), (R.WA3, 8)):
+    for buf, g in ((R.HW, 0), (R.WB, 1), (R.W1, 2), (R.W2, 3), (R.WA3, 8), (R.WA3F, 9), (R.WB3F, 10)):
         two_end(buf, g)
-    all_sum_end(R.EWH, R.EWC, R.EWR, 6)
-    all_sum_end(R.PRH, R.PRC, R.PRR, 8)
+    all_sum_end(R.EWC, R.EWH, R.EWR, 6)
+    all_sum_end(R.PRC, R.PRH, R.PRR, 8)
     for ix in range(5):
-        drain(R.RSR.at[ix], ysend.at[ix])
+        if ix == 1:
+            drain(R.OF.at[:, pl.ds(0, 768)], ysend.at[1])
+        else:
+            drain(R.RSR.at[ix], ysend.at[ix])
         drain(R.AG.at[ix, pl.ds(0, 192)], ysend.at[5 + ix])
     drain(R.TA.at[pl.ds(0, 24)], ysend.at[10])
     drain(R.HWS.at[pl.ds(0, 3)], ysend.at[11])
@@ -1078,6 +1162,10 @@
     drain(R.HGR, ysend.at[14])
     drain(R.VGR, ysend.at[15])
     drain(R.NXR, ysend.at[16])
+    drain(R.WB3F.at[pl.ds(0, 32), pl.ds(0, 768)], ysend.at[17])
+    drain(R.WA3F.at[pl.ds(0, 32), pl.ds(0, 768)], ysend.at[18])
+    drain(R.OF.at[:, pl.ds(0, 768)], ysend.at[19])
+    drain(R.OF.at[:, pl.ds(0, 768)], ysend.at[20])
 
     drain(R.NYR.at[pl.ds(0, 120)], drecv.at[16])
     stats = R.NY[...]
@@ -1089,21 +1177,21 @@
     drain(R.NYR.at[pl.ds(0, 120)], dsend.at[16])
 
 
-def mega_call(large, small):
+def mega_call(inputs):
     outs = [SHAPES[n] for n in ("emb", "vec", "agg", "attn", "mlp", "head")] + [((8, 128), F32)]
-    out_shape = tuple(pltpu.VMEM(*item) for item in outs)
+    outs += [SHAPES["vec"]] * 3 + [SHAPES["run"]]
     whole = pl.BlockSpec(memory_space=pltpu.VMEM)
     return pl.pallas_call(
         mega,
-        out_shape=out_shape,
-        in_specs=[pl.BlockSpec(memory_space=pl.ANY)] * len(large) + [whole] * len(small),
-        out_specs=tuple(whole for unused in out_shape),
+        out_shape=tuple(pltpu.VMEM(*item) for item in outs),
+        in_specs=[pl.BlockSpec(memory_space=pl.ANY)] * len(inputs),
+        out_specs=(whole,) * len(outs),
         scratch_shapes=[item for unused, item in SCRATCH],
         compiler_params=pltpu.CompilerParams(
             collective_id=0, has_side_effects=True, vmem_limit_bytes=54 * 2**20
         ),
         name="step",
-    )(*large, *small)
+    )(*inputs)
 
 
 def finish(*refs):
@@ -1171,17 +1259,23 @@
         return (agg, attn, mlp, head, embed.transpose(1, 2, 0).reshape(40, NVAR), vecs.T)
 
     weights, firsts, seconds = (turned(tensors[6 * i : 6 * i + 6]) for i in range(3))
-    large = (pixels.T, targets.T, *weights, *firsts, *seconds)
-    small = (
+    agg, attn, mlp, head, embed, vecs = weights
+    first = (embed, var_ids.reshape(1, NVAR), vecs, agg, head, mlp, attn, targets.T, pixels.T)
+    second = (
         valid_mask.T,
         segments,
         lead_index,
         latitude.reshape(1, TOK),
-        var_ids.reshape(1, NVAR),
+        running_error.reshape(1, NVAR),
     )
-    g_emb, g_vec, g_agg, g_attn, g_mlp, g_head, stats = mega_call(large, small)
+    g_emb, g_vec, g_agg, g_attn, g_mlp, g_head, stats, *rest = mega_call(
+        (*first, *second, *firsts, *seconds)
+    )
     grads = (g_agg, g_attn, g_mlp, g_head, g_emb, g_vec)
-    out = finish_call(weights, firsts, seconds, grads, stats, running_error.reshape(1, NVAR))
+    weights, firsts, seconds = (
+        (*group[:5], own) for group, own in zip((weights, firsts, seconds), rest)
+    )
+    out = finish_call(weights, firsts, seconds, grads, stats, rest[3])
 
     def back(group):
         agg, attn, mlp, head, embed, vecs = group

time: 132 us -> 126 us (0.955)
  Pallas kernels: 130 us -> 124 us
    pallas_call x1, Pallas kernels: 129 us -> 123 us  [mega_call(): pl.pallas_call(mega, out_shape=tuple((pltpu.VMEM(*item) for item in outs)...]
where the time goes in v5:
time: 126 us
  Pallas kernels  124 us (98%)
    pallas_call x1, Pallas kernels, mega_call(): pl.pallas_call(mega, out_shape=tuple((pltpu.VMEM(*item) for item in outs)...  123 us

profile of v5, /device:TPU:1, one launch (start us, length us, event | category | flops | bytes accessed | tf_op | source)
XLA Modules:
  0.0 125.9 jit_solution(15618487956328102439)
XLA Ops:
  0.7 0.0 copy-start
  0.7 0.0 copy-start.1
  0.7 0.0 copy-start.2
  0.7 0.0 copy-start.3
  0.7 0.0 copy-start.4
  0.7 0.0 copy-start.5
  0.7 0.0 copy-start.6
  0.7 0.0 copy-start.7
  0.7 0.0 copy-start.8
  0.8 0.0 copy-start.10
  0.8 0.0 copy-start.11
  0.8 0.0 copy-start.12
  0.8 0.0 copy-start.13
  0.8 0.0 copy-start.14
  0.8 122.7 %step.1 = (f32[40,48]{1,0:T(8,128)S(1)}, f32[8,17]{1,0:T(8,128)S(1)}, f32[4,32,256]{2,1,0:T(8,128)S(1)}, f32[4,32,256]{2,1,0:T(8,128)S(1)}, f32[2,32,1024]{2,1,0...) custom-call(f32[40,48]{1,0:T(8,128)} %bitcast.35, ...), custom_call_target="tpu_custom_call" | custom-call | tf_op jit(solution)/shard_map/step/pallas_call | solution.py:1184
  123.6 0.0 copy-start.9
  123.6 0.0 copy-done
  123.6 0.0 copy-done.1
  123.6 0.0 copy-done.2
  123.6 0.0 copy-done.3
  123.6 0.0 copy-done.4
  123.6 0.0 copy-done.5
  123.6 0.0 copy-done.6
  123.6 0.0 copy-done.7
  123.7 0.0 copy-done.8
  123.7 0.0 copy-done.10
  123.7 0.0 copy-done.11
  123.7 0.0 copy-done.12
  123.7 0.0 copy-done.13
  123.7 0.0 copy-done.14
  123.7 0.6 copy-done.9
  124.3 1.5 %finish.1 = (f32[1,1]{1,0:T(1,128)}, f32[1,1]{1,0:T(1,128)}, f32[1,48]{1,0:T(1,128)}, f32[1,29]{1,0:T(1,128)}, f32[1,29]{1,0:T(1,128)}, /*index=5*/f32[4,32,256]...) custom-call(f32[4,32,256]{2,1,0:T(8,128)S(1)} %copy-done.3, ...), custom_call_target="tpu_custom_call" | custom-call | tf_op jit(solution)/shard_map/finish/pallas_call | solution.py:1236
Async XLA Ops:
  0.7 122.9 %copy-start = (f32[2,32,1024]{2,1,0:T(8,128)S(1)}, f32[2,32,1024]{2,1,0:T(8,128)}, u32[]{:S(2)}) copy-start(f32[2,32,1024]{2,1,0:T(8,128)} %refs_2_.1) | copy-start | bytes 786436
  0.7 122.9 %copy-start.1 = (f32[2,32,1024]{2,1,0:T(8,128)S(1)}, f32[2,32,1024]{2,1,0:T(8,128)}, u32[]{:S(2)}) copy-start(f32[2,32,1024]{2,1,0:T(8,128)} %refs_8_.1) | copy-start | bytes 786436
  0.7 122.9 %copy-start.2 = (f32[2,32,1024]{2,1,0:T(8,128)S(1)}, f32[2,32,1024]{2,1,0:T(8,128)}, u32[]{:S(2)}) copy-start(f32[2,32,1024]{2,1,0:T(8,128)} %refs_14_.3) | copy-start | bytes 786436
  0.7 122.9 %copy-start.3 = (f32[4,32,256]{2,1,0:T(8,128)S(1)}, f32[4,32,256]{2,1,0:T(8,128)}, u32[]{:S(2)}) copy-start(f32[4,32,256]{2,1,0:T(8,128)} %refs_0_.1) | copy-start | bytes 393220
  0.7 122.9 %copy-start.4 = (f32[4,32,256]{2,1,0:T(8,128)S(1)}, f32[4,32,256]{2,1,0:T(8,128)}, u32[]{:S(2)}) copy-start(f32[4,32,256]{2,1,0:T(8,128)} %refs_1_.1) | copy-start | bytes 393220
  0.7 122.9 %copy-start.5 = (f32[4,32,256]{2,1,0:T(8,128)S(1)}, f32[4,32,256]{2,1,0:T(8,128)}, u32[]{:S(2)}) copy-start(f32[4,32,256]{2,1,0:T(8,128)} %refs_6_.3) | copy-start | bytes 393220
  0.7 122.9 %copy-start.6 = (f32[4,32,256]{2,1,0:T(8,128)S(1)}, f32[4,32,256]{2,1,0:T(8,128)}, u32[]{:S(2)}) copy-start(f32[4,32,256]{2,1,0:T(8,128)} %refs_7_.1) | copy-start | bytes 393220
  0.7 122.9 %copy-start.7 = (f32[4,32,256]{2,1,0:T(8,128)S(1)}, f32[4,32,256]{2,1,0:T(8,128)}, u32[]{:S(2)}) copy-start(f32[4,32,256]{2,1,0:T(8,128)} %refs_12_.1) | copy-start | bytes 393220
  0.7 122.9 %copy-start.8 = (f32[4,32,256]{2,1,0:T(8,128)S(1)}, f32[4,32,256]{2,1,0:T(8,128)}, u32[]{:S(2)}) copy-start(f32[4,32,256]{2,1,0:T(8,128)} %refs_13_.1) | copy-start | bytes 393220
  0.8 122.9 %copy-start.10 = (f32[48,5,8]{0,2,1:T(8,128)S(1)}, f32[48,5,8]{0,2,1:T(8,128)}, u32[]{:S(2)}) copy-start(f32[48,5,8]{0,2,1:T(8,128)} %param.44) | copy-start | bytes 23044
  0.8 122.9 %copy-start.11 = (f32[48,5,8]{0,2,1:T(8,128)S(1)}, f32[48,5,8]{0,2,1:T(8,128)}, u32[]{:S(2)}) copy-start(f32[48,5,8]{0,2,1:T(8,128)} %param.50) | copy-start | bytes 23044
  0.8 122.9 %copy-start.12 = (f32[32,48]{1,0:T(8,128)S(1)}, f32[32,48]{1,0:T(8,128)}, u32[]{:S(2)}) copy-start(f32[32,48]{1,0:T(8,128)} %refs_3_.3) | copy-start | bytes 18436
  0.8 122.9 %copy-start.13 = (f32[32,48]{1,0:T(8,128)S(1)}, f32[32,48]{1,0:T(8,128)}, u32[]{:S(2)}) copy-start(f32[32,48]{1,0:T(8,128)} %refs_9_.1) | copy-start | bytes 18436
  0.8 122.9 %copy-start.14 = (f32[32,48]{1,0:T(8,128)S(1)}, f32[32,48]{1,0:T(8,128)}, u32[]{:S(2)}) copy-start(f32[32,48]{1,0:T(8,128)} %refs_15_.3) | copy-start | bytes 18436
  123.6 0.7 copy-start.9

commit v6 on v5

--- a/solution.py
+++ b/solution.py
@@ -197,20 +197,24 @@
         ("GVP", vm((128, D), F32)),
         ("GVN", vm((128, D), F32)),
         ("TG", vm((32, 256), F32)),
-        ("TGR", vm((3, 8, 256), F32)),
+        ("TGR", vm((3, 32, 256), F32)),
+        ("TGF", vm((32, 256), F32)),
+        ("TMO", vm((32, 512), F32)),
+        ("WT", vm((32, 256), F32)),
         ("VG", vm((32, 128), F32)),
         ("VGR", vm((3, 8, 128), F32)),
         ("HG", vm((MPN, 32, 128), F32)),
         ("HGR", vm((3, 32, 128), F32)),
         ("EG", vm((40, NVAR), F32)),
         ("NX", vm((8, 128), F32)),
-        ("NXR", vm((7, 8, 128), F32)),
+        ("NXR", vm((3, 8, 128), F32)),
         ("NY", vm((8, 128), F32)),
-        ("NYR", vm((128, 128), F32)),
+        ("NYR", vm((256, 128), F32)),
     ]
     for name, width, kind in (
         ("A3", 256, BF),
-        ("B", 1024, BF),
+        ("B", 768, BF),
+        ("3", 256, BF),
         ("1", 1024, BF),
         ("2", 1024, BF),
         ("H", 256, BF),
@@ -567,10 +571,6 @@
             bar, inc=1, device_id={"dp": d, "mp": lax.rem(m + i, MPN)}, device_id_type=MESH
         )
     loop(1, DPN, greet)
-    for i in range(1, MPN):
-        pl.semaphore_signal(
-            bar, inc=1, device_id={"dp": sib, "mp": lax.rem(m + i, MPN)}, device_id_type=MESH
-        )
 
     for name in FETCH:
         fetch(name).start()
@@ -613,7 +613,7 @@
     R.NX[...] = jnp.zeros_like(R.NX)
     R.HG[...] = jnp.zeros_like(R.HG)
     R.VG[...] = jnp.zeros_like(R.VG)
-    pl.semaphore_wait(bar, DPN + 2 * MPN - 3)
+    pl.semaphore_wait(bar, DPN + MPN - 2)
 
     def first_sends(i, t):
         part = R.TA.at[my_eight]
@@ -679,6 +679,19 @@
             R.VPK[at, 32 * g : 32 * (g + 1)] = R.TA[8 * g : 8 * (g + 1), 256:288]
         R.VPK[at, 31:32] = jnp.broadcast_to(count, (8, 1))
 
+    def embed_moments():
+        for name in ("emb_f", "vec_f", "emb_s", "vec_s"):
+            fetch(name).wait()
+        R.TMO[my_eight, :] = jnp.zeros((8, 512), F32)
+        for start, held, vecs in ((0, R.in_emb_f, R.in_vec_f), (256, R.in_emb_s, R.in_vec_s)):
+            picked = nn(held[...], vhot, HIGH)
+            for p in range(5):
+                lane = start + p * 48
+                R.TMO[my_eight, lane : lane + 48] = picked[p * 8 : (p + 1) * 8, :]
+            R.TMO[my_eight, start + 240 : start + 241] = vecs[:, 0:1]
+        part = R.TMO.at[my_eight]
+        to_peers(lambda i, t: rcopy(part, part, ysend.at[21], yrecv.at[9], d, t).start())
+
     def first_bulk():
         own_vectors()
         two_second(R.WA3, 8)
@@ -686,6 +699,7 @@
         drain(R.WB3F.at[pl.ds(0, 32), pl.ds(0, 768)], yrecv.at[7])
         two_first(R.WB3F, 10)
         per_patch()
+        embed_moments()
 
     def bulk():
         two_second(R.WB, 1)
@@ -918,11 +932,11 @@
     R.GVN[6:7, my_cols] = jnp.sum(R.DQKV[:, 512:768].astype(F32), 0, keepdims=True)
 
     def grad_attn(at):
-        R.GB[at, 0:768] = tn(R.AG[0, :, at], R.DQKV[...]).astype(BF)
+        R.GB[at, :] = tn(R.AG[0, :, at], R.DQKV[...]).astype(BF)
 
     def grad_out(n):
         at = pl.ds(pl.multiple_of(n * 256, 256), 256)
-        R.GB[at, 768:1024] = tn(R.AG[3, :, at], R.OB[...]).astype(BF)
+        R.G3[at, :] = tn(R.AG[3, :, at], R.OB[...]).astype(BF)
 
     def first_rows(q):
         here = local_of(q)
@@ -939,16 +953,18 @@
         R.GVP[3:4, :] = R.GVP[3:4, :] + dgain
         R.GVP[4:5, :] = R.GVP[4:5, :] + dbias
 
-    loop(0, 4, lambda n: grad_attn(pl.ds(pl.multiple_of(n * 256, 256), 256)))
     loop(0, NQ, lambda q: share_wait(3, q))
     loop(0, 4, grad_out)
+    reduce_cross("3", 18)
+    loop(0, 4, lambda n: grad_attn(pl.ds(pl.multiple_of(n * 256, 256), 256)))
     reduce_cross("B", 11)
+    fold_first("3", 18)
     loop(0, NQ // 2, first_rows)
+    fold_second("1", 12)
     fold_first("B", 11)
+    loop(0, NQ // 2, lambda q: share_start(4, q))
     loop(NQ // 2, NQ, first_rows)
-    loop(0, NQ, lambda q: share_start(4, q))
-    fold_second("1", 12)
-    fold_second("H", 14)
+    loop(NQ // 2, NQ, lambda q: share_start(4, q))
     R.TMPV[...] = R.GVN[...].T
     R.GVT[...] = R.GVP[...].T.reshape(DPN, 4, 8, 128)
 
@@ -1023,7 +1039,7 @@
         sums["w"] = sums["w"] + jnp.where(here, square_sum(weight), 0.0)
         sums["u"] = sums["u"] + jnp.where(here, square_sum(direction), 0.0)
 
-    def hook_second():
+    def hook_first():
         loop(0, NQ, lambda q: share_wait(4, q))
 
         def piece(n):
@@ -1032,16 +1048,13 @@
 
         loop(0, 4, piece)
         reduce_cross("A3", 10)
-
-    def hook_first():
-        for name in MOMENTS:
-            fetch(name + "_f").wait()
-            fetch(name + "_s").wait()
-        R.o_mlp[1] = fold_end("2", 13)
-        R.o_mlp[0] = fold_end("1", 12)
-        for j in range(2):
-            tensor(8 + j, R.in_mlpw[j], R.o_mlp[j], R.in_mlp_f[j], R.in_mlp_s[j])
+        fold_second("H", 14)
+        fold_second("3", 18)
+        reduce_spread("A3", 10)
+
+    def hook_second():
         fold_second("B", 11)
+
     def hook_third():
         total = fold_end("H", 14)
         for j in range(MPN):
@@ -1067,12 +1080,13 @@
             ).start()
 
         to_peers(sends)
-        gsum = fold_end("B", 11)
-        for j in range(4):
-            R.o_attn[j] = gsum[:, j * 256 : (j + 1) * 256]
-        for j in range(4):
-            tensor(4 + j, R.in_attnw[j], R.o_attn[j], R.in_attn_f[j], R.in_attn_s[j])
-        reduce_spread("A3", 10)
+        for name in ("agg", "attn", "mlp", "head"):
+            fetch(name + "_f").wait()
+            fetch(name + "_s").wait()
+        R.o_mlp[1] = fold_end("2", 13)
+        R.o_mlp[0] = fold_end("1", 12)
+        for j in range(2):
+            tensor(8 + j, R.in_mlpw[j], R.o_mlp[j], R.in_mlp_f[j], R.in_mlp_s[j])
 
     all_sum(R.PRB, R.PRC, R.PRH, R.PRR, 8, (hook_first, hook_second, hook_third))
 
@@ -1086,63 +1100,83 @@
     R.TG[...] = nt(wa[1].astype(BF), pk) + nt(wa[2].astype(BF), pv)
     R.TG[:, 240:241] = jnp.sum(wa[0] * dqa, 1, keepdims=True)
 
-    def last_sends(i, t):
-        rcopy(
-            R.TG.at[pl.ds(pl.multiple_of(t * 8, 8), 8)],
-            R.TGR.at[i - 1],
-            ysend.at[13],
-            yrecv.at[3],
-            d,
-            t,
-        ).start()
-
-    to_peers(last_sends)
+    to_peers(
+        lambda i, t: rcopy(R.TG, R.TGR.at[i - 1], ysend.at[13], yrecv.at[3], d, t).start()
+    )
     R.o_agg[0] = R.TA[:, 256:257] * dqa
     emb = emb.astype(BF)
     R.o_agg[1] = nn(emb, pk)
     R.o_agg[2] = nn(emb, pv)
     for j in range(3):
         tensor(j, R.in_aggw[j], R.o_agg[j], R.in_agg_f[j], R.in_agg_s[j])
+    gsum = fold_end("B", 11)
+    for j in range(3):
+        R.o_attn[j] = gsum[:, j * 256 : (j + 1) * 256]
+    R.o_attn[3] = fold_end("3", 18)
+    for j in range(4):
+        tensor(4 + j, R.in_attnw[j], R.o_attn[j], R.in_attn_f[j], R.in_attn_s[j])
     drain(R.HGR, yrecv.at[4])
     hgrad = R.HG[m] + R.HGR[0] + R.HGR[1] + R.HGR[2]
     R.o_head[...] = hgrad[:, 0:NVAR]
     tensor(10, R.in_headw[...], R.o_head[...], R.in_head_f[...], R.in_head_s[...])
     drain(R.VGR, yrecv.at[5])
     vgrad = R.VG[my_eight, :] + R.VGR[0] + R.VGR[1] + R.VGR[2]
-    drain(R.TGR, yrecv.at[3])
-    tgrad = R.TG[my_eight, :] + R.TGR[0] + R.TGR[1] + R.TGR[2]
-    for p in range(5):
-        R.EG[p * 8 : (p + 1) * 8, :] = tgrad[:, p * 48 : (p + 1) * 48]
-    R.o_emb[...] = nt(R.EG[...], vhot, HIGH)
-    tensor(11, R.in_emb[...], R.o_emb[...], R.in_emb_f[...], R.in_emb_s[...])
     R.o_vec[...] = vgrad[:, 0:NVEC]
-    R.o_vec[:, 0:1] = tgrad[:, 240:241]
     unused, unused2, direction = adam_direction(
         R.in_vec[...], R.o_vec[...], R.in_vec_f[...], R.in_vec_s[...]
     )
     R.o_agg[3] = reduce_end("A3", 10)
     tensor(3, R.in_aggw[3], R.o_agg[3], R.in_agg_f[3], R.in_agg_s[3])
+    R.NX[0:1, :] = sums["w"]
+    R.NX[1:2, :] = sums["u"]
+    vector_w = jnp.sum(R.in_vec[...] * R.in_vec[...], 0, keepdims=True)
+    vector_u = jnp.sum(direction * direction, 0, keepdims=True)
+    R.NX[0:1, 13 : 12 + NVEC] = vector_w[:, 1:]
+    R.NX[1:2, 13 : 12 + NVEC] = vector_u[:, 1:]
+    to_peers(lambda i, t: rcopy(R.NX, R.NXR.at[i - 1], ysend.at[16], yrecv.at[6], d, t).start())
+
+    drain(R.TMO.at[pl.ds(0, 24)], yrecv.at[9])
+    R.WT[...] = R.TA[:, 0:256]
+    R.WT[:, 240:241] = R.TA[:, 256:257]
     R.o_vw[...] = R.in_vec[...]
     R.o_vf[...] = R.in_vec_f[...]
     R.o_vs[...] = R.in_vec_s[...]
     R.o_run[...] = R.in_run[...]
-    R.NX[0:1, :] = sums["w"]
-    R.NX[1:2, :] = sums["u"]
-    R.NX[0:1, 12 : 12 + NVEC] = jnp.sum(R.in_vec[...] * R.in_vec[...], 0, keepdims=True)
-    R.NX[1:2, 12 : 12 + NVEC] = jnp.sum(direction * direction, 0, keepdims=True)
-
-    for j in range(1, 2 * MPN):
-        t = lax.rem(m + j, MPN)
-        rcopy(
-            R.NX, R.NXR.at[j - 1], ysend.at[16], yrecv.at[6], sib if j >= MPN else d, t
-        ).start()
+    drain(R.TGR, yrecv.at[3])
+    whole = R.TG[...] + R.TGR[0] + R.TGR[1] + R.TGR[2]
+    R.TGF[...] = whole
+    unused, unused2, direction = adam_direction(
+        R.WT[...], whole, R.TMO[:, 0:256], R.TMO[:, 256:512]
+    )
+    lane = iota((1, 256), 1)
+
+    def two_sums(values):
+        columns = jnp.sum(values * values, 0, keepdims=True)
+        embed = jnp.sum(jnp.where(lane < 240, columns, 0.0), 1, keepdims=True)
+        first = jnp.sum(jnp.where(lane == 240, columns, 0.0), 1, keepdims=True)
+        return jnp.where(lanes == 11, embed, 0.0) + jnp.where(lanes == 12, first, 0.0)
+
+    embed_w, embed_u = two_sums(R.WT[...]), two_sums(direction)
     drain(R.NXR, yrecv.at[6])
-    norm = R.NX[...]
-    for j in range(7):
-        norm = norm + R.NXR[j]
-    R.NY[...] = norm
-    at_k = pl.ds(pl.multiple_of(k * 8, 8), 8)
-    to_chips(lambda kk, t: rcopy(R.NY, R.NYR.at[at_k], dsend.at[16], drecv.at[16], t, m).start())
+    R.NY[...] = R.NX[...] + R.NXR[0] + R.NXR[1] + R.NXR[2]
+    R.NY[0:1, :] = R.NY[0:1, :] + embed_w
+    R.NY[1:2, :] = R.NY[1:2, :] + embed_u
+    at_d = pl.ds(pl.multiple_of(d * 8, 8), 8)
+
+    def norm_send(t):
+        rcopy(R.NY, R.NYR.at[at_d], dsend.at[16], drecv.at[16], t, m).start()
+
+    for dz, dx in FAR_FIRST:
+        chip = lax.rem(z + dz, 4) * 4 + lax.rem(x + dx, 4)
+        norm_send(chip * 2)
+        norm_send(chip * 2 + 1)
+    norm_send(sib)
+
+    tgrad = R.TGF[my_eight, :]
+    for p in range(5):
+        R.EG[p * 8 : (p + 1) * 8, :] = tgrad[:, p * 48 : (p + 1) * 48]
+    R.o_emb[...] = nt(R.EG[...], vhot, HIGH)
+    R.o_vec[:, 0:1] = tgrad[:, 240:241]
 
     gather_end(R.VPK, 4)
     for buf, g in ((R.HW, 0), (R.WB, 1), (R.W1, 2), (R.W2, 3), (R.WA3, 8), (R.WA3F, 9), (R.WB3F, 10)):
@@ -1162,19 +1196,20 @@
     drain(R.HGR, ysend.at[14])
     drain(R.VGR, ysend.at[15])
     drain(R.NXR, ysend.at[16])
+    drain(R.TMO.at[pl.ds(0, 24)], ysend.at[21])
     drain(R.WB3F.at[pl.ds(0, 32), pl.ds(0, 768)], ysend.at[17])
     drain(R.WA3F.at[pl.ds(0, 32), pl.ds(0, 768)], ysend.at[18])
     drain(R.OF.at[:, pl.ds(0, 768)], ysend.at[19])
     drain(R.OF.at[:, pl.ds(0, 768)], ysend.at[20])
 
-    drain(R.NYR.at[pl.ds(0, 120)], drecv.at[16])
+    drain(R.NYR.at[pl.ds(0, 248)], drecv.at[16])
     stats = R.NY[...]
-    for dz, dx in FAR_FIRST:
-        kk = lax.rem(z + dz, 4) * 4 + lax.rem(x + dx, 4)
-        stats = stats + R.NYR[pl.ds(pl.multiple_of(kk * 8, 8), 8), :]
+    for i in range(1, DPN):
+        at = pl.multiple_of(lax.rem(d + i, DPN) * 8, 8)
+        stats = stats + R.NYR[pl.ds(at, 8), :]
     first_lane = (iota((8, 128), 0) == 0) & (iota((8, 128), 1) == 127)
     R.o_stats[...] = jnp.where(first_lane, total_count, stats)
-    drain(R.NYR.at[pl.ds(0, 120)], dsend.at[16])
+    drain(R.NYR.at[pl.ds(0, 248)], dsend.at[16])
 
 
 def mega_call(inputs):
@@ -1188,7 +1223,7 @@
         out_specs=(whole,) * len(outs),
         scratch_shapes=[item for unused, item in SCRATCH],
         compiler_params=pltpu.CompilerParams(
-            collective_id=0, has_side_effects=True, vmem_limit_bytes=54 * 2**20
+            collective_id=0, has_side_effects=True, vmem_limit_bytes=56 * 2**20
         ),
         name="step",
     )(*inputs)

time: 126 us -> 123 us (0.976)
  Pallas kernels: 124 us -> 121 us
    pallas_call x1, Pallas kernels: 123 us -> 120 us  [mega_call(): pl.pallas_call(mega, out_shape=tuple((pltpu.VMEM(*item) for item in outs)...]
where the time goes in v6:
time: 123 us
  Pallas kernels  121 us (98%)
    pallas_call x1, Pallas kernels, mega_call(): pl.pallas_call(mega, out_shape=tuple((pltpu.VMEM(*item) for item in outs)...  120 us

profile of v6, /device:TPU:1, one launch (start us, length us, event | category | flops | bytes accessed | tf_op | source)
XLA Modules:
  0.0 122.9 jit_solution(12100266802253397769)
XLA Ops:
  0.7 0.0 copy-start
  0.7 0.0 copy-start.1
  0.7 0.0 copy-start.2
  0.7 0.0 copy-start.3
  0.7 0.0 copy-start.4
  0.7 0.0 copy-start.5
  0.7 0.0 copy-start.6
  0.7 0.0 copy-start.7
  0.7 0.0 copy-start.8
  0.8 0.0 copy-start.10
  0.8 0.0 copy-start.11
  0.8 0.0 copy-start.12
  0.8 0.0 copy-start.13
  0.8 0.0 copy-start.14
  0.8 119.8 %step.1 = (f32[40,48]{1,0:T(8,128)S(1)}, f32[8,17]{1,0:T(8,128)S(1)}, f32[4,32,256]{2,1,0:T(8,128)S(1)}, f32[4,32,256]{2,1,0:T(8,128)S(1)}, f32[2,32,1024]{2,1,0...) custom-call(f32[40,48]{1,0:T(8,128)} %bitcast.35, ...), custom_call_target="tpu_custom_call" | custom-call | tf_op jit(solution)/shard_map/step/pallas_call | solution.py:1219
  120.6 0.0 copy-start.9
  120.6 0.0 copy-done
  120.6 0.0 copy-done.1
  120.6 0.0 copy-done.2
  120.6 0.0 copy-done.3
  120.6 0.0 copy-done.4
  120.6 0.0 copy-done.5
  120.6 0.0 copy-done.6
  120.7 0.0 copy-done.7
  120.7 0.0 copy-done.8
  120.7 0.0 copy-done.10
  120.7 0.0 copy-done.11
  120.7 0.0 copy-done.12
  120.7 0.0 copy-done.13
  120.7 0.0 copy-done.14
  120.7 0.6 copy-done.9
  121.3 1.5 %finish.1 = (f32[1,1]{1,0:T(1,128)}, f32[1,1]{1,0:T(1,128)}, f32[1,48]{1,0:T(1,128)}, f32[1,29]{1,0:T(1,128)}, f32[1,29]{1,0:T(1,128)}, /*index=5*/f32[4,32,256]...) custom-call(f32[4,32,256]{2,1,0:T(8,128)S(1)} %copy-done.3, ...), custom_call_target="tpu_custom_call" | custom-call | tf_op jit(solution)/shard_map/finish/pallas_call | solution.py:1271
Async XLA Ops:
  0.7 119.9 %copy-start = (f32[2,32,1024]{2,1,0:T(8,128)S(1)}, f32[2,32,1024]{2,1,0:T(8,128)}, u32[]{:S(2)}) copy-start(f32[2,32,1024]{2,1,0:T(8,128)} %refs_2_.1) | copy-start | bytes 786436
  0.7 119.9 %copy-start.1 = (f32[2,32,1024]{2,1,0:T(8,128)S(1)}, f32[2,32,1024]{2,1,0:T(8,128)}, u32[]{:S(2)}) copy-start(f32[2,32,1024]{2,1,0:T(8,128)} %refs_8_.1) | copy-start | bytes 786436
  0.7 119.9 %copy-start.2 = (f32[2,32,1024]{2,1,0:T(8,128)S(1)}, f32[2,32,1024]{2,1,0:T(8,128)}, u32[]{:S(2)}) copy-start(f32[2,32,1024]{2,1,0:T(8,128)} %refs_14_.3) | copy-start | bytes 786436
  0.7 119.9 %copy-start.3 = (f32[4,32,256]{2,1,0:T(8,128)S(1)}, f32[4,32,256]{2,1,0:T(8,128)}, u32[]{:S(2)}) copy-start(f32[4,32,256]{2,1,0:T(8,128)} %refs_0_.1) | copy-start | bytes 393220
  0.7 119.9 %copy-start.4 = (f32[4,32,256]{2,1,0:T(8,128)S(1)}, f32[4,32,256]{2,1,0:T(8,128)}, u32[]{:S(2)}) copy-start(f32[4,32,256]{2,1,0:T(8,128)} %refs_1_.1) | copy-start | bytes 393220
  0.7 119.9 %copy-start.5 = (f32[4,32,256]{2,1,0:T(8,128)S(1)}, f32[4,32,256]{2,1,0:T(8,128)}, u32[]{:S(2)}) copy-start(f32[4,32,256]{2,1,0:T(8,128)} %refs_6_.3) | copy-start | bytes 393220
  0.7 119.9 %copy-start.6 = (f32[4,32,256]{2,1,0:T(8,128)S(1)}, f32[4,32,256]{2,1,0:T(8,128)}, u32[]{:S(2)}) copy-start(f32[4,32,256]{2,1,0:T(8,128)} %refs_7_.1) | copy-start | bytes 393220
  0.7 119.9 %copy-start.7 = (f32[4,32,256]{2,1,0:T(8,128)S(1)}, f32[4,32,256]{2,1,0:T(8,128)}, u32[]{:S(2)}) copy-start(f32[4,32,256]{2,1,0:T(8,128)} %refs_12_.1) | copy-start | bytes 393220
  0.7 119.9 %copy-start.8 = (f32[4,32,256]{2,1,0:T(8,128)S(1)}, f32[4,32,256]{2,1,0:T(8,128)}, u32[]{:S(2)}) copy-start(f32[4,32,256]{2,1,0:T(8,128)} %refs_13_.1) | copy-start | bytes 393220
  0.8 119.9 %copy-start.10 = (f32[48,5,8]{0,2,1:T(8,128)S(1)}, f32[48,5,8]{0,2,1:T(8,128)}, u32[]{:S(2)}) copy-start(f32[48,5,8]{0,2,1:T(8,128)} %param.44) | copy-start | bytes 23044
  0.8 119.9 %copy-start.11 = (f32[48,5,8]{0,2,1:T(8,128)S(1)}, f32[48,5,8]{0,2,1:T(8,128)}, u32[]{:S(2)}) copy-start(f32[48,5,8]{0,2,1:T(8,128)} %param.50) | copy-start | bytes 23044
  0.8 119.9 %copy-start.12 = (f32[32,48]{1,0:T(8,128)S(1)}, f32[32,48]{1,0:T(8,128)}, u32[]{:S(2)}) copy-start(f32[32,48]{1,0:T(8,128)} %refs_3_.3) | copy-start | bytes 18436
  0.8 119.9 %copy-start.13 = (f32[32,48]{1,0:T(8,128)S(1)}, f32[32,48]{1,0:T(8,128)}, u32[]{:S(2)}) copy-start(f32[32,48]{1,0:T(8,128)} %refs_9_.1) | copy-start | bytes 18436
  0.8 119.9 %copy-start.14 = (f32[32,48]{1,0:T(8,128)S(1)}, f32[32,48]{1,0:T(8,128)}, u32[]{:S(2)}) copy-start(f32[32,48]{1,0:T(8,128)} %refs_15_.3) | copy-start | bytes 18436
  120.6 0.7 copy-start.9

commit v7 on v6

--- a/solution.py
+++ b/solution.py
@@ -104,7 +104,8 @@
 MOMENTS = ("agg", "attn", "mlp", "head", "emb", "vec")
 SMALL = ("mask", "seg", "leadi", "lat", "run")
 OUTS = ("o_emb", "o_vec", "o_agg", "o_attn", "o_mlp", "o_head", "o_stats")
-OUTS = OUTS + ("o_vw", "o_vf", "o_vs", "o_run")
+OUTS = OUTS + ("o_vw", "o_vf", "o_vs", "o_run", "o_ew", "o_ef", "o_es")
+OUTS = OUTS + ("o_hw", "o_hf", "o_hs")
 SHAPES = {
     "pix": ((NVAR * P_SIZE, TOK), BF),
     "targ": ((NVAR, TOK), F32),
@@ -897,20 +898,21 @@
         R.GVP[7:8, :] = R.GVP[7:8, :] + jnp.sum(dx1, 0, keepdims=True)
         R.GVP[8:9, :] = R.GVP[8:9, :] + dgain
         R.GVP[9:10, :] = R.GVP[9:10, :] + dbias
-        pieces(q, grad_one)
 
     for n in range(4):
         grad_two(pl.ds(n * 256, 256))
     reduce_cross("2", 13)
+    for n in range(4):
+        grad_one(pl.ds(n * 256, 256))
+    reduce_cross("1", 12)
     loop(0, NQ // 2, back_rows)
     fold_first("2", 13)
     loop(NQ // 2, NQ, back_rows)
     loop(0, NQ, lambda q: share_start(3, q))
-    reduce_cross("1", 12)
+    fold_first("1", 12)
     R.GH[...] = tn(R.H3[...], R.DP[...]).astype(BF)
     reduce_cross("H", 14)
     gather_wait(R.WA3F, 16)
-    fold_first("1", 12)
     fold_first("H", 14)
 
     loop(0, NQ, lambda q: drain(R.DOB.at[pl.ds(0, 3 * CH)], R.nrecv.at[0, q]))
@@ -1040,6 +1042,8 @@
         sums["u"] = sums["u"] + jnp.where(here, square_sum(direction), 0.0)
 
     def hook_first():
+        fold_second("H", 14)
+        fold_second("3", 18)
         loop(0, NQ, lambda q: share_wait(4, q))
 
         def piece(n):
@@ -1048,8 +1052,13 @@
 
         loop(0, 4, piece)
         reduce_cross("A3", 10)
-        fold_second("H", 14)
-        fold_second("3", 18)
+        for name in ("agg", "attn", "mlp", "head"):
+            fetch(name + "_f").wait()
+            fetch(name + "_s").wait()
+        R.o_mlp[1] = fold_end("2", 13)
+        R.o_mlp[0] = fold_end("1", 12)
+        for j in range(2):
+            tensor(8 + j, R.in_mlpw[j], R.o_mlp[j], R.in_mlp_f[j], R.in_mlp_s[j])
         reduce_spread("A3", 10)
 
     def hook_second():
@@ -1080,13 +1089,6 @@
             ).start()
 
         to_peers(sends)
-        for name in ("agg", "attn", "mlp", "head"):
-            fetch(name + "_f").wait()
-            fetch(name + "_s").wait()
-        R.o_mlp[1] = fold_end("2", 13)
-        R.o_mlp[0] = fold_end("1", 12)
-        for j in range(2):
-            tensor(8 + j, R.in_mlpw[j], R.o_mlp[j], R.in_mlp_f[j], R.in_mlp_s[j])
 
     all_sum(R.PRB, R.PRC, R.PRH, R.PRR, 8, (hook_first, hook_second, hook_third))
 
@@ -1142,6 +1144,12 @@
     R.o_vf[...] = R.in_vec_f[...]
     R.o_vs[...] = R.in_vec_s[...]
     R.o_run[...] = R.in_run[...]
+    R.o_ew[...] = R.in_emb[...]
+    R.o_ef[...] = R.in_emb_f[...]
+    R.o_es[...] = R.in_emb_s[...]
+    R.o_hw[...] = R.in_headw[...]
+    R.o_hf[...] = R.in_head_f[...]
+    R.o_hs[...] = R.in_head_s[...]
     drain(R.TGR, yrecv.at[3])
     whole = R.TG[...] + R.TGR[0] + R.TGR[1] + R.TGR[2]
     R.TGF[...] = whole
@@ -1214,7 +1222,7 @@
 
 def mega_call(inputs):
     outs = [SHAPES[n] for n in ("emb", "vec", "agg", "attn", "mlp", "head")] + [((8, 128), F32)]
-    outs += [SHAPES["vec"]] * 3 + [SHAPES["run"]]
+    outs += [SHAPES["vec"]] * 3 + [SHAPES["run"]] + [SHAPES["emb"]] * 3 + [SHAPES["head"]] * 3
     whole = pl.BlockSpec(memory_space=pltpu.VMEM)
     return pl.pallas_call(
         mega,
@@ -1308,7 +1316,8 @@
     )
     grads = (g_agg, g_attn, g_mlp, g_head, g_emb, g_vec)
     weights, firsts, seconds = (
-        (*group[:5], own) for group, own in zip((weights, firsts, seconds), rest)
+        (*group[:3], head, embed, own)
+        for group, own, embed, head in zip((weights, firsts, seconds), rest, rest[4:], rest[7:])
     )
     out = finish_call(weights, firsts, seconds, grads, stats, rest[3])
 

time: 123 us -> 122 us (level)
  no operation moved by 1% of the time
where the time goes in v7:
time: 122 us
  Pallas kernels  121 us (99%)
    pallas_call x1, Pallas kernels, mega_call(): pl.pallas_call(mega, out_shape=tuple((pltpu.VMEM(*item) for item in outs)...  120 us

profile of v7, /device:TPU:1, one launch (start us, length us, event | category | flops | bytes accessed | tf_op | source)
XLA Modules:
  0.0 122.3 jit_solution(16528840390747468995)
XLA Ops:
  0.7 0.0 copy-start
  0.7 0.0 copy-start.1
  0.7 0.0 copy-start.2
  0.7 0.0 copy-start.3
  0.7 0.0 copy-start.4
  0.7 0.0 copy-start.5
  0.7 0.0 copy-start.6
  0.7 0.0 copy-start.7
  0.7 0.0 copy-start.8
  0.8 119.7 %step.1 = (f32[40,48]{1,0:T(8,128)S(1)}, f32[8,17]{1,0:T(8,128)S(1)}, f32[4,32,256]{2,1,0:T(8,128)S(1)}, f32[4,32,256]{2,1,0:T(8,128)S(1)}, f32[2,32,1024]{2,1,0...) custom-call(f32[40,48]{1,0:T(8,128)} %bitcast.37, ...), custom_call_target="tpu_custom_call" | custom-call | tf_op jit(solution)/shard_map/step/pallas_call | solution.py:1227
  120.5 0.0 copy-done
  120.5 0.0 copy-done.1
  120.5 0.0 copy-done.2
  120.5 0.0 copy-done.3
  120.5 0.0 copy-done.4
  120.5 0.0 copy-done.5
  120.5 0.0 copy-done.6
  120.5 0.0 copy-done.7
  120.6 0.0 copy-done.8
  120.6 1.6 %finish.1 = (f32[1,1]{1,0:T(1,128)}, f32[1,1]{1,0:T(1,128)}, f32[1,48]{1,0:T(1,128)}, f32[1,29]{1,0:T(1,128)}, f32[1,29]{1,0:T(1,128)}, /*index=5*/f32[4,32,256]...) custom-call(f32[4,32,256]{2,1,0:T(8,128)S(1)} %copy-done.3, ...), custom_call_target="tpu_custom_call" | custom-call | tf_op jit(solution)/shard_map/finish/pallas_call | solution.py:1279
Async XLA Ops:
  0.7 119.8 %copy-start = (f32[2,32,1024]{2,1,0:T(8,128)S(1)}, f32[2,32,1024]{2,1,0:T(8,128)}, u32[]{:S(2)}) copy-start(f32[2,32,1024]{2,1,0:T(8,128)} %refs_2_.1) | copy-start | bytes 786436
  0.7 119.8 %copy-start.1 = (f32[2,32,1024]{2,1,0:T(8,128)S(1)}, f32[2,32,1024]{2,1,0:T(8,128)}, u32[]{:S(2)}) copy-start(f32[2,32,1024]{2,1,0:T(8,128)} %refs_8_.1) | copy-start | bytes 786436
  0.7 119.8 %copy-start.2 = (f32[2,32,1024]{2,1,0:T(8,128)S(1)}, f32[2,32,1024]{2,1,0:T(8,128)}, u32[]{:S(2)}) copy-start(f32[2,32,1024]{2,1,0:T(8,128)} %refs_14_.3) | copy-start | bytes 786436
  0.7 119.8 %copy-start.3 = (f32[4,32,256]{2,1,0:T(8,128)S(1)}, f32[4,32,256]{2,1,0:T(8,128)}, u32[]{:S(2)}) copy-start(f32[4,32,256]{2,1,0:T(8,128)} %refs_0_.1) | copy-start | bytes 393220
  0.7 119.8 %copy-start.4 = (f32[4,32,256]{2,1,0:T(8,128)S(1)}, f32[4,32,256]{2,1,0:T(8,128)}, u32[]{:S(2)}) copy-start(f32[4,32,256]{2,1,0:T(8,128)} %refs_1_.1) | copy-start | bytes 393220
  0.7 119.8 %copy-start.5 = (f32[4,32,256]{2,1,0:T(8,128)S(1)}, f32[4,32,256]{2,1,0:T(8,128)}, u32[]{:S(2)}) copy-start(f32[4,32,256]{2,1,0:T(8,128)} %refs_6_.3) | copy-start | bytes 393220
  0.7 119.8 %copy-start.6 = (f32[4,32,256]{2,1,0:T(8,128)S(1)}, f32[4,32,256]{2,1,0:T(8,128)}, u32[]{:S(2)}) copy-start(f32[4,32,256]{2,1,0:T(8,128)} %refs_7_.1) | copy-start | bytes 393220
  0.7 119.8 %copy-start.7 = (f32[4,32,256]{2,1,0:T(8,128)S(1)}, f32[4,32,256]{2,1,0:T(8,128)}, u32[]{:S(2)}) copy-start(f32[4,32,256]{2,1,0:T(8,128)} %refs_12_.1) | copy-start | bytes 393220
  0.7 119.8 %copy-start.8 = (f32[4,32,256]{2,1,0:T(8,128)S(1)}, f32[4,32,256]{2,1,0:T(8,128)}, u32[]{:S(2)}) copy-start(f32[4,32,256]{2,1,0:T(8,128)} %refs_13_.1) | copy-start | bytes 393220

commit v8 on v7

--- a/solution.py
+++ b/solution.py
@@ -648,8 +648,10 @@
 
     drain(R.TA.at[pl.ds(0, 24)], yrecv.at[0])
     emb = R.TA[:, 0:256]
-    R.EWP[:, 0:256] = tn(emb, aw[1].astype(F32), HIGH)
-    R.EWP[:, 256:512] = tn(emb, aw[2].astype(F32), HIGH)
+    high = emb.astype(BF)
+    rest = (emb - high.astype(F32)).astype(BF)
+    R.EWP[:, 0:256] = tn(high, aw[1]) + tn(rest, aw[1])
+    R.EWP[:, 256:512] = tn(high, aw[2]) + tn(rest, aw[2])
     R.EWP[240:241, 0:256] = jnp.sum(R.TA[:, 256:257] * aw[0].astype(F32), 0, keepdims=True)
     R.EWB[...] = R.EWP[...].astype(BF)
     keep = R.in_mask[...].astype(F32)
@@ -714,7 +716,10 @@
     head_of = (iota((256, 128), 0) // HEAD_DIM == iota((256, 128), 1)).astype(F32)
     ewk = R.EWR[:, 0:256].astype(F32)
     qa = ewk[240:241, :]
-    qe = nn(ewk * (qa * SCALE), head_of, HIGH)
+    keyed = ewk * (qa * SCALE)
+    high = keyed.astype(BF)
+    rest = (keyed - high.astype(F32)).astype(BF)
+    qe = nn(high, head_of.astype(BF)) + nn(rest, head_of.astype(BF))
     ewv = R.EWR[:, 256:512]
     for h in range(4):
         scores = R.PIXT[0:48, :] * qe[0:48, h : h + 1]

time: 122 us -> 122 us (level)
  no operation moved by 1% of the time
where the time goes in v8:
time: 122 us
  Pallas kernels  121 us (99%)
    pallas_call x1, Pallas kernels, mega_call(): pl.pallas_call(mega, out_shape=tuple((pltpu.VMEM(*item) for item in outs)...  119 us

profile of v8, /device:TPU:1, one launch (start us, length us, event | category | flops | bytes accessed | tf_op | source)
XLA Modules:
  0.0 121.7 jit_solution(17023807574804813000)
XLA Ops:
  0.7 0.0 copy-start
  0.7 0.0 copy-start.1
  0.7 0.0 copy-start.2
  0.7 0.0 copy-start.3
  0.7 0.0 copy-start.4
  0.7 0.0 copy-start.5
  0.7 0.0 copy-start.6
  0.7 0.0 copy-start.7
  0.7 0.0 copy-start.8
  0.8 119.1 %step.1 = (f32[40,48]{1,0:T(8,128)S(1)}, f32[8,17]{1,0:T(8,128)S(1)}, f32[4,32,256]{2,1,0:T(8,128)S(1)}, f32[4,32,256]{2,1,0:T(8,128)S(1)}, f32[2,32,1024]{2,1,0...) custom-call(f32[40,48]{1,0:T(8,128)} %bitcast.37, ...), custom_call_target="tpu_custom_call" | custom-call | tf_op jit(solution)/shard_map/step/pallas_call | solution.py:1232
  119.9 0.0 copy-done
  119.9 0.0 copy-done.1
  119.9 0.0 copy-done.2
  119.9 0.0 copy-done.3
  119.9 0.0 copy-done.4
  120.0 0.0 copy-done.5
  120.0 0.0 copy-done.6
  120.0 0.0 copy-done.7
  120.0 0.0 copy-done.8
  120.0 1.6 %finish.1 = (f32[1,1]{1,0:T(1,128)}, f32[1,1]{1,0:T(1,128)}, f32[1,48]{1,0:T(1,128)}, f32[1,29]{1,0:T(1,128)}, f32[1,29]{1,0:T(1,128)}, /*index=5*/f32[4,32,256]...) custom-call(f32[4,32,256]{2,1,0:T(8,128)S(1)} %copy-done.3, ...), custom_call_target="tpu_custom_call" | custom-call | tf_op jit(solution)/shard_map/finish/pallas_call | solution.py:1284
Async XLA Ops:
  0.7 119.2 %copy-start = (f32[2,32,1024]{2,1,0:T(8,128)S(1)}, f32[2,32,1024]{2,1,0:T(8,128)}, u32[]{:S(2)}) copy-start(f32[2,32,1024]{2,1,0:T(8,128)} %refs_2_.1) | copy-start | bytes 786436
  0.7 119.2 %copy-start.1 = (f32[2,32,1024]{2,1,0:T(8,128)S(1)}, f32[2,32,1024]{2,1,0:T(8,128)}, u32[]{:S(2)}) copy-start(f32[2,32,1024]{2,1,0:T(8,128)} %refs_8_.1) | copy-start | bytes 786436
  0.7 119.2 %copy-start.2 = (f32[2,32,1024]{2,1,0:T(8,128)S(1)}, f32[2,32,1024]{2,1,0:T(8,128)}, u32[]{:S(2)}) copy-start(f32[2,32,1024]{2,1,0:T(8,128)} %refs_14_.3) | copy-start | bytes 786436
  0.7 119.2 %copy-start.3 = (f32[4,32,256]{2,1,0:T(8,128)S(1)}, f32[4,32,256]{2,1,0:T(8,128)}, u32[]{:S(2)}) copy-start(f32[4,32,256]{2,1,0:T(8,128)} %refs_0_.1) | copy-start | bytes 393220
  0.7 119.2 %copy-start.4 = (f32[4,32,256]{2,1,0:T(8,128)S(1)}, f32[4,32,256]{2,1,0:T(8,128)}, u32[]{:S(2)}) copy-start(f32[4,32,256]{2,1,0:T(8,128)} %refs_1_.1) | copy-start | bytes 393220
  0.7 119.2 %copy-start.5 = (f32[4,32,256]{2,1,0:T(8,128)S(1)}, f32[4,32,256]{2,1,0:T(8,128)}, u32[]{:S(2)}) copy-start(f32[4,32,256]{2,1,0:T(8,128)} %refs_6_.3) | copy-start | bytes 393220
  0.7 119.2 %copy-start.6 = (f32[4,32,256]{2,1,0:T(8,128)S(1)}, f32[4,32,256]{2,1,0:T(8,128)}, u32[]{:S(2)}) copy-start(f32[4,32,256]{2,1,0:T(8,128)} %refs_7_.1) | copy-start | bytes 393220
  0.7 119.2 %copy-start.7 = (f32[4,32,256]{2,1,0:T(8,128)S(1)}, f32[4,32,256]{2,1,0:T(8,128)}, u32[]{:S(2)}) copy-start(f32[4,32,256]{2,1,0:T(8,128)} %refs_12_.1) | copy-start | bytes 393220
  0.7 119.2 %copy-start.8 = (f32[4,32,256]{2,1,0:T(8,128)S(1)}, f32[4,32,256]{2,1,0:T(8,128)}, u32[]{:S(2)}) copy-start(f32[4,32,256]{2,1,0:T(8,128)} %refs_13_.1) | copy-start | bytes 393220
